TPU v7x, 32 devices: a whole 2x2x4 slice. The times are simulated.
32 devices in a mesh: items: 4 (over y, x), seq: 8 (over z, core).
Axes of the slice: x: 2, y: 2, z: 4, core: 2. Of those that a mesh axis runs over, the one named last changes fastest.
Arguments:
- dec_in: bfloat16 [8, 512, 1024], P('items', 'seq'), may hold values from -6 to 6
- memory: bfloat16 [8, 384, 1024], P('items', 'seq'), may hold values from -6 to 6
- dec_len: int32 [8], P('items'), may hold values from 64 to 512, as said below
- mem_len: int32 [8], P('items'), may hold values from 25 to 384, as said below
- cell_mask: int32 [8, 384], P('items', 'seq'), may hold values 0 or 1
- self_query: bfloat16 [1024, 1024], P('seq'), may hold values from -0.1875 to 0.1875
- self_key: bfloat16 [1024, 1024], P('seq'), may hold values from -0.1875 to 0.1875
- self_value: bfloat16 [1024, 1024], P('seq'), may hold values from -0.1875 to 0.1875
- self_out: bfloat16 [1024, 1024], P('seq'), may hold values from -1.5 to 1.5
- cross_query: bfloat16 [1024, 1024], P('seq'), may hold values from -0.1875 to 0.1875
- cross_key: bfloat16 [1024, 1024], P('seq'), may hold values from -0.1875 to 0.1875
- cross_value: bfloat16 [1024, 1024], P('seq'), may hold values from -0.1875 to 0.1875
- cross_out: bfloat16 [1024, 1024], P('seq'), may hold values from -1.5 to 1.5
- ffn_in: bfloat16 [1024, 4096], P(None, 'seq'), may hold values from -0.1875 to 0.1875
- ffn_out: bfloat16 [4096, 1024], P('seq'), may hold values from -0.1875 to 0.1875
- norm_gain: float32 [3, 1024], replicated, may hold values from 0.5 to 1.5
- norm_bias: float32 [3, 1024], replicated, may hold values from -1 to 1
- cotangent: bfloat16 [8, 512, 1024], P('items', 'seq'), may hold values from -6 to 6
Outputs:
- layer_out: bfloat16 [8, 512, 1024], P('items', 'seq')
- grad_dec: float32 [8, 512, 1024], P('items', 'seq')
- grad_memory: float32 [8, 384, 1024], P('items', 'seq')
- grad_self_query: float32 [1024, 1024], P('seq')
- grad_self_key: float32 [1024, 1024], P('seq')
- grad_self_value: float32 [1024, 1024], P('seq')
- grad_self_out: float32 [1024, 1024], P('seq')
- grad_cross_query: float32 [1024, 1024], P('seq')
- grad_cross_key: float32 [1024, 1024], P('seq')
- grad_cross_value: float32 [1024, 1024], P('seq')
- grad_cross_out: float32 [1024, 1024], P('seq')
- grad_ffn_in: float32 [1024, 4096], P(None, 'seq')
- grad_ffn_out: float32 [4096, 1024], P('seq')
- grad_norm_gain: float32 [3, 1024], replicated
- grad_norm_bias: float32 [3, 1024], replicated
Inputs may be any that keep to these rules, and one draw needn't show every extreme that they name: `dec_len`: among the 2 consecutive items of each index of items, one has decoder length 512. `mem_len`: among the 2 consecutive items of each index of items, one has memory length 384.
All inputs are finite; a program needn't handle non-finite values. No bound on the sum of `cell_mask` on one device may be relied on, other than what follows from the above.
Results may differ from a plain program's by a relative error of at most 0.03.
Values may be sent and summed in bfloat16 or wider, within the bound.
A program may use at most 256 MiB of HBM per device.

v0:
```python
import jax
import jax.numpy as jnp
from jax import lax
from jax.sharding import PartitionSpec as P

HEAD_DIM = 64


EPS = 1e-05
NEG = -1e30


def norm_rows(value, gain, bias):
    mean = jnp.mean(value, axis=-1, keepdims=True)
    centered = value - mean
    scaled = centered * lax.rsqrt(jnp.mean(centered * centered, axis=-1, keepdims=True) + EPS)
    return scaled * gain + bias


def gelu_exact(value):
    return jax.nn.gelu(value, approximate=False)


def split_heads(value):
    return value.reshape(value.shape[0], -1, HEAD_DIM)


def scores_of(query, keys, valid):
    raw = jnp.einsum(
        "rhe,khe->hrk", split_heads(query), split_heads(keys), preferred_element_type=jnp.float32
    )
    return jnp.where(valid[None], raw * HEAD_DIM ** (-0.5), NEG)


def attend_forward(query, keys, values, valid):
    scores = scores_of(query, keys, valid)
    top = jnp.max(scores, axis=-1, keepdims=True)
    lse = top + jnp.log(jnp.sum(jnp.exp(scores - top), axis=-1, keepdims=True))
    probs = jnp.exp(scores - lse).astype(jnp.bfloat16)
    mixed = jnp.einsum(
        "hrk,khe->rhe", probs, split_heads(values), preferred_element_type=jnp.float32
    )
    return (mixed.reshape(query.shape).astype(jnp.bfloat16), lse)


def attend_backward(query, keys, values, valid, lse, grad_mixed):
    scale = HEAD_DIM ** (-0.5)
    probs = jnp.exp(scores_of(query, keys, valid) - lse)
    grad_heads = split_heads(grad_mixed)
    grad_probs = jnp.einsum(
        "rhe,khe->hrk", grad_heads, split_heads(values), preferred_element_type=jnp.float32
    )
    delta = jnp.sum(probs * grad_probs, axis=-1, keepdims=True)
    grad_scores = (probs * (grad_probs - delta)).astype(jnp.bfloat16)
    grad_query = (
        jnp.einsum(
            "hrk,khe->rhe", grad_scores, split_heads(keys), preferred_element_type=jnp.float32
        )
        * scale
    )
    grad_keys = (
        jnp.einsum(
            "hrk,rhe->khe", grad_scores, split_heads(query), preferred_element_type=jnp.float32
        )
        * scale
    )
    grad_values = jnp.einsum(
        "hrk,rhe->khe", probs.astype(jnp.bfloat16), grad_heads, preferred_element_type=jnp.float32
    )
    return (
        grad_query.reshape(query.shape),
        grad_keys.reshape(keys.shape),
        grad_values.reshape(values.shape),
    )


def self_valid(length, place, dec_dev, total):
    rows = place * dec_dev + lax.broadcasted_iota(jnp.int32, (dec_dev, total), 0)
    cols = lax.broadcasted_iota(jnp.int32, (dec_dev, total), 1)
    return (cols <= rows) & (cols < length)


def cross_valid(length, cells, dec_dev):
    places = jnp.arange(cells.shape[0], dtype=jnp.int32)
    keep = (places < length) & ((cells == 1.0) | (places == 0))
    return jnp.broadcast_to(keep[None], (dec_dev, cells.shape[0]))


def project(left, right):
    return jnp.dot(left, right, preferred_element_type=jnp.float32).astype(jnp.bfloat16)


def shards(
    dec_in,
    memory,
    dec_len,
    mem_len,
    cell_mask,
    self_query,
    self_key,
    self_value,
    self_out,
    cross_query,
    cross_key,
    cross_value,
    cross_out,
    ffn_in,
    ffn_out,
    norm_gain,
    norm_bias,
    cotangent,
):
    items_dev, dec_dev, width = dec_in.shape
    mem_dev = memory.shape[1]
    place = lax.axis_index("seq")
    tok_rows = items_dev * dec_dev
    weights = (
        lax.all_gather(self_query, "seq", axis=0, tiled=True),
        lax.all_gather(self_key, "seq", axis=0, tiled=True),
        lax.all_gather(self_value, "seq", axis=0, tiled=True),
        lax.all_gather(self_out, "seq", axis=0, tiled=True),
        lax.all_gather(cross_query, "seq", axis=0, tiled=True),
        lax.all_gather(cross_key, "seq", axis=0, tiled=True),
        lax.all_gather(cross_value, "seq", axis=0, tiled=True),
        lax.all_gather(cross_out, "seq", axis=0, tiled=True),
    )
    w_sq, w_sk, w_sv, w_so, w_cq, w_ck, w_cv, w_co = weights
    tokens = dec_in.reshape(tok_rows, width)
    mem_rows = memory.reshape(items_dev * mem_dev, width)
    self_q = project(tokens, w_sq).reshape(items_dev, dec_dev, width)
    self_k = project(tokens, w_sk).reshape(items_dev, dec_dev, width)
    self_v = project(tokens, w_sv).reshape(items_dev, dec_dev, width)
    keys_all, values_all = (
        lax.all_gather(self_k, "seq", axis=1, tiled=True),
        lax.all_gather(self_v, "seq", axis=1, tiled=True),
    )
    total_dec = keys_all.shape[1]

    def self_item(pieces):
        query, keys, values, length = pieces
        return attend_forward(query, keys, values, self_valid(length, place, dec_dev, total_dec))

    self_mixed, self_lse = lax.map(self_item, (self_q, keys_all, values_all, dec_len))
    self_flat = self_mixed.reshape(tok_rows, width)
    first_sum = tokens.astype(jnp.float32) + jnp.dot(
        self_flat, w_so, preferred_element_type=jnp.float32
    )
    first, first_back = jax.vjp(norm_rows, first_sum, norm_gain[0], norm_bias[0])
    first_low = first.astype(jnp.bfloat16)
    cross_q = project(first_low, w_cq).reshape(items_dev, dec_dev, width)
    cross_k = project(mem_rows, w_ck).reshape(items_dev, mem_dev, width)
    cross_v = project(mem_rows, w_cv).reshape(items_dev, mem_dev, width)
    ckeys_all, cvalues_all, cells_all = (
        lax.all_gather(cross_k, "seq", axis=1, tiled=True),
        lax.all_gather(cross_v, "seq", axis=1, tiled=True),
        lax.all_gather(cell_mask.astype(jnp.bfloat16), "seq", axis=1, tiled=True),
    )

    def cross_item(pieces):
        query, keys, values, length, cells = pieces
        return attend_forward(query, keys, values, cross_valid(length, cells, dec_dev))

    cross_mixed, cross_lse = lax.map(
        cross_item, (cross_q, ckeys_all, cvalues_all, mem_len, cells_all)
    )
    cross_flat = cross_mixed.reshape(tok_rows, width)
    second_sum = first + jnp.dot(cross_flat, w_co, preferred_element_type=jnp.float32)
    second, second_back = jax.vjp(norm_rows, second_sum, norm_gain[1], norm_bias[1])
    second_low = second.astype(jnp.bfloat16)
    gathered = lax.all_gather(second_low, "seq", axis=0, tiled=True)
    pre = jnp.dot(gathered, ffn_in, preferred_element_type=jnp.float32)
    act = gelu_exact(pre).astype(jnp.bfloat16)
    ffn_sum = lax.psum_scatter(
        jnp.dot(act, ffn_out, preferred_element_type=jnp.float32).astype(jnp.bfloat16),
        "seq",
        scatter_dimension=0,
        tiled=True,
    ).astype(jnp.float32)
    third_sum = second + ffn_sum
    row_pos = place * dec_dev + lax.broadcasted_iota(jnp.int32, (items_dev, dec_dev), 1)
    row_keep = (row_pos < dec_len[:, None]).reshape(tok_rows, 1)
    third, third_back = jax.vjp(norm_rows, third_sum, norm_gain[2], norm_bias[2])
    layer_out = jnp.where(row_keep, third, 0.0).astype(jnp.bfloat16).reshape(dec_in.shape)
    grad_out = jnp.where(row_keep, cotangent.reshape(tok_rows, width).astype(jnp.float32), 0.0)
    grad_third, gain_three, bias_three = third_back(grad_out)
    grad_y = grad_third.astype(jnp.bfloat16)
    grad_rows = lax.all_gather(grad_y, "seq", axis=0, tiled=True)
    pre_again = jnp.dot(gathered, ffn_in, preferred_element_type=jnp.float32)
    act_again, gelu_back = jax.vjp(gelu_exact, pre_again)
    grad_act = jnp.dot(grad_rows, ffn_out.T, preferred_element_type=jnp.float32)
    grad_pre = gelu_back(grad_act)[0].astype(jnp.bfloat16)
    grad_ffn_in = jnp.dot(gathered.T, grad_pre, preferred_element_type=jnp.float32)
    grad_ffn_out = jnp.dot(
        act_again.astype(jnp.bfloat16).T, grad_rows, preferred_element_type=jnp.float32
    )
    grad_second = grad_third + lax.psum_scatter(
        jnp.dot(grad_pre, ffn_in.T, preferred_element_type=jnp.float32).astype(jnp.bfloat16),
        "seq",
        scatter_dimension=0,
        tiled=True,
    ).astype(jnp.float32)
    grad_r2, gain_two, bias_two = second_back(grad_second)
    grad_c2 = grad_r2.astype(jnp.bfloat16)
    grad_cmix = project(grad_c2, w_co.T).reshape(items_dev, dec_dev, width)

    def cross_back(pieces):
        query, keys, values, length, cells, lse, grad_mixed = pieces
        grad_query, grad_keys, grad_values = attend_backward(
            query, keys, values, cross_valid(length, cells, dec_dev), lse, grad_mixed
        )
        own_keys, own_values = (
            lax.psum_scatter(
                grad_keys.astype(jnp.bfloat16), "seq", scatter_dimension=0, tiled=True
            ).astype(jnp.float32),
            lax.psum_scatter(
                grad_values.astype(jnp.bfloat16), "seq", scatter_dimension=0, tiled=True
            ).astype(jnp.float32),
        )
        return (
            grad_query.astype(jnp.bfloat16),
            own_keys.astype(jnp.bfloat16),
            own_values.astype(jnp.bfloat16),
        )

    grad_cq, grad_ck, grad_cv = lax.map(
        cross_back, (cross_q, ckeys_all, cvalues_all, mem_len, cells_all, cross_lse, grad_cmix)
    )
    grad_cq = grad_cq.reshape(tok_rows, width)
    grad_ck = grad_ck.reshape(items_dev * mem_dev, width)
    grad_cv = grad_cv.reshape(items_dev * mem_dev, width)
    grad_memory = jnp.dot(grad_ck, w_ck.T, preferred_element_type=jnp.float32) + jnp.dot(
        grad_cv, w_cv.T, preferred_element_type=jnp.float32
    )
    grad_first = grad_r2 + jnp.dot(grad_cq, w_cq.T, preferred_element_type=jnp.float32)
    grad_r1, gain_one, bias_one = first_back(grad_first)
    grad_c1 = grad_r1.astype(jnp.bfloat16)
    grad_smix = project(grad_c1, w_so.T).reshape(items_dev, dec_dev, width)

    def self_back(pieces):
        query, keys, values, length, lse, grad_mixed = pieces
        grad_query, grad_keys, grad_values = attend_backward(
            query, keys, values, self_valid(length, place, dec_dev, total_dec), lse, grad_mixed
        )
        own_keys, own_values = (
            lax.psum_scatter(
                grad_keys.astype(jnp.bfloat16), "seq", scatter_dimension=0, tiled=True
            ).astype(jnp.float32),
            lax.psum_scatter(
                grad_values.astype(jnp.bfloat16), "seq", scatter_dimension=0, tiled=True
            ).astype(jnp.float32),
        )
        return (
            grad_query.astype(jnp.bfloat16),
            own_keys.astype(jnp.bfloat16),
            own_values.astype(jnp.bfloat16),
        )

    grad_sq, grad_sk, grad_sv = lax.map(
        self_back, (self_q, keys_all, values_all, dec_len, self_lse, grad_smix)
    )
    grad_sq = grad_sq.reshape(tok_rows, width)
    grad_sk = grad_sk.reshape(tok_rows, width)
    grad_sv = grad_sv.reshape(tok_rows, width)
    grad_dec = grad_r1 + jnp.dot(grad_sq, w_sq.T, preferred_element_type=jnp.float32)
    grad_dec = grad_dec + jnp.dot(grad_sk, w_sk.T, preferred_element_type=jnp.float32)
    grad_dec = grad_dec + jnp.dot(grad_sv, w_sv.T, preferred_element_type=jnp.float32)
    pairs = (
        (tokens, grad_sq),
        (tokens, grad_sk),
        (tokens, grad_sv),
        (self_flat, grad_c1),
        (first_low, grad_cq),
        (mem_rows, grad_ck),
        (mem_rows, grad_cv),
        (cross_flat, grad_c2),
    )
    terms = [jnp.dot(left.T, right, preferred_element_type=jnp.float32) for left, right in pairs]
    attn_grads = lax.psum_scatter(
        jnp.concatenate(terms, axis=1).astype(jnp.bfloat16), "seq", scatter_dimension=0, tiled=True
    ).astype(jnp.float32)
    attn_grads, grad_ffn_in, grad_ffn_out = (
        lax.psum(attn_grads.astype(jnp.bfloat16), "items").astype(jnp.float32),
        lax.psum(grad_ffn_in.astype(jnp.bfloat16), "items").astype(jnp.float32),
        lax.psum(grad_ffn_out.astype(jnp.bfloat16), "items").astype(jnp.float32),
    )
    gain_grads, bias_grads = lax.psum(
        (jnp.stack([gain_one, gain_two, gain_three]), jnp.stack([bias_one, bias_two, bias_three])),
        ("items", "seq"),
    )
    pieces = tuple((attn_grads[:, index * width : (index + 1) * width] for index in range(8)))
    return (
        (layer_out, grad_dec.reshape(dec_in.shape), grad_memory.reshape(memory.shape))
        + pieces
        + (grad_ffn_in, grad_ffn_out, gain_grads, bias_grads)
    )


def solution(mesh):
    placed = (
        P("items", "seq", None),
        P("items", "seq", None),
        P("items"),
        P("items"),
        P("items", "seq"),
        P("seq", None),
        P("seq", None),
        P("seq", None),
        P("seq", None),
        P("seq", None),
        P("seq", None),
        P("seq", None),
        P("seq", None),
        P(None, "seq"),
        P("seq", None),
        P(),
        P(),
        P("items", "seq", None),
    )
    return jax.shard_map(
        shards,
        mesh=mesh,
        in_specs=placed,
        out_specs=(
            P("items", "seq", None),
            P("items", "seq", None),
            P("items", "seq", None),
            P("seq", None),
            P("seq", None),
            P("seq", None),
            P("seq", None),
            P("seq", None),
            P("seq", None),
            P("seq", None),
            P("seq", None),
            P(None, "seq"),
            P("seq", None),
            P(),
            P(),
        ),
        check_vma=False,
    )
```

profile of v0, /device:TPU:0, one launch (start us, length us, event | category | flops | bytes accessed | tf_op | source)
XLA Modules:
  0.0 1169.6 jit_solution(14898344545123585627)
XLA Ops:
  10.6 30.8 %all-gather.28.cloned.1.call-done = bf16[1024,1024]{1,0:T(8,128)(2,1)} async-done(((bf16[128,1024]{1,0:T(8,128)(2,1)}), bf16[1024,1024]{1,0:T(8,128)(2,1)}) %all-gather.28.cloned.1.call-update) | async-done | bytes 2097168 | tf_op jit(solution)/shard_map/all_gather | solution.py:124
  41.5 2.2 convolution_convert_fusion.15
  44.6 27.1 %all-gather.34.cloned.1.call-done = bf16[1024,1024]{1,0:T(8,128)(2,1)} async-done(((bf16[128,1024]{1,0:T(8,128)(2,1)}), bf16[1024,1024]{1,0:T(8,128)(2,1)}) %all-gather.34.cloned.1.call-update) | async-done | bytes 2097168 | tf_op jit(solution)/shard_map/all_gather | solution.py:123
  71.7 2.1 convolution_convert_fusion.14
  74.7 27.2 %all-gather.16.cloned.1.call-done = bf16[1024,1024]{1,0:T(8,128)(2,1)} async-done(((bf16[128,1024]{1,0:T(8,128)(2,1)}), bf16[1024,1024]{1,0:T(8,128)(2,1)}) %all-gather.16.cloned.1.call-update) | async-done | bytes 2097168 | tf_op jit(solution)/shard_map/all_gather | solution.py:120
  105.1 27.0 %all-gather.22.cloned.1.call-done = bf16[1024,1024]{1,0:T(8,128)(2,1)} async-done(((bf16[128,1024]{1,0:T(8,128)(2,1)}), bf16[1024,1024]{1,0:T(8,128)(2,1)}) %all-gather.22.cloned.1.call-update) | async-done | bytes 2097168 | tf_op jit(solution)/shard_map/all_gather | solution.py:119
  137.0 10.3 all-gather
  149.2 12.9 %all-gather.20.cloned.1.call-done = bf16[1024,1024]{1,0:T(8,128)(2,1)} async-done(((bf16[128,1024]{1,0:T(8,128)(2,1)}), bf16[1024,1024]{1,0:T(8,128)(2,1)}) %all-gather.20.cloned.1.call-update) | async-done | bytes 2097168 | tf_op jit(solution)/shard_map/all_gather | solution.py:118
  162.1 2.7 convolution_convert_fusion.12
  164.8 23.9 %all-gather.30.cloned.1.call-done = bf16[2,384,1024]{2,0,1:T(2,128)(2,1)} async-done(((bf16[2,48,1024]{2,0,1:T(2,128)(2,1)}), bf16[2,384,1024]{2,0,1:T(2,128)(2,1)}) %all-gather.30.cloned.1.call-update) | async-done | bytes 1572880 | tf_op jit(solution)/shard_map/all_gather | solution.py:155
  188.7 5.0 copy.108
  193.7 21.8 %all-gather.36.cloned.1.call-done = bf16[2,384,1024]{2,0,1:T(2,128)(2,1)} async-done(((bf16[2,48,1024]{2,0,1:T(2,128)(2,1)}), bf16[2,384,1024]{2,0,1:T(2,128)(2,1)}) %all-gather.36.cloned.1.call-update) | async-done | bytes 1572880 | tf_op jit(solution)/shard_map/all_gather | solution.py:154
  215.6 5.0 copy.109
  220.5 25.9 %all-gather.18.cloned.1.call-done = bf16[2,512,1024]{2,0,1:T(2,128)(2,1)} async-done(((bf16[2,64,1024]{2,0,1:T(2,128)(2,1)}), bf16[2,512,1024]{2,0,1:T(2,128)(2,1)}) %all-gather.18.cloned.1.call-update) | async-done | bytes 2097168 | tf_op jit(solution)/shard_map/all_gather | solution.py:135
  246.4 4.7 copy.102
  251.1 26.1 %all-gather.24.cloned.1.call-done = bf16[2,512,1024]{2,0,1:T(2,128)(2,1)} async-done(((bf16[2,64,1024]{2,0,1:T(2,128)(2,1)}), bf16[2,512,1024]{2,0,1:T(2,128)(2,1)}) %all-gather.24.cloned.1.call-update) | async-done | bytes 2097168 | tf_op jit(solution)/shard_map/all_gather | solution.py:134
  277.2 6.1 copy.103
  284.1 15.7 %while.56 = (s32[]{:T(128)}, bf16[2,64,1024]{2,1,0:T(8,128)(2,1)}, f32[2,16,64,1]{2,1,3,0:T(8,128)S(1)}, bf16[2,512,1024]{1,2,0:T(8,128)(2,1)S(1)}, s32[]{:T(128...) while((s32[]{:T(128)}, bf16[2,64,1024]{2,1,0:T(8,128)(2,1)}, ...), condition=%wide.region_3.4_spmd, body=%wide.region_0.3_spmd.sunk | while | flops 138018368 | bytes 14141093 | solution.py:143
  299.8 7.5 all-gather.26.cloned.1.call-done
  307.3 2.2 fusion.39
  310.5 27.0 %all-gather.32.cloned.1.call-done = bf16[1024,1024]{1,0:T(8,128)(2,1)} async-done(((bf16[128,1024]{1,0:T(8,128)(2,1)}), bf16[1024,1024]{1,0:T(8,128)(2,1)}) %all-gather.32.cloned.1.call-update) | async-done | bytes 2097168 | tf_op jit(solution)/shard_map/all_gather | solution.py:122
  337.5 2.3 convolution_convert_fusion.10
  339.9 9.5 while.57
  349.5 18.2 %all-gather.38.cloned.1.call-done = bf16[1024,1024]{1,0:T(8,128)(2,1)} async-done(((bf16[128,1024]{1,0:T(8,128)(2,1)}), bf16[1024,1024]{1,0:T(8,128)(2,1)}) %all-gather.38.cloned.1.call-update) | async-done | bytes 2097168 | tf_op jit(solution)/shard_map/all_gather | solution.py:125
  367.6 2.2 fusion.40
  371.2 28.5 %all-gather.40.cloned.1.call-done = bf16[1024,1024]{1,0:T(8,128)(2,1)} async-done(((bf16[128,1024]{1,0:T(8,128)(2,1)}), bf16[1024,1024]{1,0:T(8,128)(2,1)}) %all-gather.40.cloned.1.call-update) | async-done | bytes 2097168 | tf_op jit(solution)/shard_map/all_gather | solution.py:170
  399.7 8.3 multiply_convert_fusion.4
  409.0 3.9 convolution_convert_fusion.5
  413.8 34.5 %reduce-scatter.26.cloned.1.call-done = bf16[128,1024]{1,0:T(8,128)(2,1)} async-done(((bf16[1024,1024]{1,0:T(8,128)(2,1)}), bf16[128,1024]{1,0:T(8,128)(2,1)}) %reduce-scatter.26.cloned.1.call-update) | async-done | bytes 262160 | tf_op jit(solution)/shard_map/reduce_scatter | solution.py:173
  452.0 28.0 %all-gather.42.cloned.1.call-done = bf16[1024,1024]{1,0:T(8,128)(2,1)} async-done(((bf16[128,1024]{1,0:T(8,128)(2,1)}), bf16[1024,1024]{1,0:T(8,128)(2,1)}) %all-gather.42.cloned.1.call-update) | async-done | bytes 2097168 | tf_op jit(solution)/shard_map/all_gather | solution.py:187
  480.0 5.0 add_convert_fusion
  486.0 2.6 convolution_convert_fusion.4
  488.7 35.4 %reduce-scatter.28.cloned.1.call-done = bf16[128,1024]{1,0:T(8,128)(2,1)} async-done(((bf16[1024,1024]{1,0:T(8,128)(2,1)}), bf16[128,1024]{1,0:T(8,128)(2,1)}) %reduce-scatter.28.cloned.1.call-update) | async-done | bytes 262160 | tf_op jit(solution)/shard_map/reduce_scatter | solution.py:196
  526.7 2.6 convolution_convert_fusion.9
  530.1 143.8 %while.58 = (s32[]{:T(128)}, bf16[2,64,1024]{2,1,0:T(8,128)(2,1)}, bf16[2,48,1024]{1,2,0:T(8,128)(2,1)}, bf16[2,48,1024]{1,2,0:T(8,128)(2,1)}, bf16[2,384,1024]{...) while((s32[]{:T(128)}, bf16[2,64,1024]{2,1,0:T(8,128)(2,1)}, ...), condition=%wide.region_24.25_spmd, body=%wide.region_20.24_spmd.sunk | while | flops 256509568 | bytes 47799140 | solution.py:225
  541.3 26.7 %reduce-scatter.34.cloned.1.call-done = bf16[48,1024]{1,0:T(8,128)(2,1)} async-done(((bf16[384,1024]{1,0:T(8,128)(2,1)}), bf16[48,1024]{1,0:T(8,128)(2,1)}) %reduce-scatter.34.cloned.1.call-update) | async-done | bytes 98320 | tf_op jit(solution)/shard_map/while
  569.1 31.5 %reduce-scatter.32.cloned.1.call-done = bf16[48,1024]{1,0:T(8,128)(2,1)} async-done(((bf16[384,1024]{1,0:T(8,128)(2,1)}), bf16[48,1024]{1,0:T(8,128)(2,1)}) %reduce-scatter.32.cloned.1.call-update) | async-done | bytes 98320 | tf_op jit(solution)/shard_map/while
  613.6 26.0 %reduce-scatter.34.cloned.1.call-done = bf16[48,1024]{1,0:T(8,128)(2,1)} async-done(((bf16[384,1024]{1,0:T(8,128)(2,1)}), bf16[48,1024]{1,0:T(8,128)(2,1)}) %reduce-scatter.34.cloned.1.call-update) | async-done | bytes 98320 | tf_op jit(solution)/shard_map/while
  640.7 31.3 %reduce-scatter.32.cloned.1.call-done = bf16[48,1024]{1,0:T(8,128)(2,1)} async-done(((bf16[384,1024]{1,0:T(8,128)(2,1)}), bf16[48,1024]{1,0:T(8,128)(2,1)}) %reduce-scatter.32.cloned.1.call-update) | async-done | bytes 98320 | tf_op jit(solution)/shard_map/while
  673.9 3.0 multiply_reduce_fusion.4
  678.1 152.8 %while.59 = (s32[]{:T(128)}, bf16[2,64,1024]{1,2,0:T(8,128)(2,1)}, bf16[2,64,1024]{1,2,0:T(8,128)(2,1)}, bf16[2,64,1024]{1,2,0:T(8,128)(2,1)}, bf16[2,512,1024]{...) while((s32[]{:T(128)}, bf16[2,64,1024]{1,2,0:T(8,128)(2,1)}, ...), condition=%wide.region_31.32_spmd, body=%wide.region_27.31_spmd.sunk | while | flops 342031936 | bytes 63789072 | solution.py:258
  693.3 25.9 %reduce-scatter.38.cloned.1.call-done = bf16[64,1024]{1,0:T(8,128)(2,1)} async-done(((bf16[512,1024]{1,0:T(8,128)(2,1)}), bf16[64,1024]{1,0:T(8,128)(2,1)}) %reduce-scatter.38.cloned.1.call-update) | async-done | bytes 131088 | tf_op jit(solution)/shard_map/while
  720.4 32.5 %reduce-scatter.36.cloned.1.call-done = bf16[64,1024]{1,0:T(8,128)(2,1)} async-done(((bf16[512,1024]{1,0:T(8,128)(2,1)}), bf16[64,1024]{1,0:T(8,128)(2,1)}) %reduce-scatter.36.cloned.1.call-update) | async-done | bytes 131088 | tf_op jit(solution)/shard_map/while
  769.9 25.6 %reduce-scatter.38.cloned.1.call-done = bf16[64,1024]{1,0:T(8,128)(2,1)} async-done(((bf16[512,1024]{1,0:T(8,128)(2,1)}), bf16[64,1024]{1,0:T(8,128)(2,1)}) %reduce-scatter.38.cloned.1.call-update) | async-done | bytes 131088 | tf_op jit(solution)/shard_map/while
  796.7 32.3 %reduce-scatter.36.cloned.1.call-done = bf16[64,1024]{1,0:T(8,128)(2,1)} async-done(((bf16[512,1024]{1,0:T(8,128)(2,1)}), bf16[64,1024]{1,0:T(8,128)(2,1)}) %reduce-scatter.36.cloned.1.call-update) | async-done | bytes 131088 | tf_op jit(solution)/shard_map/while
  831.2 3.2 bitcast_dynamic-update-slice_fusion.10
  834.4 2.1 bitcast_dynamic-update-slice_fusion.9
  836.5 2.1 bitcast_dynamic-update-slice_fusion.8
  838.6 2.2 convert_dynamic-update-slice_fusion.2
  840.8 2.1 convert_dynamic-update-slice_fusion.1
  843.0 2.2 bitcast_dynamic-update-slice_fusion.7
  845.1 2.1 bitcast_dynamic-update-slice_fusion.6
  847.2 2.1 convert_dynamic-update-slice_fusion
  849.3 21.3 %copy.147 = bf16[1024,8192]{1,0:T(8,128)(2,1)} copy(bf16[1024,8192]{0,1:T(8,128)(2,1)} %convert_dynamic-update-slice_fusion) | data formatting | bytes 33554432
  872.2 3.7 convolution_convert_fusion.6
  875.9 2.3 convolution_convert_fusion.7
  878.2 159.4 %reduce-scatter.30.cloned.1.call-done = bf16[128,8192]{1,0:T(8,128)(2,1)} async-done(((bf16[1024,8192]{1,0:T(8,128)(2,1)}), bf16[128,8192]{1,0:T(8,128)(2,1)}) %reduce-scatter.30.cloned.1.call-update) | async-done | bytes 2097168
  1037.5 4.1 copy.148
  1047.7 39.5 %all-reduce = (f32[3,1024]{1,0:T(4,128)}, f32[3,1024]{1,0:T(4,128)}) all-reduce(f32[3,1024]{1,0:T(4,128)S(1)} %get-tuple-element.578, f32[3,1024]{1,0:T(4,128)S(1)} %get-tuple-element.579), channel_id=1, replica_groups=mesh['items'=4,'seq'=8] {'items','seq'}, use_global_device_ids=true, to_apply=%region_39.40 | all-reduce | flops 6144 | bytes 49152 | tf_op jit(solution)/shard_map/psum | solution.py:286
  1087.2 2.5 fusion.43
  1089.8 2.6 convolution_add_fusion.6
  1096.7 49.3 %all-reduce.4.cloned.1.call-done = (bf16[128,8192]{0,1:T(8,128)(2,1)}, bf16[1024,512]{1,0:T(8,128)(2,1)}, bf16[512,1024]{1,0:T(8,128)(2,1)}) async-done(((bf16[128,8192]{0,1:T(8,128)(2,1)}, bf16[1024,512]{1,0:T(8,128)(2,1)}, bf16[512,1024]{1,0:T(8,128)(2,1)}), (bf16[128,8192]{0,1:T(8,128)(2,1)}, bf16[1024,512]{1,0:T(8,128)(2,1)}, bf16[512,1024]{1,0:T(8,128)(2,1)})) %all-reduce.4.cloned.1.call-update) | async-done | bytes 4194320 | tf_op jit(solution)/shard_map/psum | solution.py:282
  1146.0 2.9 convert_element_type.260
  1152.5 2.0 copy.133
  (461 shorter events, 141.5 us)
Async XLA Ops:
  7.2 392.5 %copy-start = (bf16[1024,512]{1,0:T(8,128)(2,1)S(1)}, bf16[1024,512]{1,0:T(8,128)(2,1)}, u32[]{:S(2)}) copy-start(bf16[1024,512]{1,0:T(8,128)(2,1)} %param.39) | copy-start | bytes 3145732
  7.2 34.3 %all-gather.28.cloned.1.call-start = ((), (), s32[]{:S(2)}) async-start(), calls=%async_computation.13 | async-start | bytes 2359296 | tf_op jit(solution)/shard_map/all_gather | solution.py:124
  7.9 63.8 %copy-start.46 = (bf16[2,48,1024]{2,1,0:T(8,128)(2,1)S(1)}, bf16[2,48,1024]{2,1,0:T(8,128)(2,1)}, u32[]{:S(2)}) copy-start(bf16[2,48,1024]{2,1,0:T(8,128)(2,1)} %param.27) | copy-start | bytes 589828
  7.9 63.7 %all-gather.34.cloned.1.call-start = ((), (), s32[]{:S(2)}) async-start(), calls=%async_computation.16 | async-start | bytes 2359296 | tf_op jit(solution)/shard_map/all_gather | solution.py:123
  8.7 93.2 %all-gather.16.cloned.1.call-start = ((), (), s32[]{:S(2)}) async-start(), calls=%async_computation.7 | async-start | bytes 2359296 | tf_op jit(solution)/shard_map/all_gather | solution.py:120
  9.4 122.6 %all-gather.22.cloned.1.call-start = ((), (), s32[]{:S(2)}) async-start(), calls=%async_computation.10 | async-start | bytes 2359296 | tf_op jit(solution)/shard_map/all_gather | solution.py:119
  10.0 152.1 %all-gather.20.cloned.1.call-start = ((), (), s32[]{:S(2)}) async-start(), calls=%async_computation.9 | async-start | bytes 2359296 | tf_op jit(solution)/shard_map/all_gather | solution.py:118
  10.6 178.1 %all-gather.30.cloned.1.call-start = ((), (), s32[]{:S(2)}) async-start(), calls=%async_computation.14 | async-start | bytes 1769472 | tf_op jit(solution)/shard_map/all_gather | solution.py:155
  43.6 58.3 %copy-start.26 = (bf16[2,64,1024]{2,1,0:T(8,128)(2,1)S(1)}, bf16[2,64,1024]{2,1,0:T(8,128)(2,1)}, u32[]{:S(2)}) copy-start(bf16[2,64,1024]{2,1,0:T(8,128)(2,1)} %param.26) | copy-start | bytes 786436
  44.6 171.0 %all-gather.36.cloned.1.call-start = ((), (), s32[]{:S(2)}) async-start(), calls=%async_computation.17 | async-start | bytes 1769472 | tf_op jit(solution)/shard_map/all_gather | solution.py:154
  74.7 171.8 %all-gather.18.cloned.1.call-start = ((), (), s32[]{:S(2)}) async-start(), calls=%async_computation.8 | async-start | bytes 2359296 | tf_op jit(solution)/shard_map/all_gather | solution.py:135
  105.0 32.0 %copy-start.74 = (s32[2,48]{1,0:T(2,128)S(1)}, s32[2,48]{1,0:T(2,128)}, u32[]{:S(2)}) copy-start(s32[2,48]{1,0:T(2,128)} %param.30) | copy-start | bytes 1156
  105.0 43.0 %copy-start.71 = (f32[3,1024]{1,0:T(4,128)S(1)}, f32[3,1024]{1,0:T(4,128)}, u32[]{:S(2)}) copy-start(f32[3,1024]{1,0:T(4,128)} %param.41) | copy-start | bytes 36868
  105.0 43.6 %copy-start.72 = (f32[3,1024]{1,0:T(4,128)S(1)}, f32[3,1024]{1,0:T(4,128)}, u32[]{:S(2)}) copy-start(f32[3,1024]{1,0:T(4,128)} %param.42) | copy-start | bytes 36868
  105.0 172.2 %all-gather.24.cloned.1.call-start = ((), (), s32[]{:S(2)}) async-start(), calls=%async_computation.11 | async-start | bytes 2359296 | tf_op jit(solution)/shard_map/all_gather | solution.py:134
  135.0 172.2 %all-gather.26.cloned.1.call-start = ((), (), s32[]{:S(2)}) async-start(), calls=%async_computation.12 | async-start | bytes 2359296 | tf_op jit(solution)/shard_map/all_gather | solution.py:121
  135.6 201.9 %all-gather.32.cloned.1.call-start = ((), (), s32[]{:S(2)}) async-start(), calls=%async_computation.15 | async-start | bytes 2359296 | tf_op jit(solution)/shard_map/all_gather | solution.py:122
  136.4 231.2 %all-gather.38.cloned.1.call-start = ((), (), s32[]{:S(2)}) async-start(), calls=%async_computation.18 | async-start | bytes 2359296 | tf_op jit(solution)/shard_map/all_gather | solution.py:125
  137.0 262.7 %all-gather.40.cloned.1.call-start = ((), (), s32[]{:S(2)}) async-start(), calls=%async_computation.19 | async-start | bytes 2359296 | tf_op jit(solution)/shard_map/all_gather | solution.py:170
  299.8 40.0 %copy-start.6 = (bf16[2,512,1024]{1,2,0:T(8,128)(2,1)}, bf16[2,512,1024]{1,2,0:T(8,128)(2,1)S(1)}, u32[]{:S(2)}) copy-start(bf16[2,512,1024]{1,2,0:T(8,128)(2,1)S(1)} %get-tuple-element.1021) | copy-start | bytes 6291460
  299.8 37.7 %copy-start.65 = (f32[1,1024]{1,0:T(1,128)S(1)}, f32[1,1024]{1,0:T(1,128)}, u32[]{:S(2)}) copy-start(f32[1,1024]{1,0:T(1,128)} %get-tuple-element.567) | copy-start | bytes 12292
  299.8 37.7 %copy-start.67 = (f32[1,1024]{1,0:T(1,128)S(1)}, f32[1,1024]{1,0:T(1,128)}, u32[]{:S(2)}) copy-start(f32[1,1024]{1,0:T(1,128)} %get-tuple-element.570) | copy-start | bytes 12292
  309.5 30.4 %copy-start.64 = (bf16[384,2]{0,1:T(2,128)(2,1)S(1)}, bf16[384,2]{0,1:T(2,128)(2,1)}, u32[]{:S(2)}) copy-start(bf16[384,2]{0,1:T(2,128)(2,1)} %reshape.510) | copy-start | bytes 4612
  309.5 30.4 %copy-start.75 = (s32[2]{0:T(128)S(1)}, s32[2]{0:T(128)}, u32[]{:S(2)}) copy-start(s32[2]{0:T(128)} %param.29) | copy-start | bytes 28
  339.9 27.7 %copy-start.11 = (f32[128,1024]{1,0:T(8,128)S(1)}, f32[128,1024]{1,0:T(8,128)}, u32[]{:S(2)}) copy-start(f32[128,1024]{1,0:T(8,128)} %copy-done.10) | copy-start | bytes 1572868
  349.4 21.5 %copy-start.39 = (bf16[2,64,1024]{2,1,0:T(8,128)(2,1)}, bf16[2,64,1024]{2,1,0:T(8,128)(2,1)S(1)}, u32[]{:S(2)}) copy-start(bf16[2,64,1024]{2,1,0:T(8,128)(2,1)S(1)} %get-tuple-element.342) | copy-start | bytes 786436
  349.4 20.6 %copy-start.66 = (f32[1,1024]{1,0:T(1,128)S(1)}, f32[1,1024]{1,0:T(1,128)}, u32[]{:S(2)}) copy-start(f32[1,1024]{1,0:T(1,128)} %get-tuple-element.568) | copy-start | bytes 12292
  370.9 77.4 %reduce-scatter.26.cloned.1.call-start = ((), (), s32[]{:S(2)}) async-start(), calls=%async_computation.20 | async-start | bytes 2359296 | tf_op jit(solution)/shard_map/reduce_scatter | solution.py:173
  412.9 36.9 %copy-start.33 = (bf16[2,64,1024]{2,1,0:T(8,128)(2,1)S(1)}, bf16[2,64,1024]{2,1,0:T(8,128)(2,1)}, u32[]{:S(2)}) copy-start(bf16[2,64,1024]{2,1,0:T(8,128)(2,1)} %param.43) | copy-start | bytes 786436
  412.9 36.9 %copy-start.68 = (f32[1,1024]{1,0:T(1,128)S(1)}, f32[1,1024]{1,0:T(1,128)}, u32[]{:S(2)}) copy-start(f32[1,1024]{1,0:T(1,128)} %get-tuple-element.566) | copy-start | bytes 12292
  412.9 37.2 %copy-start.70 = (f32[1,1024]{1,0:T(1,128)S(1)}, f32[1,1024]{1,0:T(1,128)}, u32[]{:S(2)}) copy-start(f32[1,1024]{1,0:T(1,128)} %get-tuple-element.569) | copy-start | bytes 12292
  413.0 67.1 %all-gather.42.cloned.1.call-start = ((), (), s32[]{:S(2)}) async-start(), calls=%async_computation.21 | async-start | bytes 2359296 | tf_op jit(solution)/shard_map/all_gather | solution.py:187
  452.0 72.1 %reduce-scatter.28.cloned.1.call-start = ((), (), s32[]{:S(2)}) async-start(), calls=%async_computation.22 | async-start | bytes 2359296 | tf_op jit(solution)/shard_map/reduce_scatter | solution.py:196
  530.3 37.7 %reduce-scatter.34.cloned.1.call-start = ((), (), s32[]{:S(2)}) async-start(), calls=%async_computation.26 | async-start | bytes 884736 | tf_op jit(solution)/shard_map/while
  537.4 63.2 %reduce-scatter.32.cloned.1.call-start = ((), (), s32[]{:S(2)}) async-start(), calls=%async_computation.25 | async-start | bytes 884736 | tf_op jit(solution)/shard_map/while
  540.7 28.4 %copy-start.56 = (bf16[2,48,1024]{1,2,0:T(8,128)(2,1)S(1)}, bf16[2,48,1024]{1,2,0:T(8,128)(2,1)}, u32[]{:S(2)}) copy-start(bf16[2,48,1024]{1,2,0:T(8,128)(2,1)} %get-tuple-element.929) | copy-start | bytes 589828 | tf_op jit(solution)/shard_map/while
  540.7 61.0 %copy-start.60 = (bf16[2,48,1024]{1,2,0:T(8,128)(2,1)S(1)}, bf16[2,48,1024]{1,2,0:T(8,128)(2,1)}, u32[]{:S(2)}) copy-start(bf16[2,48,1024]{1,2,0:T(8,128)(2,1)} %get-tuple-element.928) | copy-start | bytes 589828 | tf_op jit(solution)/shard_map/while
  541.1 61.4 %copy-start.15 = (bf16[2,64,1024]{2,1,0:T(8,128)(2,1)S(1)}, bf16[2,64,1024]{2,1,0:T(8,128)(2,1)}, u32[]{:S(2)}) copy-start(bf16[2,64,1024]{2,1,0:T(8,128)(2,1)} %copy-done.14) | copy-start | bytes 786436 | tf_op jit(solution)/shard_map/while
  541.1 61.4 %copy-start.30 = (bf16[2,64,1024]{2,1,0:T(8,128)(2,1)S(1)}, bf16[2,64,1024]{2,1,0:T(8,128)(2,1)}, u32[]{:S(2)}) copy-start(bf16[2,64,1024]{2,1,0:T(8,128)(2,1)} %copy-done.29) | copy-start | bytes 786436 | tf_op jit(solution)/shard_map/while
  541.3 60.4 %copy-start.36 = (bf16[2,64,1024]{2,1,0:T(8,128)(2,1)}, bf16[2,64,1024]{2,1,0:T(8,128)(2,1)S(1)}, u32[]{:S(2)}) copy-start(bf16[2,64,1024]{2,1,0:T(8,128)(2,1)S(1)} %constant_dynamic-update-slice_fusion.10) | copy-start | bytes 786436 | tf_op jit(solution)/shard_map/while
  569.1 32.6 %copy-start.57 = (bf16[2,48,1024]{1,2,0:T(8,128)(2,1)}, bf16[2,48,1024]{1,2,0:T(8,128)(2,1)S(1)}, u32[]{:S(2)}) copy-start(bf16[2,48,1024]{1,2,0:T(8,128)(2,1)S(1)} %bitcast_dynamic-update-slice_fusion.20) | copy-start | bytes 589828 | tf_op jit(solution)/shard_map/while
  602.5 37.0 %reduce-scatter.34.cloned.1.call-start = ((), (), s32[]{:S(2)}) async-start(), calls=%async_computation.26 | async-start | bytes 884736 | tf_op jit(solution)/shard_map/while
  609.7 62.2 %reduce-scatter.32.cloned.1.call-start = ((), (), s32[]{:S(2)}) async-start(), calls=%async_computation.25 | async-start | bytes 884736 | tf_op jit(solution)/shard_map/while
  612.9 27.7 %copy-start.56 = (bf16[2,48,1024]{1,2,0:T(8,128)(2,1)S(1)}, bf16[2,48,1024]{1,2,0:T(8,128)(2,1)}, u32[]{:S(2)}) copy-start(bf16[2,48,1024]{1,2,0:T(8,128)(2,1)} %get-tuple-element.929) | copy-start | bytes 589828 | tf_op jit(solution)/shard_map/while
  612.9 60.1 %copy-start.60 = (bf16[2,48,1024]{1,2,0:T(8,128)(2,1)S(1)}, bf16[2,48,1024]{1,2,0:T(8,128)(2,1)}, u32[]{:S(2)}) copy-start(bf16[2,48,1024]{1,2,0:T(8,128)(2,1)} %get-tuple-element.928) | copy-start | bytes 589828 | tf_op jit(solution)/shard_map/while
  613.4 60.5 %copy-start.15 = (bf16[2,64,1024]{2,1,0:T(8,128)(2,1)S(1)}, bf16[2,64,1024]{2,1,0:T(8,128)(2,1)}, u32[]{:S(2)}) copy-start(bf16[2,64,1024]{2,1,0:T(8,128)(2,1)} %copy-done.14) | copy-start | bytes 786436 | tf_op jit(solution)/shard_map/while
  613.4 60.5 %copy-start.30 = (bf16[2,64,1024]{2,1,0:T(8,128)(2,1)S(1)}, bf16[2,64,1024]{2,1,0:T(8,128)(2,1)}, u32[]{:S(2)}) copy-start(bf16[2,64,1024]{2,1,0:T(8,128)(2,1)} %copy-done.29) | copy-start | bytes 786436 | tf_op jit(solution)/shard_map/while
  613.6 59.5 %copy-start.36 = (bf16[2,64,1024]{2,1,0:T(8,128)(2,1)}, bf16[2,64,1024]{2,1,0:T(8,128)(2,1)S(1)}, u32[]{:S(2)}) copy-start(bf16[2,64,1024]{2,1,0:T(8,128)(2,1)S(1)} %constant_dynamic-update-slice_fusion.10) | copy-start | bytes 786436 | tf_op jit(solution)/shard_map/while
  640.7 32.4 %copy-start.57 = (bf16[2,48,1024]{1,2,0:T(8,128)(2,1)}, bf16[2,48,1024]{1,2,0:T(8,128)(2,1)S(1)}, u32[]{:S(2)}) copy-start(bf16[2,48,1024]{1,2,0:T(8,128)(2,1)S(1)} %bitcast_dynamic-update-slice_fusion.20) | copy-start | bytes 589828 | tf_op jit(solution)/shard_map/while
  678.1 41.1 %reduce-scatter.38.cloned.1.call-start = ((), (), s32[]{:S(2)}) async-start(), calls=%async_computation.28 | async-start | bytes 1179648 | tf_op jit(solution)/shard_map/while
  688.4 64.4 %reduce-scatter.36.cloned.1.call-start = ((), (), s32[]{:S(2)}) async-start(), calls=%async_computation.27 | async-start | bytes 1179648 | tf_op jit(solution)/shard_map/while
  692.1 28.2 %copy-start.48 = (bf16[2,64,1024]{1,2,0:T(8,128)(2,1)S(1)}, bf16[2,64,1024]{1,2,0:T(8,128)(2,1)}, u32[]{:S(2)}) copy-start(bf16[2,64,1024]{1,2,0:T(8,128)(2,1)} %get-tuple-element.965) | copy-start | bytes 786436 | tf_op jit(solution)/shard_map/while
  692.1 61.8 %copy-start.52 = (bf16[2,64,1024]{1,2,0:T(8,128)(2,1)S(1)}, bf16[2,64,1024]{1,2,0:T(8,128)(2,1)}, u32[]{:S(2)}) copy-start(bf16[2,64,1024]{1,2,0:T(8,128)(2,1)} %get-tuple-element.964) | copy-start | bytes 786436 | tf_op jit(solution)/shard_map/while
  692.6 62.2 %copy-start.32 = (bf16[2,64,1024]{2,1,0:T(8,128)(2,1)S(1)}, bf16[2,64,1024]{2,1,0:T(8,128)(2,1)}, u32[]{:S(2)}) copy-start(bf16[2,64,1024]{2,1,0:T(8,128)(2,1)} %copy-done.31) | copy-start | bytes 786436 | tf_op jit(solution)/shard_map/while
  720.4 33.6 %copy-start.49 = (bf16[2,64,1024]{1,2,0:T(8,128)(2,1)}, bf16[2,64,1024]{1,2,0:T(8,128)(2,1)S(1)}, u32[]{:S(2)}) copy-start(bf16[2,64,1024]{1,2,0:T(8,128)(2,1)S(1)} %bitcast_dynamic-update-slice_fusion.22) | copy-start | bytes 786436 | tf_op jit(solution)/shard_map/while
  754.8 40.7 %reduce-scatter.38.cloned.1.call-start = ((), (), s32[]{:S(2)}) async-start(), calls=%async_computation.28 | async-start | bytes 1179648 | tf_op jit(solution)/shard_map/while
  765.0 63.9 %reduce-scatter.36.cloned.1.call-start = ((), (), s32[]{:S(2)}) async-start(), calls=%async_computation.27 | async-start | bytes 1179648 | tf_op jit(solution)/shard_map/while
  768.7 27.9 %copy-start.48 = (bf16[2,64,1024]{1,2,0:T(8,128)(2,1)S(1)}, bf16[2,64,1024]{1,2,0:T(8,128)(2,1)}, u32[]{:S(2)}) copy-start(bf16[2,64,1024]{1,2,0:T(8,128)(2,1)} %get-tuple-element.965) | copy-start | bytes 786436 | tf_op jit(solution)/shard_map/while
  768.7 61.3 %copy-start.52 = (bf16[2,64,1024]{1,2,0:T(8,128)(2,1)S(1)}, bf16[2,64,1024]{1,2,0:T(8,128)(2,1)}, u32[]{:S(2)}) copy-start(bf16[2,64,1024]{1,2,0:T(8,128)(2,1)} %get-tuple-element.964) | copy-start | bytes 786436 | tf_op jit(solution)/shard_map/while
  769.1 61.7 %copy-start.32 = (bf16[2,64,1024]{2,1,0:T(8,128)(2,1)S(1)}, bf16[2,64,1024]{2,1,0:T(8,128)(2,1)}, u32[]{:S(2)}) copy-start(bf16[2,64,1024]{2,1,0:T(8,128)(2,1)} %copy-done.31) | copy-start | bytes 786436 | tf_op jit(solution)/shard_map/while
  796.7 33.4 %copy-start.49 = (bf16[2,64,1024]{1,2,0:T(8,128)(2,1)}, bf16[2,64,1024]{1,2,0:T(8,128)(2,1)S(1)}, u32[]{:S(2)}) copy-start(bf16[2,64,1024]{1,2,0:T(8,128)(2,1)S(1)} %bitcast_dynamic-update-slice_fusion.22) | copy-start | bytes 786436 | tf_op jit(solution)/shard_map/while
  830.9 206.6 %reduce-scatter.30.cloned.1.call-start = ((), (), s32[]{:S(2)}) async-start(), calls=%async_computation.23 | async-start | bytes 18874368
  870.7 275.3 %all-reduce.4.cloned.1.call-start = ((), (), s32[]{:S(2)}) async-start(), calls=%async_computation.24 | async-start | bytes 8388608 | tf_op jit(solution)/shard_map/psum | solution.py:282
  1045.4 44.4 %copy-start.16 = (bf16[1024,1024]{1,0:T(8,128)(2,1)S(1)}, bf16[1024,1024]{1,0:T(8,128)(2,1)}, u32[]{:S(2)}) copy-start(bf16[1024,1024]{1,0:T(8,128)(2,1)} %all-gather.28.cloned.1.call-done) | copy-start | bytes 6291460
  (64 other events, 155.4 us)
Sparse Core Ops, SparseCore 0:
  9.6 31.7 all-gather.27
  43.1 28.5 all-gather.33
  73.3 28.5 all-gather.15
  103.4 28.5 all-gather.21
  133.5 28.5 all-gather.19
  164.2 24.5 all-gather.29
  191.0 24.5 all-gather.35
  217.7 28.6 all-gather.17
  248.6 28.5 all-gather.23
  278.7 28.5 all-gather.25
  308.9 28.5 all-gather.31
  339.0 28.5 all-gather.37
  371.1 28.5 all-gather.39
  413.1 35.2 reduce-scatter.25
  452.1 27.8 all-gather.41
  488.8 35.2 reduce-scatter.27
  537.6 30.3 reduce-scatter.33
  570.7 29.8 reduce-scatter.31
  609.8 29.6 reduce-scatter.33
  642.2 29.6 reduce-scatter.31
  688.6 30.6 reduce-scatter.37
  722.2 30.6 reduce-scatter.35
  765.1 30.3 reduce-scatter.37
  798.3 30.5 reduce-scatter.35
  870.8 166.6 reduce-scatter.29
  1041.8 104.1 all-reduce.3
where the time goes:
time: 1180 us; the launch traced here: 1170 us
  waiting for transfers between devices  847 us (72%)
  local copies, waits for them, and re-layouts  134 us (11%)
  matrix products  90.3 us (8%)
  blocking collectives  49.7 us (4%)
  other arithmetic  29.7 us (3%)
  between operations  15.1 us (1%)
    while x16, waiting for transfers between devices  232 us
    unnamed x19, waiting for transfers between devices  164 us
    psum x1, waiting for transfers between devices, shards(): lax.psum(attn_grads.astype(jnp.bfloat16), 'items').astype(jnp.float32)  49.3 us
    unnamed x119, local copies, waits for them, and re-layouts  43.2 us
    psum x1, blocking collectives, shards(): lax.psum((jnp.stack([gain_one, gain_two, gain_three]), jnp.stack([bias_on...  39.5 us
    reduce_scatter x1, waiting for transfers between devices, shards(): lax.psum_scatter(jnp.dot(grad_pre, ffn_in.T, preferred_element_type=jnp.f...  35.4 us
    reduce_scatter x1, waiting for transfers between devices, shards(): lax.psum_scatter(jnp.dot(act, ffn_out, preferred_element_type=jnp.float32...  34.5 us
    all_gather x1, waiting for transfers between devices, shards(): lax.all_gather(cross_value, 'seq', axis=0, tiled=True)  30.8 us
  transfers between devices with their start and end apart: 26, of which 26 were waited for; matrix products, arithmetic and copies ran while one was open for 9% of the time, Pallas kernels for 0%

commit v1 on v0

v1 whole, which is shorter than its diff:
```python
import functools

import jax
import jax.numpy as jnp
from jax import lax
from jax.experimental import pallas as pl
from jax.experimental.pallas import tpu as pltpu
from jax.sharding import PartitionSpec as P

HEAD_DIM = 64
EPS = 1e-05
NEG = -1e30
SCALE = HEAD_DIM ** (-0.5)
BF = jnp.bfloat16
F32 = jnp.float32
VMEM_BYTES = 58 * 1024 * 1024
MESH = pl.DeviceIdType.MESH
VM = pl.BlockSpec(memory_space=pltpu.VMEM)
HBM = pl.BlockSpec(memory_space=pl.ANY)
SM = pl.BlockSpec(memory_space=pltpu.SMEM)


def nn(left, right):
    return lax.dot_general(left, right, (((1,), (0,)), ((), ())), preferred_element_type=F32)


def nt(left, right):
    return lax.dot_general(left, right, (((1,), (1,)), ((), ())), preferred_element_type=F32)


def tn(left, right):
    return lax.dot_general(left, right, (((0,), (0,)), ((), ())), preferred_element_type=F32)


class Link:
    def __init__(self, send_sems, recv_sems):
        self.send_sems, self.recv_sems, self.count, self.open = send_sems, recv_sems, 0, []

    def make(self, src, dst, device):
        index = self.count
        self.count += 1
        return pltpu.make_async_remote_copy(
            src_ref=src,
            dst_ref=dst,
            send_sem=self.send_sems.at[index],
            recv_sem=self.recv_sems.at[index],
            device_id=device,
            device_id_type=MESH,
        )

    def send(self, src, dst, device):
        copy = self.make(src, dst, device)
        copy.start()
        self.open.append(copy)
        return copy

    def local(self, src, dst):
        index = self.count
        self.count += 1
        copy = pltpu.make_async_copy(src, dst, self.send_sems.at[index])
        copy.start()
        return copy

    def finish(self):
        for copy in self.open:
            copy.wait_send()


def greet(devices):
    barrier = pltpu.get_barrier_semaphore()
    for device in devices:
        pl.semaphore_signal(barrier, inc=1, device_id=device, device_id_type=MESH)
    pl.semaphore_wait(barrier, len(devices))


class Place:
    def __init__(self, dims):
        self.dims = dims
        group, share = dims["group"], dims["share"]
        self.me = lax.axis_index("seq")
        self.h = self.me // group
        self.q = self.me % group
        self.b0 = self.q % 2
        self.b1 = (self.q // 2) % 2
        self.c = self.q // 4
        it = lax.axis_index("items")
        self.base = (it // share) * share
        self.t = it % share

    def across(self, bit):
        value = (self.q // (1 << bit)) % 2
        return {"seq": self.me + (1 - 2 * value) * (1 << bit)}

    def partner(self):
        return {"seq": (1 - self.h) * self.dims["group"] + self.q}

    def seq_shift(self, d):
        return lax.rem(self.me + d, self.dims["seq"])

    def share_shift(self, e):
        return lax.rem(self.t + e, self.dims["share"])

    def group_peers(self):
        return [self.across(bit) for bit in range(self.dims["bits"])]

    def seq_peers(self):
        return [{"seq": self.seq_shift(d)} for d in range(1, self.dims["seq"])]

    def share_peers(self):
        return [
            {"items": self.base + self.share_shift(e)} for e in range(1, self.dims["share"])
        ]


def spread_start(link, place, out, k):
    bits = place.dims["bits"]
    c, b1, b0 = place.c, place.b1, place.b0
    if bits == 3:
        step = link.send(out.at[k, c, b1, b0], out.at[k, c, b1, b0], place.across(2))
        step.wait_recv()
    waits = []
    high = link.send(out.at[k, :, b1, b0], out.at[k, :, b1, b0], place.across(1))
    waits.append(link.send(out.at[k, :, b1, b0], out.at[k, :, b1, b0], place.across(0)))
    return high, waits


def spread_end(link, place, out, k, started):
    high, waits = started
    b1, b0 = place.b1, place.b0
    high.wait_recv()
    waits.append(link.send(out.at[k, :, 1 - b1, b0], out.at[k, :, 1 - b1, b0], place.across(0)))
    return waits


def comm_call(body, name, cid, args, in_specs, out_shape, out_specs, scratch, copies):
    return pl.pallas_call(
        body,
        name=name,
        out_shape=out_shape,
        in_specs=in_specs,
        out_specs=out_specs,
        scratch_shapes=list(scratch)
        + [pltpu.SemaphoreType.DMA((copies,)), pltpu.SemaphoreType.DMA((copies,))],
        compiler_params=pltpu.CompilerParams(
            collective_id=cid, has_side_effects=True, vmem_limit_bytes=VMEM_BYTES
        ),
    )(*args)


def columns_out(link, place, src, dst, width):
    seq, group = place.dims["seq"], place.dims["group"]
    steps = []
    for d in range(1, seq):
        target = place.seq_shift(d)
        cols = pl.ds(pl.multiple_of(lax.rem(target, group) * width, width), width)
        steps.append(
            link.send(src.at[:, :, cols], dst.at[:, place.me, place.t], {"seq": target})
        )
    cols = pl.ds(pl.multiple_of(place.q * width, width), width)
    own = link.local(src.at[:, :, cols], dst.at[:, place.me, place.t])
    return steps, own


def rows_out(link, place, src, dst):
    dims, me = place.dims, place.me
    slot = lax.rem(me, dims["items_dev"])
    base = link.count
    link.count += dims["items_dev"] + 1
    copies = []
    for half in range(dims["items_dev"]):
        target = half * dims["group"] + me // dims["items_dev"]
        copy = pltpu.make_async_remote_copy(
            src_ref=src,
            dst_ref=dst.at[slot, place.t],
            send_sem=link.send_sems.at[base + half],
            recv_sem=link.recv_sems.at[base + slot],
            device_id={"seq": target},
            device_id_type=MESH,
        )
        copies.append((target != me, copy))
        pl.when(target != me)(copy.start)
    own = pltpu.make_async_copy(
        src, dst.at[slot, place.t], link.send_sems.at[base + dims["items_dev"]]
    )
    mine = me // dims["items_dev"] == place.q
    pl.when(mine)(own.start)

    def arrived():
        pl.when(mine)(own.wait)
        for block in range(dims["items_dev"]):
            copy = pltpu.make_async_remote_copy(
                src_ref=src,
                dst_ref=dst.at[block, place.t],
                send_sem=link.send_sems.at[base],
                recv_sem=link.recv_sems.at[base + block],
                device_id={"seq": me},
                device_id_type=MESH,
            )
            pl.when(place.q * dims["items_dev"] + block != me)(copy.wait_recv)

    def sent():
        for other, copy in copies:
            pl.when(other)(copy.wait_send)

    return arrived, sent


def to_share(link, place, src, dst):
    steps = []
    for e in range(1, place.dims["share"]):
        other = place.share_shift(e)
        steps.append(link.send(src(other), dst, {"items": place.base + other}))
    return steps


def arrive(steps):
    for step in steps:
        step.wait_recv()


def start_kernel(
    dims, dec, mem, cot, w_self, w_cross, w_rows, f_in, f_out,
    x_all, m_all, x_own, c_own, o_self, o_cross, o_so, o_co, o_fin, o_fout,
    send_sems, recv_sems,
):
    place = Place(dims)
    link = Link(send_sems, recv_sems)
    width = dims["width"]
    h, t = place.h, place.t
    c, b1, b0 = place.c, place.b1, place.b0
    partner = place.partner()
    greet(place.seq_peers() + place.share_peers())
    swap_x = link.send(dec.at[1 - h], x_all.at[h, c, b1, b0], partner)
    steps_self, own_self = columns_out(link, place, w_self, o_self, width)
    x_all[h, c, b1, b0] = dec[h]
    m_all[h, c, b1, b0] = mem[h]
    x_own[h] = dec[h]
    c_own[h] = cot[h]
    first_x = spread_start(link, place, x_all, h)
    so_arrived, so_sent = rows_out(link, place, w_rows.at[0], o_so)
    waits = spread_end(link, place, x_all, h, first_x)
    swap_x.wait_recv()
    x_own[1 - h] = x_all[1 - h, c, b1, b0]
    second_x = spread_start(link, place, x_all, 1 - h)
    arrive(steps_self)
    own_self.wait()
    waits += to_share(link, place, lambda _: o_self.at[:, :, t], o_self.at[:, :, t])
    so_arrived()
    waits += to_share(link, place, lambda _: o_so.at[:, t], o_so.at[:, t])
    waits += spread_end(link, place, x_all, 1 - h, second_x)
    swap_m = link.send(mem.at[1 - h], m_all.at[h, c, b1, b0], partner)
    swap_c = link.send(cot.at[1 - h], c_own.at[h], partner)
    first_m = spread_start(link, place, m_all, h)
    steps_cross, own_cross = columns_out(link, place, w_cross, o_cross, width)
    co_arrived, co_sent = rows_out(link, place, w_rows.at[1], o_co)
    step_fin = link.send(f_in, o_fin.at[t], partner)
    step_fout = link.send(f_out, o_fout.at[t], partner)
    waits += spread_end(link, place, m_all, h, first_m)
    swap_m.wait_recv()
    second_m = spread_start(link, place, m_all, 1 - h)
    waits += spread_end(link, place, m_all, 1 - h, second_m)
    arrive(steps_cross)
    own_cross.wait()
    waits += to_share(link, place, lambda _: o_cross.at[:, :, t], o_cross.at[:, :, t])
    co_arrived()
    waits += to_share(link, place, lambda _: o_co.at[:, t], o_co.at[:, t])
    step_fin.wait_recv()
    waits += to_share(link, place, lambda _: o_fin.at[t], o_fin.at[t])
    step_fout.wait_recv()
    waits += to_share(link, place, lambda _: o_fout.at[t], o_fout.at[t])
    swap_c.wait_recv()
    arrive(waits)
    so_sent()
    co_sent()
    link.finish()


class Reduce:
    def __init__(self, link, place, part, bufs):
        self.link, self.place, self.part, self.bufs = link, place, part, bufs
        self.zero, self.one = {}, {}

    def start(self, index, k):
        place = self.place
        self.zero[index] = self.link.send(
            self.part.at[k, :, :, 1 - place.b0], self.bufs[0].at[index], place.across(0)
        )

    def middle(self, index, k):
        place, part = self.place, self.part
        recv0, send1, recv1, keep1 = self.bufs[:4]
        self.zero[index].wait_recv()
        b1, b0 = place.b1, place.b0
        for c in range(part.shape[1]):
            value = part[k, c, 1 - b1, b0].astype(F32) + recv0[index, c, 1 - b1].astype(F32)
            send1[index, c] = value.astype(BF)
        self.one[index] = self.link.send(send1.at[index], recv1.at[index], place.across(1))
        for c in range(part.shape[1]):
            keep1[index, c] = part[k, c, b1, b0].astype(F32) + recv0[index, c, b1].astype(F32)

    def end(self, index):
        place = self.place
        recv1, keep1 = self.bufs[2:4]
        self.one[index].wait_recv()
        if place.dims["bits"] == 2:
            return keep1[index, 0] + recv1[index, 0].astype(F32)
        send2, recv2 = self.bufs[4:6]
        c = place.c
        send2[index] = (keep1[index, 1 - c] + recv1[index, 1 - c].astype(F32)).astype(BF)
        step = self.link.send(send2.at[index], recv2.at[index], place.across(2))
        kept = keep1[index, c] + recv1[index, c].astype(F32)
        step.wait_recv()
        return kept + recv2[index].astype(F32)


def reduce_bufs(dims, rows):
    items_dev, width, chips = dims["items_dev"], dims["model"], dims["chips"]
    bufs = [
        pltpu.VMEM((items_dev, chips, 2, rows, width), BF),
        pltpu.VMEM((items_dev, chips, rows, width), BF),
        pltpu.VMEM((items_dev, chips, rows, width), BF),
        pltpu.VMEM((items_dev, chips, rows, width), F32),
    ]
    if dims["bits"] == 3:
        bufs += [pltpu.VMEM((items_dev, rows, width), BF) for _ in range(2)]
    return bufs


def moments(value):
    mean = jnp.mean(value, axis=-1, keepdims=True)
    centered = value - mean
    inv = lax.rsqrt(jnp.mean(centered * centered, axis=-1, keepdims=True) + EPS)
    return centered * inv, inv


def norm_back(normed, inv, gain, grad):
    scaled = grad * gain
    mean = jnp.mean(scaled, axis=-1, keepdims=True)
    cross = jnp.mean(scaled * normed, axis=-1, keepdims=True)
    return inv * (scaled - mean - normed * cross)


def stage_kernel(dims, n_in, n_out, mid, *refs):
    part, ins = refs[0], refs[1 : 1 + n_in]
    outs = refs[1 + n_in : 1 + n_in + n_out]
    spread = outs[0]
    bufs = refs[1 + n_in + n_out : -2]
    place = Place(dims)
    link = Link(*refs[-2:])
    greet(place.group_peers())
    reduce = Reduce(link, place, part, bufs)
    count = dims["items_dev"]
    for k in range(count):
        reduce.start(k, k)
    for k in range(count):
        reduce.middle(k, k)
    started, waits = [], []
    for k in range(count):
        spread[k, place.c, place.b1, place.b0] = mid(k, reduce.end(k), ins, outs[1:])
        started.append(spread_start(link, place, spread, k))
    for k in range(count):
        waits += spread_end(link, place, spread, k, started[k])
    arrive(waits)
    link.finish()


def mid_forward(k, total, ins, outs):
    res, gain, bias = ins
    summed, out = outs
    value = res[k].astype(F32) + total
    summed[k] = value
    normed, _ = moments(value)
    result = normed * gain[...] + bias[...]
    out[k] = result
    return result.astype(BF)


def add_sums(k, sums, normed, grad):
    new = jnp.concatenate(
        [jnp.sum(grad * normed, axis=0, keepdims=True), jnp.sum(grad, axis=0, keepdims=True)], axis=0
    )
    sums[...] = new if k == 0 else sums[...] + new


def mid_turn(k, total, ins, outs):
    res, gain, bias, keep, cot = ins
    layer, grad_out, sums = outs
    normed, inv = moments(res[k] + total)
    kept = keep[k, :, 0:1] > 0.5
    layer[k] = jnp.where(kept, normed * gain[...] + bias[...], 0.0).astype(BF)
    grad = jnp.where(kept, cot[k].astype(F32), 0.0)
    add_sums(k, sums, normed, grad)
    result = norm_back(normed, inv, gain[...], grad)
    grad_out[k] = result
    return result.astype(BF)


def mid_backward(k, total, ins, outs):
    res, summed, gain = ins
    grad_out, sums = outs
    normed, inv = moments(summed[k])
    grad = res[k] + total
    add_sums(k, sums, normed, grad)
    result = norm_back(normed, inv, gain[...], grad)
    grad_out[k] = result
    return result.astype(BF)


def last_kernel(dims, part_x, part_m, res, layer, grad_dec, grad_mem, layer_out, *refs):
    place = Place(dims)
    link = Link(*refs[-2:])
    many = len(refs[:-2]) // 2
    bufs_x, send_x, recv_x = refs[: many - 2], refs[many - 2], refs[many - 1]
    bufs_m, send_m, recv_m = refs[many : 2 * many - 2], refs[2 * many - 2], refs[2 * many - 1]
    h, partner = place.h, place.partner()
    greet(place.group_peers() + [partner])
    red_x = Reduce(link, place, part_x, bufs_x)
    red_m = Reduce(link, place, part_m, bufs_m)
    ks = (1 - h, h)
    for red in (red_x, red_m):
        for index in range(2):
            red.start(index, ks[index])
    for red in (red_x, red_m):
        for index in range(2):
            red.middle(index, ks[index])
    swap_l = link.send(layer.at[1 - h], layer_out.at[h], partner)
    layer_out[h] = layer[h]
    send_x[...] = (red_x.end(0) + res[1 - h]).astype(BF)
    swap_x = link.send(send_x, recv_x, partner)
    grad_dec[h] = red_x.end(1) + res[h]
    send_m[...] = red_m.end(0).astype(BF)
    swap_m = link.send(send_m, recv_m, partner)
    grad_mem[h] = red_m.end(1)
    swap_x.wait_recv()
    grad_dec[1 - h] = recv_x[...].astype(F32)
    swap_m.wait_recv()
    grad_mem[1 - h] = recv_m[...].astype(F32)
    swap_l.wait_recv()
    link.finish()


def grads_items_kernel(
    dims, g_cross, g_self, g_co, g_so, g_fin, g_fout, sums,
    r_cross, r_self, r_co, r_so, r_fin, r_fout, r_sums, send_sems, recv_sems,
):
    place = Place(dims)
    link = Link(send_sems, recv_sems)
    t = place.t
    greet(place.seq_peers() + place.share_peers())
    waits, own = [], []
    for src, dst in (
        (g_fin, r_fin), (g_fout, r_fout), (g_co, r_co), (g_so, r_so),
    ):
        waits += to_share(link, place, lambda p, s=src: s.at[:, p], dst.at[t])
        own.append(link.local(src.at[:, t], dst.at[t]))
    for src, dst in ((g_cross, r_cross), (g_self, r_self)):
        waits += to_share(link, place, lambda p, s=src: s.at[:, :, p], dst.at[t])
        own.append(link.local(src.at[:, :, t], dst.at[t]))
    for d in range(1, dims["seq"]):
        target = {"seq": place.seq_shift(d)}
        waits.append(link.send(sums, r_sums.at[place.me], target))
    own.append(link.local(sums, r_sums.at[place.me]))
    arrive(waits)
    for copy in own:
        copy.wait()
    link.finish()


def rows_back(link, place, src, dst):
    dims, me, h = place.dims, place.me, place.h
    count = dims["items_dev"]
    base = link.count
    link.count += count + 1
    copies = []
    for k in range(count):
        target = place.q * count + k
        copy = pltpu.make_async_remote_copy(
            src_ref=src.at[k],
            dst_ref=dst.at[h],
            send_sem=link.send_sems.at[base + k],
            recv_sem=link.recv_sems.at[base + h],
            device_id={"seq": target},
            device_id_type=MESH,
        )
        copies.append((target != me, copy))
        pl.when(target != me)(copy.start)
    own = pltpu.make_async_copy(
        src.at[lax.rem(me, count)], dst.at[h], link.send_sems.at[base + count]
    )
    mine = me // count == place.q
    pl.when(mine)(own.start)

    def done():
        pl.when(mine)(own.wait)
        for half in range(count):
            copy = pltpu.make_async_remote_copy(
                src_ref=src.at[0],
                dst_ref=dst.at[half],
                send_sem=link.send_sems.at[base],
                recv_sem=link.recv_sems.at[base + half],
                device_id={"seq": me},
                device_id_type=MESH,
            )
            pl.when(half * dims["group"] + me // count != me)(copy.wait_recv)
        for other, copy in copies:
            pl.when(other)(copy.wait_send)

    return done


def grads_seq_kernel(
    dims, s_cross, s_self, s_co, s_so, s_fin, s_fout, sums,
    z_cross, z_self, z_co, z_so, z_fin, z_fout, z_sums, send_sems, recv_sems,
):
    place = Place(dims)
    link = Link(send_sems, recv_sems)
    me = place.me
    greet(place.seq_peers() + place.share_peers())
    waits, own = [], []
    for src, dst in ((s_fin, z_fin), (s_fout, z_fout)):
        waits.append(link.send(src.at[1], dst, place.partner()))
    for src, dst in ((s_cross, z_cross), (s_self, z_self)):
        for d in range(1, dims["seq"]):
            target = place.seq_shift(d)
            waits.append(link.send(src.at[:, target], dst.at[me], {"seq": target}))
        own.append(link.local(src.at[:, me], dst.at[me]))
    done = [rows_back(link, place, s_co, z_co), rows_back(link, place, s_so, z_so)]
    waits += to_share(link, place, lambda p: sums, z_sums.at[place.t])
    own.append(link.local(sums, z_sums.at[place.t]))
    arrive(waits)
    for copy in own:
        copy.wait()
    for wait in done:
        wait()
    link.finish()


def grads_gather_kernel(dims, count, *refs):
    place = Place(dims)
    link = Link(*refs[-2:])
    greet(place.share_peers())
    waits, own = [], []
    for src, dst in zip(refs[:count], refs[count : 2 * count]):
        waits += to_share(link, place, lambda p, s=src: s, dst.at[place.t])
        own.append(link.local(src, dst.at[place.t]))
    arrive(waits)
    for copy in own:
        copy.wait()
    link.finish()


def call(body, name, args, in_specs, out_shape, scratch=()):
    return pl.pallas_call(
        body,
        name=name,
        out_shape=out_shape,
        in_specs=in_specs,
        out_specs=[VM] * len(out_shape),
        scratch_shapes=list(scratch),
        compiler_params=pltpu.CompilerParams(vmem_limit_bytes=VMEM_BYTES),
    )(*args)


def shape(dims, dtype):
    return jax.ShapeDtypeStruct(tuple(dims), dtype)


def half_mask(rows, half):
    return (lax.broadcasted_iota(jnp.int32, (rows, 128), 1) // HEAD_DIM) == half


def attend(q_ref, k_ref, v_ref, valid, p_ref, mix_ref, causal, block):
    rows, keys = q_ref.shape[0], k_ref.shape[0]
    for pair in range(q_ref.shape[1] // 128):
        lanes = slice(pair * 128, pair * 128 + 128)
        for start in range(0, rows, block):
            stop = start + block if causal else keys
            halves = []
            for half in range(2):
                query = q_ref[start : start + block, lanes]
                query = jnp.where(half_mask(block, half), query, jnp.zeros_like(query))
                scores = nt(k_ref[:stop, lanes], query) * SCALE
                scores = jnp.where(valid(start, stop), scores, NEG)
                top = jnp.max(scores, axis=0, keepdims=True)
                grown = jnp.exp(scores - top)
                probs = (grown * (1.0 / jnp.sum(grown, axis=0, keepdims=True))).astype(BF)
                p_ref[2 * pair + half, :stop, start : start + block] = probs
                mixed = tn(v_ref[:stop, lanes], probs)
                halves.append(mixed[half * HEAD_DIM : (half + 1) * HEAD_DIM])
            mix_ref[start : start + block, lanes] = jnp.concatenate(halves, axis=0).T.astype(BF)


def attend_back(q_ref, k_ref, v_ref, p_ref, grad_ref, dq_ref, dk_ref, dv_ref, causal, block):
    rows, keys = q_ref.shape[0], k_ref.shape[0]
    for pair in range(q_ref.shape[1] // 128):
        lanes = slice(pair * 128, pair * 128 + 128)
        dk = jnp.zeros((keys, 128), F32)
        dv = jnp.zeros((keys, 128), F32)
        for start in range(0, rows, block):
            stop = start + block if causal else keys
            halves = []
            for half in range(2):
                mask = half_mask(block, half)
                query = q_ref[start : start + block, lanes]
                query = jnp.where(mask, query, jnp.zeros_like(query))
                grad = grad_ref[start : start + block, lanes]
                grad = jnp.where(mask, grad, jnp.zeros_like(grad))
                low = p_ref[2 * pair + half, :stop, start : start + block]
                probs = low.astype(F32)
                grad_probs = nt(v_ref[:stop, lanes], grad)
                delta = jnp.sum(probs * grad_probs, axis=0, keepdims=True)
                grad_scores = (probs * (grad_probs - delta)).astype(BF)
                turned = tn(k_ref[:stop, lanes], grad_scores) * SCALE
                halves.append(turned[half * HEAD_DIM : (half + 1) * HEAD_DIM])
                new_k, new_v = nn(grad_scores, query), nn(low, grad)
                if stop < keys:
                    rest = jnp.zeros((keys - stop, 128), F32)
                    new_k = jnp.concatenate([new_k, rest], axis=0)
                    new_v = jnp.concatenate([new_v, rest], axis=0)
                dk, dv = dk + new_k, dv + new_v
            dq_ref[start : start + block, lanes] = jnp.concatenate(halves, axis=0).T.astype(BF)
        dk_ref[:, lanes] = (dk * SCALE).astype(BF)
        dv_ref[:, lanes] = dv.astype(BF)


def self_valid(length):
    def valid(start, stop, block):
        keys = lax.broadcasted_iota(jnp.int32, (stop, block), 0)
        rows = lax.broadcasted_iota(jnp.int32, (stop, block), 1) + start
        return (keys <= rows) & (keys < length)

    return valid


def self_forward(block, length, x, w, so, q, k, v, p, mix, part):
    rows = x[...]
    q[...] = nn(rows, w[0]).astype(BF)
    k[...] = nn(rows, w[1]).astype(BF)
    v[...] = nn(rows, w[2]).astype(BF)
    check = self_valid(length[0])
    attend(q, k, v, lambda a, b: check(a, b, block), p, mix, True, block)
    part[...] = nn(mix[...], so[...]).astype(BF)


def cross_forward(block, x, m, keep, w, co, q, k, v, p, mix, part):
    q[...] = nn(x[...], w[0]).astype(BF)
    k[...] = nn(m[...], w[1]).astype(BF)
    v[...] = nn(m[...], w[2]).astype(BF)
    attend(q, k, v, lambda a, b: keep[:, 0:1] > 0.5, p, mix, False, block)
    part[...] = nn(mix[...], co[...]).astype(BF)


def ffn_forward(x, w_in0, w_in1, w_out0, w_out1, act, slope, part):
    rows = x[...]
    width = w_in0.shape[1]
    for index, w_in in enumerate((w_in0, w_in1)):
        pre = nn(rows, w_in[...])
        cdf = 0.5 * (1.0 + lax.erf(pre * (0.5**0.5)))
        cols = slice(index * width, (index + 1) * width)
        act[:, cols] = (pre * cdf).astype(BF)
        slope[:, cols] = (
            cdf + pre * (jnp.exp(-0.5 * pre * pre) * 0.3989422804014327)
        ).astype(BF)
    part[...] = (nn(act[:, :width], w_out0[...]) + nn(act[:, width:], w_out1[...])).astype(BF)


def ffn_backward(x, gy, w_in0, w_in1, w_out0, w_out1, act, slope, part, g_in, g_out):
    rows, grad = x[...], gy[...]
    width = w_in0.shape[1]
    total = None
    for index, (w_in, w_out) in enumerate(((w_in0, w_out0), (w_in1, w_out1))):
        cols = slice(index * width, (index + 1) * width)
        grad_pre = (nt(grad, w_out[...]) * slope[:, cols].astype(F32)).astype(BF)
        term = nt(grad_pre, w_in[...])
        total = term if total is None else total + term
        g_in[index] = tn(rows, grad_pre).astype(BF)
        g_out[index] = tn(act[:, cols], grad).astype(BF)
    part[...] = total.astype(BF)


def cross_backward(
    block, gc, x, m, w, co, q, k, v, p, mix, part_x, part_m, g_w, g_co, dmix, dq, dk, dv
):
    grad = gc[...]
    dmix[...] = nt(grad, co[...]).astype(BF)
    attend_back(q, k, v, p, dmix, dq, dk, dv, False, block)
    part_x[...] = nt(dq[...], w[0]).astype(BF)
    part_m[...] = (nt(dk[...], w[1]) + nt(dv[...], w[2])).astype(BF)
    g_w[0] = tn(x[...], dq[...]).astype(BF)
    g_w[1] = tn(m[...], dk[...]).astype(BF)
    g_w[2] = tn(m[...], dv[...]).astype(BF)
    g_co[...] = tn(mix[...], grad).astype(BF)


def self_backward(block, gc, x, w, so, q, k, v, p, mix, part_x, g_w, g_so, dmix, dq, dk, dv):
    grad = gc[...]
    dmix[...] = nt(grad, so[...]).astype(BF)
    attend_back(q, k, v, p, dmix, dq, dk, dv, True, block)
    part_x[...] = (nt(dq[...], w[0]) + nt(dk[...], w[1]) + nt(dv[...], w[2])).astype(BF)
    rows = x[...]
    g_w[0] = tn(rows, dq[...]).astype(BF)
    g_w[1] = tn(rows, dk[...]).astype(BF)
    g_w[2] = tn(rows, dv[...]).astype(BF)
    g_so[...] = tn(mix[...], grad).astype(BF)


def shards(
    mesh, dec_in, memory, dec_len, mem_len, cell_mask, self_query, self_key, self_value, self_out,
    cross_query, cross_key, cross_value, cross_out, ffn_in, ffn_out, norm_gain, norm_bias, cotangent,
):
    items_dev, rb, model = dec_in.shape
    mb = memory.shape[1]
    seq, items = mesh.shape["seq"], mesh.shape["items"]
    group = seq // items_dev
    share = 4
    bits = group.bit_length() - 1
    chips = group // 4
    width = model // group
    dims = {
        "items_dev": items_dev, "seq": seq, "group": group, "share": share, "bits": bits,
        "chips": chips, "width": width, "model": model,
    }
    me, it = lax.axis_index("seq"), lax.axis_index("items")
    h, q, t = me // group, me % group, it % share
    total_dec, total_mem = rb * seq, mb * seq
    heads = width // HEAD_DIM
    hidden = ffn_in.shape[1]
    wr = self_query.shape[0] // share
    block = 256

    length = lax.dynamic_index_in_dim(dec_len, h, 0, keepdims=True)
    cells = lax.all_gather(cell_mask.astype(BF), "seq", axis=1, tiled=True)
    cells = lax.dynamic_index_in_dim(cells, h, 0, keepdims=False)
    spots = jnp.arange(total_mem, dtype=jnp.int32)
    mem_length = lax.dynamic_index_in_dim(mem_len, h, 0, keepdims=False)
    keep_mem = (spots < mem_length) & ((cells == 1.0) | (spots == 0))
    keep_mem = jnp.broadcast_to(keep_mem.astype(F32)[:, None], (total_mem, 128))
    row_pos = (
        lax.broadcasted_iota(jnp.int32, (items_dev, rb, 128), 0) * group + q
    ) * rb + lax.broadcasted_iota(jnp.int32, (items_dev, rb, 128), 1)
    keep_row = (row_pos < length[0]).astype(F32)

    def quarter(value, rows):
        return lax.dynamic_slice_in_dim(value, t * rows, rows, axis=0)

    w_self_q = jnp.stack([quarter(w, wr) for w in (self_query, self_key, self_value)])
    w_cross_q = jnp.stack([quarter(w, wr) for w in (cross_query, cross_key, cross_value)])
    w_rows_q = jnp.stack([quarter(w, wr) for w in (self_out, cross_out)])
    fr, gr = model // share, hidden // share
    f_in_q, f_out_q = quarter(ffn_in, fr), quarter(ffn_out, gr)

    grid = (items_dev, chips, 2, 2)
    (
        x_all, m_all, x_own, c_own, w_self, w_cross, w_so, w_co, p_fin, p_fout,
    ) = comm_call(
        functools.partial(start_kernel, dims),
        "start", 0,
        (dec_in, memory, cotangent, w_self_q, w_cross_q, w_rows_q, f_in_q, f_out_q),
        [VM, VM, VM, HBM, HBM, HBM, HBM, HBM],
        [
            shape(grid + (rb, model), BF),
            shape(grid + (mb, model), BF),
            shape((items_dev, rb, model), BF),
            shape((items_dev, rb, model), BF),
            shape((3, seq, share, wr, width), BF),
            shape((3, seq, share, wr, width), BF),
            shape((items_dev, share, wr, model), BF),
            shape((items_dev, share, wr, model), BF),
            shape((share, fr, hidden), BF),
            shape((share, gr, model), BF),
        ],
        [VM, VM, VM, VM] + [HBM] * 6,
        [], 112,
    )
    x_rows = x_all.reshape(total_dec, model)
    m_rows = m_all.reshape(total_mem, model)
    w_self = w_self.reshape(3, model, width)
    w_cross = w_cross.reshape(3, model, width)
    w_so, w_co = w_so.reshape(width, model), w_co.reshape(width, model)
    p_fin, p_fout = p_fin.reshape(model, hidden), p_fout.reshape(hidden, model)
    gains = [norm_gain[k : k + 1] for k in range(3)]
    biases = [norm_bias[k : k + 1] for k in range(3)]
    own = (items_dev, rb, model)

    def stage(name, cid, part, mid, ins, outs):
        return comm_call(
            functools.partial(stage_kernel, dims, len(ins), 1 + len(outs), mid),
            name, cid, (part.reshape(grid + (rb, model)),) + tuple(ins),
            [VM] * (1 + len(ins)),
            [shape(grid + (rb, model), BF)] + list(outs),
            [VM] * (1 + len(outs)),
            reduce_bufs(dims, rb), 24,
        )

    sq, sk, sv, sp, smix, part = call(
        functools.partial(self_forward, block), "self_forward",
        (length, x_rows, w_self, w_so), [SM, VM, VM, VM],
        [shape((total_dec, width), BF)] * 3
        + [shape((heads, total_dec, total_dec), BF), shape((total_dec, width), BF),
           shape((total_dec, model), BF)],
    )
    first_all, sum_one, first = stage(
        "first", 1, part, mid_forward, (x_own, gains[0], biases[0]), [shape(own, F32)] * 2
    )
    first_all = first_all.reshape(total_dec, model)
    cq, ck, cv, cp, cmix, part = call(
        functools.partial(cross_forward, block), "cross_forward",
        (first_all, m_rows, keep_mem, w_cross, w_co), [VM] * 5,
        [shape((total_dec, width), BF)] + [shape((total_mem, width), BF)] * 2
        + [shape((heads, total_mem, total_dec), BF), shape((total_dec, width), BF),
           shape((total_dec, model), BF)],
    )
    second_all, sum_two, second = stage(
        "second", 2, part, mid_forward, (first, gains[1], biases[1]), [shape(own, F32)] * 2
    )
    second_all = second_all.reshape(total_dec, model)
    act, slope, part = call(
        ffn_forward, "ffn_forward", (second_all, ffn_in, p_fin, ffn_out, p_fout), [VM] * 5,
        [shape((total_dec, 2 * hidden), BF)] * 2 + [shape((total_dec, model), BF)],
    )
    gy_all, layer, grad_third, sums_three = stage(
        "turn", 3, part, mid_turn, (second, gains[2], biases[2], keep_row, c_own),
        [shape(own, BF), shape(own, F32), shape((2, model), F32)],
    )
    part, g_fin, g_fout = call(
        ffn_backward, "ffn_backward",
        (second_all, gy_all.reshape(total_dec, model), ffn_in, p_fin, ffn_out, p_fout, act, slope),
        [VM] * 8,
        [shape((total_dec, model), BF), shape((2, model, hidden), BF), shape((2, hidden, model), BF)],
    )
    gc_all, grad_r2, sums_two = stage(
        "back_second", 4, part, mid_backward, (grad_third, sum_two, gains[1]),
        [shape(own, F32), shape((2, model), F32)],
    )
    part, part_m, g_cross, g_co = call(
        functools.partial(cross_backward, block), "cross_backward",
        (gc_all.reshape(total_dec, model), first_all, m_rows, w_cross, w_co, cq, ck, cv, cp, cmix),
        [VM] * 10,
        [shape((total_dec, model), BF), shape((total_mem, model), BF),
         shape((3, model, width), BF), shape((width, model), BF)],
        [pltpu.VMEM((total_dec, width), BF)] * 2 + [pltpu.VMEM((total_mem, width), BF)] * 2,
    )
    gc_all, grad_r1, sums_one = stage(
        "back_first", 5, part, mid_backward, (grad_r2, sum_one, gains[0]),
        [shape(own, F32), shape((2, model), F32)],
    )
    part, g_self, g_so = call(
        functools.partial(self_backward, block), "self_backward",
        (gc_all.reshape(total_dec, model), x_rows, w_self, w_so, sq, sk, sv, sp, smix),
        [VM] * 9,
        [shape((total_dec, model), BF), shape((3, model, width), BF), shape((width, model), BF)],
        [pltpu.VMEM((total_dec, width), BF)] * 4,
    )
    swap = [pltpu.VMEM((rb, model), BF)] * 2, [pltpu.VMEM((mb, model), BF)] * 2
    grad_dec, grad_memory, layer_out = comm_call(
        functools.partial(last_kernel, dims), "last", 6,
        (part.reshape(grid + (rb, model)), part_m.reshape(grid + (mb, model)), grad_r1, layer),
        [VM] * 4,
        [shape(own, F32), shape((items_dev, mb, model), F32), shape(own, BF)],
        [VM] * 3,
        reduce_bufs(dims, rb) + swap[0] + reduce_bufs(dims, mb) + swap[1], 24,
    )
    sums = jnp.concatenate([sums_one, sums_two, sums_three, jnp.zeros((2, model), F32)], axis=0)
    received = comm_call(
        functools.partial(grads_items_kernel, dims), "grads_items", 7,
        (
            g_cross.reshape(3, seq, share, wr, width),
            g_self.reshape(3, seq, share, wr, width),
            g_co.reshape(items_dev, share, wr, model),
            g_so.reshape(items_dev, share, wr, model),
            g_fin.reshape(2, share, fr, hidden),
            g_fout.reshape(2, share, gr, model),
            sums,
        ),
        [HBM] * 7,
        [
            shape((share, 3, seq, wr, width), BF),
            shape((share, 3, seq, wr, width), BF),
            shape((share, items_dev, wr, model), BF),
            shape((share, items_dev, wr, model), BF),
            shape((share, 2, fr, hidden), BF),
            shape((share, 2, gr, model), BF),
            shape((seq, 8, model), F32),
        ],
        [HBM] * 7, [], 56,
    )

    def over_groups(value):
        if items == share:
            return value
        lines = [[a * share + b for a in range(items // share)] for b in range(share)]
        return lax.psum(value, "items", axis_index_groups=lines)

    quarters = [
        over_groups(jnp.sum(value.astype(F32), axis=0).astype(BF)) for value in received[:6]
    ]
    sums = over_groups(jnp.sum(received[6], axis=0))
    moved = comm_call(
        functools.partial(grads_seq_kernel, dims), "grads_seq", 8,
        tuple(quarters) + (sums,), [HBM] * 7,
        [
            shape((seq, 3, wr, width), BF),
            shape((seq, 3, wr, width), BF),
            shape((items_dev, wr, model), BF),
            shape((items_dev, wr, model), BF),
            shape((fr, hidden), BF),
            shape((gr, model), BF),
            shape((share, 8, model), F32),
        ],
        [HBM] * 7, [], 56,
    )

    def whole_rows(value):
        value = value.reshape(items_dev, group, 3, wr, width).astype(F32).sum(axis=0)
        return value.transpose(1, 2, 0, 3).reshape(3, wr, model).astype(BF)

    done = [
        whole_rows(moved[0]),
        whole_rows(moved[1]),
        moved[2].astype(F32).sum(axis=0).astype(BF),
        moved[3].astype(F32).sum(axis=0).astype(BF),
        (moved[4].astype(F32) + quarters[4][0].astype(F32)).astype(BF),
        (moved[5].astype(F32) + quarters[5][0].astype(F32)).astype(BF),
    ]
    sums = jnp.sum(moved[6], axis=0)
    final = comm_call(
        functools.partial(grads_gather_kernel, dims, 6), "grads_gather", 9,
        tuple(done), [HBM] * 6,
        [shape((share,) + value.shape, BF) for value in done],
        [HBM] * 6, [], 24,
    )
    f_cross = final[0].transpose(1, 0, 2, 3).reshape(3, share * wr, model).astype(F32)
    f_self = final[1].transpose(1, 0, 2, 3).reshape(3, share * wr, model).astype(F32)
    f_co = final[2].reshape(share * wr, model).astype(F32)
    f_so = final[3].reshape(share * wr, model).astype(F32)
    return (
        layer_out, grad_dec, grad_memory,
        f_self[0], f_self[1], f_self[2], f_so,
        f_cross[0], f_cross[1], f_cross[2], f_co,
        final[4].reshape(model, hidden).astype(F32),
        final[5].reshape(hidden, model).astype(F32),
        sums[0:6:2], sums[1:6:2],
    )


def solution(mesh):
    rows = P("seq", None)
    tokens = P("items", "seq", None)
    placed = (
        (tokens, tokens, P("items"), P("items"), P("items", "seq"))
        + (rows,) * 8
        + (P(None, "seq"), rows, P(), P(), tokens)
    )
    return jax.shard_map(
        functools.partial(shards, mesh),
        mesh=mesh,
        in_specs=placed,
        out_specs=(tokens,) * 3 + (rows,) * 8 + (P(None, "seq"), rows, P(), P()),
        check_vma=False,
    )
```

time: 1180 us -> 541 us (0.46)
  waiting for transfers between devices: 847 us -> 0 us
  Pallas kernels: 0 us -> 480 us
  local copies, waits for them, and re-layouts: 134 us -> 20.1 us
  matrix products: 90.3 us -> 0 us
  blocking collectives: 49.7 us -> 11.2 us
  between operations: 15.1 us -> 0.96 us
    pallas_call x0 -> x16, Pallas kernels: none -> 480 us  [the longest x10 429 us: comm_call(): pl.pallas_call(body, name=name, out_shape=out_shape, in_specs=in_specs, o...]
    all_gather x14 -> x0, waiting for transfers between devices: 332 us -> none  [the longest x1 30.8 us: shards(): lax.all_gather(cross_value, 'seq', axis=0, tiled=True)]
    while x16 -> x0, waiting for transfers between devices: 232 us -> none
    unnamed x19 -> x0, waiting for transfers between devices: 164 us -> none
    dot_general x58 -> x0, matrix products: 90.3 us -> none  [the longest x8 18.1 us: shards(): jnp.dot(left.T, right, preferred_element_type=jnp.float32)]
    reduce_scatter x2 -> x0, waiting for transfers between devices: 69.9 us -> none  [the longest x1 35.4 us: shards(): lax.psum_scatter(jnp.dot(grad_pre, ffn_in.T, preferred_element_type=jnp.f...]
    while x121 -> x0, local copies, waits for them, and re-layouts: 52.4 us -> none
    psum x1 -> x0, waiting for transfers between devices: 49.3 us -> none  [shards(): lax.psum(attn_grads.astype(jnp.bfloat16), 'items').astype(jnp.float32)]
  transfers between devices with their start and end apart: 26 -> 0, of which waited for: 26 -> 0; matrix products, arithmetic and copies ran while one was open for 9% -> 0% of each run, Pallas kernels for 0% -> 0%
where the time goes in v1:
time: 541 us; the launch traced here: 540 us
  Pallas kernels  480 us (89%)
  other arithmetic  27.5 us (5%)
  local copies, waits for them, and re-layouts  20.1 us (4%)
  blocking collectives  11.2 us (2%)
    pallas_call x10, Pallas kernels, comm_call(): pl.pallas_call(body, name=name, out_shape=out_shape, in_specs=in_specs, o...  429 us
    pallas_call x6, Pallas kernels, call(): pl.pallas_call(body, name=name, out_shape=out_shape, in_specs=in_specs, o...  51 us
    all_gather x1, blocking collectives, shards(): cells = lax.all_gather(cell_mask.astype(BF), 'seq', axis=1, tiled=True)  11.2 us

profile of v1, /device:TPU:0, one launch (start us, length us, event | category | flops | bytes accessed | tf_op | source)
XLA Modules:
  0.0 539.8 jit_solution(411258204854480167)
XLA Ops:
  0.7 0.9 dynamic-slice_bitcast_fusion.2
  1.6 0.9 dynamic-slice_bitcast_fusion.4
  2.4 0.7 pad_maximum_fusion.1.w_cross
  3.1 0.9 dynamic-slice_bitcast_fusion.6
  4.0 0.7 pad_maximum_fusion.w_self
  4.7 0.9 dynamic-slice_bitcast_fusion
  5.6 0.7 pad_maximum_fusion.2.w_rows
  6.3 1.7 constant_dynamic-slice_fusion.1.f_out
  8.0 1.7 constant_dynamic-slice_fusion.2.f_in
  9.6 106.5 %start.1 = (bf16[2,1,2,2,64,1024]{5,4,3,2,1,0:T(8,128)(2,1)}, bf16[2,1,2,2,48,1024]{5,4,3,2,1,0:T(8,128)(2,1)}, bf16[2,64,1024]{2,1,0:T(8,128)(2,1)}, bf16[2,64,...) custom-call(bf16[2,64,1024]{2,1,0:T(8,128)(2,1)} %dec.1, ...), custom_call_target="tpu_custom_call" | custom-call | tf_op jit(solution)/shard_map/start/pallas_call | solution.py:136
  116.2 0.6 dynamic_slice.42.length
  116.8 7.8 %self_forward.1 = (bf16[512,256]{1,0:T(8,128)(2,1)}, bf16[512,256]{1,0:T(8,128)(2,1)}, bf16[512,256]{1,0:T(8,128)(2,1)}, bf16[4,512,512]{2,1,0:T(8,128)(2,1)}, b...) custom-call(s32[1]{0:T(128)} %dynamic_slice.42.length, bf16[512,1024]{1,0:T(8,128)(2,1)} %bitcast.94, ...), custom_call_target="tpu_custom_call" | custom-call | tf_op jit(solution)/shard_map/self_forward/pallas_call | solution.py:553
  124.7 0.6 fusion.8
  125.3 20.5 %first.1 = (bf16[2,1,2,2,64,1024]{5,4,3,2,1,0:T(8,128)(2,1)}, f32[2,64,1024]{2,1,0:T(8,128)}, f32[2,64,1024]{2,1,0:T(8,128)}) custom-call(bf16[2,1,2,2,64,1024]{5,4,3,2,1,0:T(8,128)(2,1)} %bitcast.116, bf16[2,64,1024]{2,1,0:T(8,128)(2,1)} %get-tuple-element.93.refs_1_, f32[1,1024]{1,0:T(1,128)} %get-tuple-element.184.refs_2_.refs_3_, ...), custom_call_target="tpu_custom_call" | custom-call | tf_op jit(solution)/shard_map/first/pallas_call | solution.py:136
  145.9 11.2 %all-gather = bf16[8,48,2]{1,2,0:T(2,128)(2,1)S(1)} all-gather(bf16[1,48,2]{1,2,0:T(2,128)(2,1)S(1)} %convert_bitcast_fusion.2), channel_id=1, replica_groups=mesh['items'=4,'seq'=8] {'seq'}, dimensions={0}, use_global_device_ids=true | all-gather | bytes 1728 | tf_op jit(solution)/shard_map/all_gather | solution.py:732
  157.1 0.1 reshape.199
  157.2 0.6 dynamic_slice.53
  157.8 0.7 fusion.4
  158.4 0.8 broadcast_in_dim.4.keep
  159.2 7.2 %cross_forward.1 = (bf16[512,256]{1,0:T(8,128)(2,1)}, bf16[384,256]{1,0:T(8,128)(2,1)}, bf16[384,256]{1,0:T(8,128)(2,1)}, bf16[4,384,512]{2,1,0:T(8,128)(2,1)}, ...) custom-call(bf16[512,1024]{1,0:T(8,128)(2,1)} %bitcast.96, bf16[384,1024]{1,0:T(8,128)(2,1)} %bitcast.104, ...), custom_call_target="tpu_custom_call" | custom-call | tf_op jit(solution)/shard_map/cross_forward/pallas_call | solution.py:553
  166.4 19.8 %second.1 = (bf16[2,1,2,2,64,1024]{5,4,3,2,1,0:T(8,128)(2,1)}, f32[2,64,1024]{2,1,0:T(8,128)}, f32[2,64,1024]{2,1,0:T(8,128)}) custom-call(bf16[2,1,2,2,64,1024]{5,4,3,2,1,0:T(8,128)(2,1)} %bitcast.117, f32[2,64,1024]{2,1,0:T(8,128)} %get-tuple-element.99.refs_1_, f32[1,1024]{1,0:T(1,128)} %get-tuple-element.183.refs_2_.refs_3_, ...), custom_call_target="tpu_custom_call" | custom-call | tf_op jit(solution)/shard_map/second/pallas_call | solution.py:136
  186.2 6.4 %ffn_forward.1 = (bf16[512,1024]{1,0:T(8,128)(2,1)}, bf16[512,1024]{1,0:T(8,128)(2,1)}, bf16[512,1024]{1,0:T(8,128)(2,1)}) custom-call(bf16[512,1024]{1,0:T(8,128)(2,1)} %bitcast.102, bf16[1024,512]{1,0:T(8,128)(2,1)} %w_in0.3, bf16[1024,512]{1,0:T(8,128)(2,1)} %bitcast.98, bf16[512,1024]{1,0:T(8,128)(2,1)} %w_out0.3, bf16[512,1024]{1,0:T(8,128)(2,1)} %bitcast.100), custom_call_target="tpu_custom_call" | custom-call | tf_op jit(solution)/shard_map/ffn_forward/pallas_call | solution.py:553
  192.6 1.3 fusion.2.refs_4_
  194.0 19.8 %turn.1 = (bf16[2,1,2,2,64,1024]{5,4,3,2,1,0:T(8,128)(2,1)}, bf16[2,64,1024]{2,1,0:T(8,128)(2,1)}, f32[2,64,1024]{2,1,0:T(8,128)}, f32[2,1024]{1,0:T(2,128)}) custom-call(bf16[2,1,2,2,64,1024]{5,4,3,2,1,0:T(8,128)(2,1)} %bitcast.119, f32[2,64,1024]{2,1,0:T(8,128)} %get-tuple-element.104.refs_1_, f32[1,1024]{1,0:T(1,128)} %get-tuple-element.185.refs_2_, ...), custom_call_target="tpu_custom_call" | custom-call | tf_op jit(solution)/shard_map/turn/pallas_call | solution.py:136
  213.8 9.5 %ffn_backward.1 = (bf16[512,1024]{1,0:T(8,128)(2,1)}, bf16[2,1024,512]{2,1,0:T(8,128)(2,1)}, bf16[2,512,1024]{2,1,0:T(8,128)(2,1)}) custom-call(bf16[512,1024]{1,0:T(8,128)(2,1)} %bitcast.103, bf16[512,1024]{1,0:T(8,128)(2,1)} %bitcast.122, bf16[1024,512]{1,0:T(8,128)(2,1)} %w_in0.3, bf16[1024,512]{1,0:T(8,128)(2,1)} %bitcast.99, bf16[512,1024]{1,0:T(8,128)(2,1)} %w_out0.3, ...), custom_call_target="tpu_custom_call" | custom-call | tf_op jit(solution)/shard_map/ffn_backward/pallas_call | solution.py:553
  223.3 20.1 %back_second.1 = (bf16[2,1,2,2,64,1024]{5,4,3,2,1,0:T(8,128)(2,1)}, f32[2,64,1024]{2,1,0:T(8,128)}, f32[2,1024]{1,0:T(2,128)}) custom-call(bf16[2,1,2,2,64,1024]{5,4,3,2,1,0:T(8,128)(2,1)} %bitcast.121, f32[2,64,1024]{2,1,0:T(8,128)} %get-tuple-element.110.refs_1_, f32[2,64,1024]{2,1,0:T(8,128)} %get-tuple-element.111.refs_2_, ...), custom_call_target="tpu_custom_call" | custom-call | tf_op jit(solution)/shard_map/back_second/pallas_call | solution.py:136
  243.4 9.6 %cross_backward.1 = (bf16[512,1024]{1,0:T(8,128)(2,1)}, bf16[384,1024]{1,0:T(8,128)(2,1)}, bf16[3,1024,256]{2,1,0:T(8,128)(2,1)}, bf16[256,1024]{1,0:T(8,128)(2,1)}) custom-call(bf16[512,1024]{1,0:T(8,128)(2,1)} %bitcast.115, bf16[512,1024]{1,0:T(8,128)(2,1)} %bitcast.97, bf16[384,1024]{1,0:T(8,128)(2,1)} %bitcast.105, bf16[3,1024,256]{2,1,0:T(8,128)(2,1)} %bitcast.93, ...), custom_call_target="tpu_custom_call" | custom-call | tf_op jit(solution)/shard_map/cross_backward/pallas_call | solution.py:553
  253.0 19.8 %back_first.1 = (bf16[2,1,2,2,64,1024]{5,4,3,2,1,0:T(8,128)(2,1)}, f32[2,64,1024]{2,1,0:T(8,128)}, f32[2,1024]{1,0:T(2,128)}) custom-call(bf16[2,1,2,2,64,1024]{5,4,3,2,1,0:T(8,128)(2,1)} %bitcast.120, f32[2,64,1024]{2,1,0:T(8,128)} %get-tuple-element.119.refs_1_, f32[2,64,1024]{2,1,0:T(8,128)} %get-tuple-element.120.refs_2_, ...), custom_call_target="tpu_custom_call" | custom-call | tf_op jit(solution)/shard_map/back_first/pallas_call | solution.py:136
  272.9 1.4 maximum_maximum_fusion.sums
  274.3 10.5 %self_backward.1 = (bf16[512,1024]{1,0:T(8,128)(2,1)}, bf16[3,1024,256]{2,1,0:T(8,128)(2,1)}, bf16[256,1024]{1,0:T(8,128)(2,1)}) custom-call(bf16[512,1024]{1,0:T(8,128)(2,1)} %bitcast.114, bf16[512,1024]{1,0:T(8,128)(2,1)} %bitcast.95, bf16[3,1024,256]{2,1,0:T(8,128)(2,1)} %bitcast.91, bf16[256,1024]{1,0:T(8,128)(2,1)} %bitcast.109, ...), custom_call_target="tpu_custom_call" | custom-call | tf_op jit(solution)/shard_map/self_backward/pallas_call | solution.py:553
  284.8 95.5 %grads_items.1 = (bf16[4,3,8,32,256]{4,3,2,1,0:T(8,128)(2,1)}, bf16[4,3,8,32,256]{4,3,2,1,0:T(8,128)(2,1)}, bf16[4,2,32,1024]{3,2,1,0:T(8,128)(2,1)}, bf16[4,2,3...) custom-call(bf16[3,8,4,32,256]{4,3,2,1,0:T(8,128)(2,1)} %bitcast.112, ...), custom_call_target="tpu_custom_call" | custom-call | tf_op jit(solution)/shard_map/grads_items/pallas_call | solution.py:136
  380.4 3.0 reduce_sum.136.s_fin
  383.4 1.6 reduce_sum.137.s_fout
  384.9 2.7 reduce_sum.132.s_cross
  387.6 1.1 reduce_sum.133.s_self
  388.8 0.7 reduce_sum.134.s_co
  389.5 0.7 reduce_sum.135.s_so
  390.3 0.6 reduce_sum.138.sums
  390.9 49.3 %grads_seq.1 = (bf16[8,3,32,256]{3,2,1,0:T(8,128)(2,1)}, bf16[8,3,32,256]{3,2,1,0:T(8,128)(2,1)}, bf16[2,32,1024]{2,1,0:T(8,128)(2,1)}, bf16[2,32,1024]{2,1,0:T(...) custom-call(bf16[3,8,32,256]{3,2,1,0:T(8,128)(2,1)} %reduce_sum.132.s_cross, ...), custom_call_target="tpu_custom_call" | custom-call | tf_op jit(solution)/shard_map/grads_seq/pallas_call | solution.py:136
  440.3 1.8 fusion.refs_5_
  442.1 1.8 fusion.1.refs_4_
  443.8 0.1 reduce.8
  443.9 0.7 copy.37
  444.6 0.1 reduce.9
  444.7 0.7 copy.38
  445.4 0.7 reduce_sum.141.refs_2_
  446.0 0.7 reduce_sum.142.refs_3_
  446.7 50.0 %grads_gather.1 = (bf16[4,3,32,1024]{3,2,1,0:T(8,128)(2,1)}, bf16[4,3,32,1024]{3,2,1,0:T(8,128)(2,1)}, bf16[4,32,1024]{2,1,0:T(8,128)(2,1)}, bf16[4,32,1024]{2,1...) custom-call(bf16[3,32,1024]{2,1,0:T(8,128)(2,1)} %bitcast.123, ...), custom_call_target="tpu_custom_call" | custom-call | tf_op jit(solution)/shard_map/grads_gather/pallas_call | solution.py:136
  496.7 1.3 convert_bitcast_fusion.1
  498.0 1.2 fusion.7
  499.1 0.4 copy-done.6
  499.5 0.2 convert_bitcast_fusion
  499.7 1.2 fusion.6
  500.9 0.6 copy-done.5
  501.5 1.6 bitcast_convert_fusion
  503.2 1.7 bitcast_convert_fusion.1
  504.8 0.9 bitcast_convert_fusion.2
  505.7 0.9 bitcast_convert_fusion.3
  506.6 0.6 slice.68
  507.2 0.6 slice.69
  507.8 27.6 %last.1 = (f32[2,64,1024]{2,1,0:T(8,128)}, f32[2,48,1024]{2,1,0:T(8,128)}, bf16[2,64,1024]{2,1,0:T(8,128)(2,1)}) custom-call(bf16[2,1,2,2,64,1024]{5,4,3,2,1,0:T(8,128)(2,1)} %bitcast.118, bf16[2,1,2,2,48,1024]{5,4,3,2,1,0:T(8,128)(2,1)} %bitcast.127, f32[2,64,1024]{2,1,0:T(8,128)} %get-tuple-element.129.res, bf16[2,64,1024]{2,1,0:T(8,128)(2,1)} %get-tuple-element.130.layer), custom_call_target="tpu_custom_call" | custom-call | tf_op jit(solution)/shard_map/last/pallas_call | solution.py:136
  535.4 1.7 copy.42
  537.1 1.9 copy.43
  539.0 0.7 copy.44
  (55 shorter events, 0.2 us)
Async XLA Ops:
  5.6 110.6 %copy-start.23 = (s32[2]{0:T(128)S(1)}, s32[2]{0:T(128)}, u32[]{:S(2)}) copy-start(s32[2]{0:T(128)} %param.20) | copy-start | bytes 28
  116.8 7.9 %copy-start.18 = (f32[3,1024]{1,0:T(4,128)S(1)}, f32[3,1024]{1,0:T(4,128)}, u32[]{:S(2)}) copy-start(f32[3,1024]{1,0:T(4,128)} %param.34) | copy-start | bytes 36868
  116.8 7.9 %copy-start.19 = (f32[3,1024]{1,0:T(4,128)S(1)}, f32[3,1024]{1,0:T(4,128)}, u32[]{:S(2)}) copy-start(f32[3,1024]{1,0:T(4,128)} %param.33) | copy-start | bytes 36868
  116.8 29.0 %copy-start.22 = (s32[2,48]{1,0:T(2,128)S(1)}, s32[2,48]{1,0:T(2,128)}, u32[]{:S(2)}) copy-start(s32[2,48]{1,0:T(2,128)} %param.22) | copy-start | bytes 1156
  116.8 40.3 %copy-start.24 = (s32[2]{0:T(128)S(1)}, s32[2]{0:T(128)}, u32[]{:S(2)}) copy-start(s32[2]{0:T(128)} %param.21) | copy-start | bytes 28
  253.0 19.9 %copy-start.20 = (f32[2,1024]{1,0:T(2,128)S(1)}, f32[2,1024]{1,0:T(2,128)}, u32[]{:S(2)}) copy-start(f32[2,1024]{1,0:T(2,128)} %get-tuple-element.142) | copy-start | bytes 24580
  253.0 19.9 %copy-start.21 = (f32[2,1024]{1,0:T(2,128)S(1)}, f32[2,1024]{1,0:T(2,128)}, u32[]{:S(2)}) copy-start(f32[2,1024]{1,0:T(2,128)} %get-tuple-element.141) | copy-start | bytes 24580
  380.4 3.0 copy-start.2
  384.9 2.7 copy-start.3
  384.9 3.8 copy-start.8
  387.6 1.9 copy-start.7
  387.6 2.6 copy-start.14
  389.5 50.7 %copy-start.1 = (bf16[2,128,1024]{2,1,0:T(8,128)(2,1)S(1)}, bf16[2,128,1024]{2,1,0:T(8,128)(2,1)}, u32[]{:S(2)}) copy-start(bf16[2,128,1024]{2,1,0:T(8,128)(2,1)} %reduce_sum.137.s_fout) | copy-start | bytes 1572868
  390.3 51.8 %copy-start = (bf16[2,256,512]{2,1,0:T(8,128)(2,1)S(1)}, bf16[2,256,512]{2,1,0:T(8,128)(2,1)}, u32[]{:S(2)}) copy-start(bf16[2,256,512]{2,1,0:T(8,128)(2,1)} %reduce_sum.136.s_fin) | copy-start | bytes 1572868
  440.2 3.6 copy-start.11
  440.2 4.4 copy-start.10
  442.0 3.3 copy-start.17
  442.0 4.0 copy-start.16
  498.0 1.6 copy-start.6
  499.7 1.8 copy-start.5
  501.5 1.6 copy-start.4
  503.2 1.7 copy-start.13
  503.2 2.5 copy-start.12
  504.8 1.7 copy-start.15
  535.4 3.6 copy-start.9

commit v2 on v1

v2 whole, which is shorter than its diff:
```python
import functools

import jax
import jax.numpy as jnp
from jax import lax
from jax.experimental import pallas as pl
from jax.experimental.pallas import tpu as pltpu
from jax.sharding import PartitionSpec as P

HEAD_DIM = 64
EPS = 1e-05
NEG = -1e30
SCALE = HEAD_DIM ** (-0.5)
BF = jnp.bfloat16
F32 = jnp.float32
VMEM_BYTES = 61 * 1024 * 1024
MESH = pl.DeviceIdType.MESH
VM = pl.BlockSpec(memory_space=pltpu.VMEM)
HBM = pl.BlockSpec(memory_space=pl.ANY)
SM = pl.BlockSpec(memory_space=pltpu.SMEM)


def nn(left, right):
    return lax.dot_general(left, right, (((1,), (0,)), ((), ())), preferred_element_type=F32)


def nt(left, right):
    return lax.dot_general(left, right, (((1,), (1,)), ((), ())), preferred_element_type=F32)


def tn(left, right):
    return lax.dot_general(left, right, (((0,), (0,)), ((), ())), preferred_element_type=F32)


class Link:
    def __init__(self, send_sems, recv_sems):
        self.send_sems, self.recv_sems, self.count, self.open = send_sems, recv_sems, 0, []

    def make(self, src, dst, device):
        index = self.count
        self.count += 1
        return pltpu.make_async_remote_copy(
            src_ref=src,
            dst_ref=dst,
            send_sem=self.send_sems.at[index],
            recv_sem=self.recv_sems.at[index],
            device_id=device,
            device_id_type=MESH,
        )

    def send(self, src, dst, device):
        copy = self.make(src, dst, device)
        copy.start()
        self.open.append(copy)
        return copy

    def local(self, src, dst):
        index = self.count
        self.count += 1
        copy = pltpu.make_async_copy(src, dst, self.send_sems.at[index])
        copy.start()
        return copy

    def finish(self):
        for copy in self.open:
            copy.wait_send()


def greet(devices):
    barrier = pltpu.get_barrier_semaphore()
    for device in devices:
        pl.semaphore_signal(barrier, inc=1, device_id=device, device_id_type=MESH)
    pl.semaphore_wait(barrier, len(devices))


class Place:
    def __init__(self, dims):
        self.dims = dims
        group, share = dims["group"], dims["share"]
        self.me = lax.axis_index("seq")
        self.h = self.me // group
        self.q = self.me % group
        self.b0 = self.q % 2
        self.b1 = (self.q // 2) % 2
        self.c = self.q // 4
        self.it = lax.axis_index("items")
        self.base = (self.it // share) * share
        self.t = self.it % share

    def across(self, bit):
        value = (self.q // (1 << bit)) % 2
        return {"seq": self.me + (1 - 2 * value) * (1 << bit)}

    def partner(self):
        return {"seq": (1 - self.h) * self.dims["group"] + self.q}

    def seq_shift(self, d):
        return lax.rem(self.me + d, self.dims["seq"])

    def share_shift(self, e):
        return lax.rem(self.t + e, self.dims["share"])

    def seq_peers(self):
        return [{"seq": self.seq_shift(d)} for d in range(1, self.dims["seq"])]

    def items_peers(self):
        count = self.dims["items"]
        return [{"items": lax.rem(self.it + e, count)} for e in range(1, count)]


def spread_start(link, place, out, k):
    bits = place.dims["bits"]
    c, b1, b0 = place.c, place.b1, place.b0
    if bits == 3:
        step = link.send(out.at[k, c, b1, b0], out.at[k, c, b1, b0], place.across(2))
        step.wait_recv()
    waits = []
    high = link.send(out.at[k, :, b1, b0], out.at[k, :, b1, b0], place.across(1))
    waits.append(link.send(out.at[k, :, b1, b0], out.at[k, :, b1, b0], place.across(0)))
    return high, waits


def spread_end(link, place, out, k, started):
    high, waits = started
    b1, b0 = place.b1, place.b0
    high.wait_recv()
    waits.append(link.send(out.at[k, :, 1 - b1, b0], out.at[k, :, 1 - b1, b0], place.across(0)))
    return waits


def columns_out(link, place, src, dst, width):
    seq, group = place.dims["seq"], place.dims["group"]
    steps = []
    for d in range(1, seq):
        target = place.seq_shift(d)
        cols = pl.ds(pl.multiple_of(lax.rem(target, group) * width, width), width)
        steps.append(link.send(src.at[:, cols], dst.at[place.me, place.t], {"seq": target}))
    cols = pl.ds(pl.multiple_of(place.q * width, width), width)
    return steps, link.local(src.at[:, cols], dst.at[place.me, place.t])


def rows_out(link, place, src, dst):
    dims, me = place.dims, place.me
    slot = lax.rem(me, dims["items_dev"])
    base = link.count
    link.count += dims["items_dev"] + 1
    copies = []
    for half in range(dims["items_dev"]):
        target = half * dims["group"] + me // dims["items_dev"]
        copy = pltpu.make_async_remote_copy(
            src_ref=src,
            dst_ref=dst.at[slot, place.t],
            send_sem=link.send_sems.at[base + half],
            recv_sem=link.recv_sems.at[base + slot],
            device_id={"seq": target},
            device_id_type=MESH,
        )
        copies.append((target != me, copy))
        pl.when(target != me)(copy.start)
    own = pltpu.make_async_copy(
        src, dst.at[slot, place.t], link.send_sems.at[base + dims["items_dev"]]
    )
    mine = me // dims["items_dev"] == place.q
    pl.when(mine)(own.start)

    def arrived():
        pl.when(mine)(own.wait)
        for block in range(dims["items_dev"]):
            copy = pltpu.make_async_remote_copy(
                src_ref=src,
                dst_ref=dst.at[block, place.t],
                send_sem=link.send_sems.at[base],
                recv_sem=link.recv_sems.at[base + block],
                device_id={"seq": me},
                device_id_type=MESH,
            )
            pl.when(place.q * dims["items_dev"] + block != me)(copy.wait_recv)

    def sent():
        for other, copy in copies:
            pl.when(other)(copy.wait_send)

    return arrived, sent


def to_share(link, place, src, dst):
    steps = []
    for e in range(1, place.dims["share"]):
        other = place.share_shift(e)
        steps.append(link.send(src(other), dst, {"items": place.base + other}))
    return steps


def arrive(steps):
    for step in steps:
        step.wait_recv()


class Reduce:
    def __init__(self, link, place, part, bufs):
        self.link, self.place, self.part, self.bufs = link, place, part, bufs
        self.zero, self.one = {}, {}

    def start(self, index, k):
        place = self.place
        self.zero[index] = self.link.send(
            self.part.at[k, :, :, 1 - place.b0], self.bufs[0].at[index], place.across(0)
        )

    def middle(self, index, k):
        place, part = self.place, self.part
        recv0, send1, recv1, keep1 = self.bufs[:4]
        self.zero[index].wait_recv()
        b1, b0 = place.b1, place.b0
        for c in range(part.shape[1]):
            value = part[k, c, 1 - b1, b0].astype(F32) + recv0[index, c, 1 - b1].astype(F32)
            send1[index, c] = value.astype(BF)
        self.one[index] = self.link.send(send1.at[index], recv1.at[index], place.across(1))
        for c in range(part.shape[1]):
            keep1[index, c] = part[k, c, b1, b0].astype(F32) + recv0[index, c, b1].astype(F32)

    def end(self, index):
        place = self.place
        recv1, keep1 = self.bufs[2:4]
        self.one[index].wait_recv()
        if place.dims["bits"] == 2:
            return keep1[index, 0] + recv1[index, 0].astype(F32)
        send2, recv2 = self.bufs[4:6]
        c = place.c
        send2[index] = (keep1[index, 1 - c] + recv1[index, 1 - c].astype(F32)).astype(BF)
        step = self.link.send(send2.at[index], recv2.at[index], place.across(2))
        kept = keep1[index, c] + recv1[index, c].astype(F32)
        step.wait_recv()
        return kept + recv2[index].astype(F32)


def reduce_bufs(dims, rows):
    items_dev, width, chips = dims["items_dev"], dims["model"], dims["chips"]
    bufs = [
        pltpu.VMEM((items_dev, chips, 2, rows, width), BF),
        pltpu.VMEM((items_dev, chips, rows, width), BF),
        pltpu.VMEM((items_dev, chips, rows, width), BF),
        pltpu.VMEM((items_dev, chips, rows, width), F32),
    ]
    if dims["bits"] == 3:
        bufs += [pltpu.VMEM((items_dev, rows, width), BF) for _ in range(2)]
    return bufs


def moments(value):
    mean = jnp.mean(value, axis=-1, keepdims=True)
    centered = value - mean
    inv = lax.rsqrt(jnp.mean(centered * centered, axis=-1, keepdims=True) + EPS)
    return centered * inv, inv


def norm_back(normed, inv, gain, grad):
    scaled = grad * gain
    mean = jnp.mean(scaled, axis=-1, keepdims=True)
    cross = jnp.mean(scaled * normed, axis=-1, keepdims=True)
    return inv * (scaled - mean - normed * cross)


def rows_back(link, place, src, dst):
    dims, me, h = place.dims, place.me, place.h
    count = dims["items_dev"]
    base = link.count
    link.count += count + 1
    copies = []
    for k in range(count):
        target = place.q * count + k
        copy = pltpu.make_async_remote_copy(
            src_ref=src.at[k],
            dst_ref=dst.at[h],
            send_sem=link.send_sems.at[base + k],
            recv_sem=link.recv_sems.at[base + h],
            device_id={"seq": target},
            device_id_type=MESH,
        )
        copies.append((target != me, copy))
        pl.when(target != me)(copy.start)
    own = pltpu.make_async_copy(
        src.at[lax.rem(me, count)], dst.at[h], link.send_sems.at[base + count]
    )
    mine = me // count == place.q
    pl.when(mine)(own.start)

    def done():
        pl.when(mine)(own.wait)
        for half in range(count):
            copy = pltpu.make_async_remote_copy(
                src_ref=src.at[0],
                dst_ref=dst.at[half],
                send_sem=link.send_sems.at[base],
                recv_sem=link.recv_sems.at[base + half],
                device_id={"seq": me},
                device_id_type=MESH,
            )
            pl.when(half * dims["group"] + me // count != me)(copy.wait_recv)
        for other, copy in copies:
            pl.when(other)(copy.wait_send)

    return done


def half_mask(rows, half):
    return (lax.broadcasted_iota(jnp.int32, (rows, 128), 1) // HEAD_DIM) == half


def attend(q_ref, k_ref, v_ref, valid, p_ref, mix_ref, causal, block, first, last):
    keys = k_ref.shape[0]
    for pair in range(q_ref.shape[1] // 128):
        lanes = slice(pair * 128, pair * 128 + 128)
        for start in range(first, last, block):
            stop = start + block if causal else keys
            halves = []
            for half in range(2):
                query = q_ref[start : start + block, lanes]
                query = jnp.where(half_mask(block, half), query, jnp.zeros_like(query))
                scores = nt(k_ref[:stop, lanes], query) * SCALE
                scores = jnp.where(valid(start, stop), scores, NEG)
                top = jnp.max(scores, axis=0, keepdims=True)
                grown = jnp.exp(scores - top)
                probs = (grown * (1.0 / jnp.sum(grown, axis=0, keepdims=True))).astype(BF)
                p_ref[2 * pair + half, :stop, start : start + block] = probs
                mixed = tn(v_ref[:stop, lanes], probs)
                halves.append(mixed[half * HEAD_DIM : (half + 1) * HEAD_DIM])
            mix_ref[start : start + block, lanes] = jnp.concatenate(halves, axis=0).T.astype(BF)


def attend_back(
    q_ref, k_ref, v_ref, p_ref, grad_ref, dq_ref, dk_ref, dv_ref, causal, block, first, last
):
    keys = k_ref.shape[0]
    for pair in range(q_ref.shape[1] // 128):
        lanes = slice(pair * 128, pair * 128 + 128)
        for start in range(first, last, block):
            stop = start + block if causal else keys
            halves = []
            sum_k, sum_v = None, None
            for half in range(2):
                mask = half_mask(block, half)
                query = q_ref[start : start + block, lanes]
                query = jnp.where(mask, query, jnp.zeros_like(query))
                grad = grad_ref[start : start + block, lanes]
                grad = jnp.where(mask, grad, jnp.zeros_like(grad))
                low = p_ref[2 * pair + half, :stop, start : start + block]
                probs = low.astype(F32)
                grad_probs = nt(v_ref[:stop, lanes], grad)
                delta = jnp.sum(probs * grad_probs, axis=0, keepdims=True)
                grad_scores = (probs * (grad_probs - delta)).astype(BF)
                turned = tn(k_ref[:stop, lanes], grad_scores) * SCALE
                halves.append(turned[half * HEAD_DIM : (half + 1) * HEAD_DIM])
                new_k, new_v = nn(grad_scores, query), nn(low, grad)
                sum_k = new_k if sum_k is None else sum_k + new_k
                sum_v = new_v if sum_v is None else sum_v + new_v
            old = start if causal else (keys if start else 0)
            for ref, value in ((dk_ref, sum_k), (dv_ref, sum_v)):
                if old:
                    ref[:old, lanes] = ref[:old, lanes] + value[:old]
                if old < stop:
                    ref[old:stop, lanes] = value[old:]
            dq_ref[start : start + block, lanes] = jnp.concatenate(halves, axis=0).T.astype(BF)


class Box:
    def __init__(self, names, refs):
        for name, ref in zip(names, refs):
            setattr(self, name, ref)


class Quarters:
    def __init__(self, link, place, grad, box_names, box):
        self.link, self.place, self.grad = link, place, grad
        self.recv, self.lines, self.total, self.moved, self.done, self.out = (
            getattr(box, name) if name else None for name in box_names
        )

    def send(self):
        place = self.place
        self.steps = []
        for e in range(1, place.dims["share"]):
            other = place.share_shift(e)
            self.steps.append(
                self.link.send(
                    self.pick(other), self.recv.at[e - 1], {"items": place.base + other}
                )
            )

    def add(self):
        place = self.place
        arrive(self.steps)
        value = self.mine().astype(F32)
        for e in range(1, place.dims["share"]):
            value = value + self.recv[e - 1].astype(F32)
        self.total[...] = value.astype(BF)
        if self.lines is not None:
            share, items = place.dims["share"], place.dims["items"]
            steps = []
            for a in range(1, items // share):
                target = {"items": lax.rem(place.it + a * share, items)}
                steps.append(self.link.send(self.total, self.lines.at[a - 1], target))
            arrive(steps)
            for step in steps:
                step.wait_send()
            del self.link.open[-len(steps) :]
            for a in range(1, items // share):
                value = value + self.lines[a - 1].astype(F32)
            self.total[...] = value.astype(BF)
        self.along()

    def gather(self):
        self.close()
        place = self.place
        self.steps = to_share(self.link, place, lambda p: self.done, self.out.at[place.t])
        self.own = self.link.local(self.done, self.out.at[place.t])

    def finish(self):
        arrive(self.steps)
        self.own.wait()


class Hidden(Quarters):
    def pick(self, other):
        return self.grad.at[:, other]

    def mine(self):
        return self.grad[:, self.place.t]

    def along(self):
        self.steps = [self.link.send(self.total.at[1], self.moved, self.place.partner())]

    def close(self):
        arrive(self.steps)
        self.done[...] = (self.total[0].astype(F32) + self.moved[...].astype(F32)).astype(BF)


class Columns(Quarters):
    def pick(self, other):
        return self.grad.at[:, :, other]

    def mine(self):
        return self.grad[:, :, self.place.t]

    def along(self):
        place = self.place
        self.steps = []
        for d in range(1, place.dims["seq"]):
            target = place.seq_shift(d)
            self.steps.append(
                self.link.send(
                    self.total.at[:, target], self.moved.at[place.me], {"seq": target}
                )
            )
        self.own = self.link.local(self.total.at[:, place.me], self.moved.at[place.me])

    def close(self):
        arrive(self.steps)
        self.own.wait()
        dims = self.place.dims
        group, width = dims["group"], dims["width"]
        for index in range(3):
            for q in range(group):
                value = self.moved[q, index].astype(F32)
                for half in range(1, dims["items_dev"]):
                    value = value + self.moved[half * group + q, index].astype(F32)
                self.done[index, :, q * width : (q + 1) * width] = value.astype(BF)


class Rows(Quarters):
    pick, mine = Hidden.pick, Hidden.mine

    def along(self):
        self.moved_done = rows_back(self.link, self.place, self.total, self.moved)

    def close(self):
        self.moved_done()
        value = self.moved[0].astype(F32)
        for half in range(1, self.place.dims["items_dev"]):
            value = value + self.moved[half].astype(F32)
        self.done[...] = value.astype(BF)


class Stage:
    def __init__(self, link, place, part, bufs, mid, spread):
        self.link, self.place, self.mid, self.spread = link, place, mid, spread
        self.reduce = Reduce(link, place, part, bufs)
        self.started, self.waits = {}, {}

    def start(self, k):
        self.reduce.start(k, k)

    def middle(self, k):
        self.reduce.middle(k, k)

    def end(self, k):
        place, spread = self.place, self.spread
        spread[k, place.c, place.b1, place.b0] = self.mid(k, self.reduce.end(k))
        self.started[k] = spread_start(self.link, place, spread, k)

    def forward(self, k):
        self.waits[k] = spread_end(self.link, self.place, self.spread, k, self.started[k])

    def arrive(self, k):
        arrive(self.waits[k])


def stage_steps(stage, compute, flight=None, ended=None):
    compute(0)
    stage.start(0)
    compute(1)
    stage.start(1)
    stage.middle(0)
    stage.middle(1)
    if flight:
        flight()
    stage.end(0)
    stage.end(1)
    if ended:
        ended()
    stage.forward(0)
    stage.forward(1)


def layer_kernel(dims, names, *refs):
    b = Box(names, refs)
    b.grad_third, b.grad_r2, b.grad_r1, b.gc1_all = b.first, b.second, b.first, b.gy_all
    place = Place(dims)
    link = Link(b.send_sems, b.recv_sems)
    width, block, items_dev = dims["width"], dims["block"], dims["items_dev"]
    h, t, q_place = place.h, place.t, place.q
    c, b1, b0 = place.c, place.b1, place.b0
    partner = place.partner()
    wr = b.w_sq.shape[0] // dims["share"]
    model = dims["model"]
    total_dec, total_mem = dims["total_dec"], dims["total_mem"]
    rb = b.dec.shape[1]

    def rows_of(ref, cols=model):
        return ref[...].reshape(-1, ref.shape[-1])[:, :cols]

    def chunk(ref, k):
        return ref[k].reshape(-1, model)

    half_rows = total_dec // 2

    def span(k):
        return slice(k * half_rows, (k + 1) * half_rows)

    def put(k, value):
        b.part[k] = value.astype(BF).reshape(b.part.shape[1:])

    def weight(ref, index):
        return ref[index].reshape(model, width)

    weights = (b.w_sq, b.w_sk, b.w_sv, b.w_so, b.w_ck, b.w_cv, b.w_cq, b.w_co)
    rows_t = pl.ds(pl.multiple_of(t * wr, wr), wr)
    staged = [link.local(w.at[rows_t], b.staged.at[i]) for i, w in enumerate(weights)]
    own_fin = link.local(b.f_in, b.own_fin)
    own_fout = link.local(b.f_out, b.own_fout)
    greet(place.seq_peers() + place.items_peers())

    swap_x = link.send(b.dec.at[1 - h], b.x_all.at[h, c, b1, b0], partner)
    b.x_all[h, c, b1, b0] = b.dec[h]
    first_x = spread_start(link, place, b.x_all, h)
    for copy in staged:
        copy.wait()
    self_steps = [columns_out(link, place, b.staged.at[i], b.o_self.at[i], width) for i in range(3)]
    waits = spread_end(link, place, b.x_all, h, first_x)
    swap_x.wait_recv()
    second_x = spread_start(link, place, b.x_all, 1 - h)
    so_arrived, so_sent = rows_out(link, place, b.staged.at[3], b.o_so)

    def share_columns(steps, dst):
        arrive(steps[0])
        steps[1].wait()
        return to_share(link, place, lambda _: dst.at[:, t], dst.at[:, t])

    self_share = [share_columns(self_steps[i], b.o_self.at[i]) for i in range(3)]
    waits += spread_end(link, place, b.x_all, 1 - h, second_x)
    so_arrived()
    so_share = to_share(link, place, lambda _: b.o_so.at[:, t], b.o_so.at[:, t])

    b.m_all[h, c, b1, b0] = b.mem[h]
    swap_m = link.send(b.mem.at[1 - h], b.m_all.at[h, c, b1, b0], partner)
    first_m = spread_start(link, place, b.m_all, h)
    cross_steps = [
        columns_out(link, place, b.staged.at[4 + i], b.o_cross.at[i], width) for i in range(3)
    ]
    co_arrived, co_sent = rows_out(link, place, b.staged.at[7], b.o_co)
    b.c_own[h] = b.cot[h]
    swap_c = link.send(b.cot.at[1 - h], b.c_own.at[h], partner)
    own_fin.wait()
    own_fout.wait()
    fr, gr = b.o_fin.shape[1], b.o_fout.shape[1]
    step_fin = link.send(b.own_fin.at[pl.ds(pl.multiple_of(t * fr, fr), fr)], b.o_fin.at[t], partner)
    step_fout = link.send(
        b.own_fout.at[pl.ds(pl.multiple_of(t * gr, gr), gr)], b.o_fout.at[t], partner
    )
    mem_waits = spread_end(link, place, b.m_all, h, first_m)
    swap_m.wait_recv()
    second_m = spread_start(link, place, b.m_all, 1 - h)
    mem_waits += spread_end(link, place, b.m_all, 1 - h, second_m)

    arrive(waits)
    rows = rows_of(b.x_all)
    for index, dst in enumerate((b.sq, b.sk, b.sv)):
        arrive(self_share[index])
        dst[...] = nn(rows, weight(b.o_self, index)).astype(BF)
    cross_share = [share_columns(cross_steps[i], b.o_cross.at[i]) for i in range(3)]
    co_arrived()
    co_share = to_share(link, place, lambda _: b.o_co.at[:, t], b.o_co.at[:, t])
    length, mem_length = b.dec_len[h], b.mem_len[h]

    def self_ok(start, stop):
        keys = lax.broadcasted_iota(jnp.int32, (stop, block), 0)
        spots = lax.broadcasted_iota(jnp.int32, (stop, block), 1) + start
        return (keys <= spots) & (keys < length)

    bufs = [b.recv0, b.send1, b.recv1, b.keep1]
    if dims["bits"] == 3:
        bufs += [b.send2, b.recv2]

    def forward(index, res, summed, out):
        def mid(k, total):
            value = res(k) + total
            summed[k] = value
            normed, _ = moments(value)
            result = normed * b.gain[index : index + 1] + b.bias[index : index + 1]
            out[k] = result
            return result.astype(BF)

        return mid

    def sent(kept=()):
        late = {id(copy) for copy in kept}
        for copy in link.open:
            if id(copy) not in late:
                copy.wait_send()
        link.open[:] = [copy for copy in link.open if id(copy) in late]

    def self_part(k):
        attend(
            b.sq, b.sk, b.sv, self_ok, b.sp, b.smix, True, block,
            k * half_rows, (k + 1) * half_rows,
        )
        if k == 0:
            arrive(so_share)
        put(k, nn(b.smix[span(k)], rows_of(b.o_so)))

    def memory_part():
        arrive(mem_waits)
        mems = rows_of(b.m_all)
        arrive(cross_share[0])
        b.ck[...] = nn(mems, weight(b.o_cross, 0)).astype(BF)
        arrive(cross_share[1])
        b.cv[...] = nn(mems, weight(b.o_cross, 1)).astype(BF)
        spots = lax.broadcasted_iota(jnp.int32, (total_mem, 128), 0)
        cells = b.m_all[...].reshape(-1, b.m_all.shape[-1])[:, model:].astype(F32)
        b.keep[...] = ((spots < mem_length) & ((cells > 0.5) | (spots == 0))).astype(F32)

    stage = Stage(
        link, place, b.part, bufs,
        forward(0, lambda k: b.x_all[k, c, b1, b0].astype(F32), b.sum_one, b.first), b.first_all,
    )
    stage_steps(stage, self_part)
    step_fin.wait_recv()
    step_fout.wait_recv()
    ffn_share = to_share(link, place, lambda _: b.o_fin.at[t], b.o_fin.at[t])
    ffn_share += to_share(link, place, lambda _: b.o_fout.at[t], b.o_fout.at[t])
    memory_part()

    def cross_part(k):
        last.arrive(k)
        if k == 0:
            sent(ffn_share)
            arrive(cross_share[2])
        b.cq[span(k)] = nn(chunk(b.first_all, k), weight(b.o_cross, 2)).astype(BF)
        attend(
            b.cq, b.ck, b.cv, lambda start, stop: b.keep[:, 0:1] > 0.5, b.cp, b.cmix, False, block,
            k * half_rows, (k + 1) * half_rows,
        )
        if k == 0:
            arrive(co_share)
        put(k, nn(b.cmix[span(k)], rows_of(b.o_co)))

    last = stage
    stage = Stage(
        link, place, b.part, bufs, forward(1, lambda k: b.first[k], b.sum_two, b.second),
        b.second_all,
    )
    stage_steps(stage, cross_part)

    w_ins = (lambda: b.own_fin[...], lambda: b.o_fin[...].reshape(model, -1))
    w_outs = (lambda: b.own_fout[...], lambda: b.o_fout[...].reshape(-1, model))
    hidden = b.own_fin.shape[1]
    last_second = stage

    def ffn_part(k):
        last_second.arrive(k)
        if k == 0:
            sent()
            arrive(ffn_share)
        rows = chunk(b.second_all, k)
        for index in range(2):
            pre = nn(rows, w_ins[index]())
            cdf = 0.5 * (1.0 + lax.erf(pre * (0.5**0.5)))
            cols = slice(index * hidden, (index + 1) * hidden)
            b.act[span(k), cols] = (pre * cdf).astype(BF)
            b.slope[span(k), cols] = (
                cdf + pre * (jnp.exp(-0.5 * pre * pre) * 0.3989422804014327)
            ).astype(BF)
        put(k, nn(b.act[span(k), :hidden], w_outs[0]()) + nn(b.act[span(k), hidden:], w_outs[1]()))

    swap_c.wait_recv()

    def add_sums(index, k, normed, grad):
        new = (jnp.sum(grad * normed, axis=0, keepdims=True), jnp.sum(grad, axis=0, keepdims=True))
        for row, value in zip((index, 3 + index), new):
            b.sums[row : row + 1] = value if k == 0 else b.sums[row : row + 1] + value

    def turn(k, total):
        gain = b.gain[2:3]
        normed, inv = moments(b.second[k] + total)
        spots = lax.broadcasted_iota(jnp.int32, (rb, model), 0) + (k * dims["group"] + q_place) * rb
        kept = spots < length
        b.layer[k] = jnp.where(kept, normed * gain + b.bias[2:3], 0.0).astype(BF)
        grad = jnp.where(kept, b.c_own[k].astype(F32), 0.0)
        add_sums(2, k, normed, grad)
        result = norm_back(normed, inv, gain, grad)
        b.grad_third[k] = result
        return result.astype(BF)

    stage = Stage(link, place, b.part, bufs, turn, b.gy_all)
    stage_steps(stage, ffn_part)

    last_turn = stage

    def ffn_back(k):
        last_turn.arrive(k)
        if k == 0:
            sent()
        grad = chunk(b.gy_all, k)
        total = None
        for index in range(2):
            cols = slice(index * hidden, (index + 1) * hidden)
            grad_pre = (nt(grad, w_outs[index]()) * b.slope[span(k), cols].astype(F32)).astype(BF)
            b.slope[span(k), cols] = grad_pre
            term = nt(grad_pre, w_ins[index]())
            total = term if total is None else total + term
        put(k, total)

    way_fout = Hidden(
        link, place, b.g_fout, ("q_fout", dims["lines"] and "l_fout", "s_fout", "z_fout", "d_fout", "r_fout"), b
    )
    way_fin = Hidden(
        link, place, b.g_fin, ("q_fin", dims["lines"] and "l_fin", "s_fin", "z_fin", "d_fin", "r_fin"), b
    )
    way_cross = Columns(
        link, place, b.g_cross, ("q_cross", dims["lines"] and "l_cross", "s_cross", "z_cross", "d_cross", "r_cross"), b
    )
    way_self = Columns(
        link, place, b.g_self, ("q_self", dims["lines"] and "l_self", "s_self", "z_self", "d_self", "r_self"), b
    )
    way_co = Rows(
        link, place, b.g_co, ("q_co", dims["lines"] and "l_co", "s_co", "z_co", "d_co", "r_co"), b
    )
    way_so = Rows(
        link, place, b.g_so, ("q_so", dims["lines"] and "l_so", "s_so", "z_so", "d_so", "r_so"), b
    )

    def backward(index, res, summed, out):
        def mid(k, total):
            normed, inv = moments(summed[k])
            grad = res[k] + total
            add_sums(index, k, normed, grad)
            result = norm_back(normed, inv, b.gain[index : index + 1], grad)
            out[k] = result
            return result.astype(BF)

        return mid

    def out_grads():
        grad = rows_of(b.gy_all)
        for index in range(2):
            cols = slice(index * hidden, (index + 1) * hidden)
            value = tn(b.act[:, cols], grad)
            b.g_fout[index] = value.astype(BF).reshape(b.g_fout.shape[1:])
        way_fout.send()

    def in_grads():
        rows = rows_of(b.second_all)
        for index in range(2):
            cols = slice(index * hidden, (index + 1) * hidden)
            value = tn(rows, b.slope[:, cols])
            b.g_fin[index] = value.astype(BF).reshape(b.g_fin.shape[1:])
        way_fin.send()

    stage = Stage(
        link, place, b.part, bufs, backward(1, b.grad_third, b.sum_two, b.grad_r2), b.gc2_all
    )
    stage_steps(stage, ffn_back, out_grads, in_grads)

    last_back = stage
    flying = way_fout.steps + way_fin.steps

    def cross_back(k):
        last_back.arrive(k)
        if k == 0:
            sent(flying)
        b.dmix[span(k)] = nt(chunk(b.gc2_all, k), rows_of(b.o_co)).astype(BF)
        attend_back(
            b.cq, b.ck, b.cv, b.cp, b.dmix, b.dq, b.sum_dk, b.sum_dv, False, block,
            k * half_rows, (k + 1) * half_rows,
        )
        put(k, nt(b.dq[span(k)], weight(b.o_cross, 2)))

    def cross_grads():
        mems = rows_of(b.m_all)
        shape = b.g_cross.shape[1:]
        b.dck[...] = (b.sum_dk[:total_mem] * SCALE).astype(BF)
        b.dcv[...] = b.sum_dv[:total_mem].astype(BF)
        b.g_cross[0] = tn(rows_of(b.first_all), b.dq[...]).astype(BF).reshape(shape)
        b.g_cross[1] = tn(mems, b.dck[...]).astype(BF).reshape(shape)
        b.g_cross[2] = tn(mems, b.dcv[...]).astype(BF).reshape(shape)
        way_cross.send()
        b.g_co[...] = tn(b.cmix[...], rows_of(b.gc2_all)).astype(BF).reshape(b.g_co.shape)
        way_co.send()

    def part_mem():
        value = nt(b.dck[...], weight(b.o_cross, 0)) + nt(b.dcv[...], weight(b.o_cross, 1))
        b.part_m[...] = value.astype(BF).reshape(b.part_m.shape)

    stage = Stage(
        link, place, b.part, bufs, backward(0, b.grad_r2, b.sum_one, b.grad_r1), b.gc1_all
    )
    stage_steps(stage, cross_back, cross_grads, part_mem)
    flying += way_cross.steps + way_co.steps

    for k in range(2):
        stage.arrive(k)
        b.dmix[span(k)] = nt(chunk(b.gc1_all, k), rows_of(b.o_so)).astype(BF)
        attend_back(
            b.sq, b.sk, b.sv, b.sp, b.dmix, b.dq, b.sum_dk, b.sum_dv, True, block,
            k * half_rows, (k + 1) * half_rows,
        )
    sent(flying)
    b.dsk[...] = (b.sum_dk[...] * SCALE).astype(BF)
    b.dsv[...] = b.sum_dv[...].astype(BF)
    for k in range(2):
        total = nt(b.dq[span(k)], weight(b.o_self, 0)) + nt(b.dsk[span(k)], weight(b.o_self, 1))
        put(k, total + nt(b.dsv[span(k)], weight(b.o_self, 2)))
    seq_sums = []
    for d in range(1, dims["seq"]):
        seq_sums.append(
            link.send(b.sums, b.sums_seq.at[d - 1], {"seq": place.seq_shift(d)})
        )
    ks = (1 - h, h)
    red_x = Reduce(link, place, b.part, bufs)
    mem_bufs = [b.recv0_m, b.send1_m, b.recv1_m, b.keep1_m]
    if dims["bits"] == 3:
        mem_bufs += [b.send2_m, b.recv2_m]
    red_m = Reduce(link, place, b.part_m, mem_bufs)
    for red in (red_x, red_m):
        for index in range(2):
            red.start(index, ks[index])
    for red in (red_x, red_m):
        for index in range(2):
            red.middle(index, ks[index])
    swap_l = link.send(b.layer.at[1 - h], b.layer_out.at[h], partner)
    b.layer_out[h] = b.layer[h]
    rows = rows_of(b.x_all)
    shape = b.g_self.shape[1:]
    b.g_self[0] = tn(rows, b.dq[...]).astype(BF).reshape(shape)
    b.g_self[1] = tn(rows, b.dsk[...]).astype(BF).reshape(shape)
    b.g_self[2] = tn(rows, b.dsv[...]).astype(BF).reshape(shape)
    way_self.send()
    b.g_so[...] = tn(b.smix[...], rows_of(b.gc1_all)).astype(BF).reshape(b.g_so.shape)
    way_so.send()
    way_fout.add()
    b.send_x[...] = (red_x.end(0) + b.grad_r1[1 - h]).astype(BF)
    swap_x = link.send(b.send_x, b.recv_x, partner)
    b.grad_dec[h] = red_x.end(1) + b.grad_r1[h]
    b.send_m[...] = red_m.end(0).astype(BF)
    swap_m = link.send(b.send_m, b.recv_m, partner)
    b.grad_mem[h] = red_m.end(1)
    arrive(seq_sums)
    value = b.sums[...]
    for d in range(1, dims["seq"]):
        value = value + b.sums_seq[d - 1]
    b.sums_line[...] = value
    item_sums = []
    for e in range(1, dims["items"]):
        target = {"items": lax.rem(place.it + e, dims["items"])}
        item_sums.append(link.send(b.sums_line, b.sums_items.at[e - 1], target))
    way_fin.add()
    swap_x.wait_recv()
    b.grad_dec[1 - h] = b.recv_x[...].astype(F32)
    swap_m.wait_recv()
    b.grad_mem[1 - h] = b.recv_m[...].astype(F32)
    swap_l.wait_recv()
    way_fout.gather()
    way_cross.add()
    way_co.add()
    way_fin.gather()
    way_self.add()
    way_so.add()
    way_cross.gather()
    way_co.gather()
    arrive(item_sums)
    value = b.sums_line[...]
    for e in range(1, dims["items"]):
        value = value + b.sums_items[e - 1]
    b.sums_out[...] = value
    way_self.gather()
    way_so.gather()
    for way in (way_fout, way_fin, way_cross, way_co, way_self, way_so):
        way.finish()
    so_sent()
    co_sent()
    link.finish()


def shape(dims, dtype):
    return jax.ShapeDtypeStruct(tuple(dims), dtype)


def shards(
    mesh, dec_in, memory, dec_len, mem_len, cell_mask, self_query, self_key, self_value, self_out,
    cross_query, cross_key, cross_value, cross_out, ffn_in, ffn_out, norm_gain, norm_bias, cotangent,
):
    items_dev, rb, model = dec_in.shape
    mb = memory.shape[1]
    seq, items = mesh.shape["seq"], mesh.shape["items"]
    group = seq // items_dev
    share = 4
    bits = group.bit_length() - 1
    chips = group // 4
    width = model // group
    total_dec, total_mem = rb * seq, mb * seq
    heads = width // HEAD_DIM
    hidden = ffn_in.shape[1]
    wr = self_query.shape[0] // share
    fr, gr = model // share, hidden // share
    lines = items // share - 1
    dims = {
        "items_dev": items_dev, "items": items, "seq": seq, "group": group, "share": share,
        "bits": bits, "chips": chips, "width": width, "model": model, "block": 256,
        "total_dec": total_dec, "total_mem": total_mem, "lines": lines,
    }
    cells = jnp.broadcast_to((cell_mask == 1).astype(BF)[:, :, None], (items_dev, mb, 128))
    mem_cells = jnp.concatenate([memory, cells], axis=2)

    ins = [
        ("dec", dec_in, VM), ("mem", mem_cells, VM), ("cot", cotangent, VM),
        ("dec_len", dec_len, SM), ("mem_len", mem_len, SM),
        ("w_sq", self_query, HBM), ("w_sk", self_key, HBM), ("w_sv", self_value, HBM),
        ("w_so", self_out, HBM), ("w_cq", cross_query, HBM), ("w_ck", cross_key, HBM),
        ("w_cv", cross_value, HBM), ("w_co", cross_out, HBM), ("f_in", ffn_in, HBM),
        ("f_out", ffn_out, HBM), ("gain", norm_gain, VM), ("bias", norm_bias, VM),
    ]
    own, own_m = (items_dev, rb, model), (items_dev, mb, model)
    grid = (items_dev, chips, 2, 2)
    outs = [
        ("layer_out", own, BF, VM), ("grad_dec", own, F32, VM), ("grad_mem", own_m, F32, VM),
        ("sums_out", (8, model), F32, VM),
        ("r_cross", (share, 3, wr, model), BF, HBM), ("r_self", (share, 3, wr, model), BF, HBM),
        ("r_co", (share, wr, model), BF, HBM), ("r_so", (share, wr, model), BF, HBM),
        ("r_fin", (share, fr, hidden), BF, HBM), ("r_fout", (share, gr, model), BF, HBM),
    ]
    cols = (3, seq, share, wr, width)
    scratch = [
        ("x_all", grid + (rb, model), BF), ("m_all", grid + (mb, model + 128), BF),
        ("c_own", own, BF), ("staged", (8, wr, model), BF),
        ("own_fin", (model, hidden), BF), ("own_fout", (hidden, model), BF),
        ("o_self", cols, BF), ("o_cross", cols, BF),
        ("o_so", (items_dev, share, wr, model), BF), ("o_co", (items_dev, share, wr, model), BF),
        ("o_fin", (share, fr, hidden), BF), ("o_fout", (share, gr, model), BF),
        ("sq", (total_dec, width), BF), ("sk", (total_dec, width), BF), ("sv", (total_dec, width), BF),
        ("cq", (total_dec, width), BF), ("ck", (total_mem, width), BF), ("cv", (total_mem, width), BF),
        ("sp", (heads, total_dec, total_dec), BF), ("cp", (heads, total_mem, total_dec), BF),
        ("smix", (total_dec, width), BF), ("cmix", (total_dec, width), BF),
        ("keep", (total_mem, 128), F32),
        ("part", grid + (rb, model), BF), ("part_m", grid + (mb, model), BF),
        ("first_all", grid + (rb, model), BF), ("second_all", grid + (rb, model), BF),
        ("gy_all", grid + (rb, model), BF), ("gc2_all", grid + (rb, model), BF),
        ("sum_one", own, F32), ("sum_two", own, F32), ("first", own, F32), ("second", own, F32),
        ("layer", own, BF), ("sum_dk", (total_dec, width), F32), ("sum_dv", (total_dec, width), F32),
        ("act", (total_dec, 2 * hidden), BF), ("slope", (total_dec, 2 * hidden), BF),
        ("dmix", (total_dec, width), BF), ("dq", (total_dec, width), BF),
        ("dsk", (total_dec, width), BF), ("dsv", (total_dec, width), BF),
        ("dck", (total_mem, width), BF), ("dcv", (total_mem, width), BF),
        ("send_x", (rb, model), BF), ("recv_x", (rb, model), BF),
        ("send_m", (mb, model), BF), ("recv_m", (mb, model), BF),
        ("sums", (8, model), F32), ("sums_line", (8, model), F32),
        ("sums_seq", (seq - 1, 8, model), F32), ("sums_items", (items - 1, 8, model), F32),
    ]
    for name, rows in (("", rb), ("_m", mb)):
        scratch += [
            ("recv0" + name, (items_dev, chips, 2, rows, model), BF),
            ("send1" + name, (items_dev, chips, rows, model), BF),
            ("recv1" + name, (items_dev, chips, rows, model), BF),
            ("keep1" + name, (items_dev, chips, rows, model), F32),
        ]
        if bits == 3:
            scratch += [
                ("send2" + name, (items_dev, rows, model), BF),
                ("recv2" + name, (items_dev, rows, model), BF),
            ]
    for name, grad, quarter, moved, done in (
        ("fin", (2, share, fr, hidden), (2, fr, hidden), (fr, hidden), (fr, hidden)),
        ("fout", (2, share, gr, model), (2, gr, model), (gr, model), (gr, model)),
        ("cross", cols, (3, seq, wr, width), (seq, 3, wr, width), (3, wr, model)),
        ("self", cols, (3, seq, wr, width), (seq, 3, wr, width), (3, wr, model)),
        ("co", (items_dev, share, wr, model), (items_dev, wr, model), (items_dev, wr, model), (wr, model)),
        ("so", (items_dev, share, wr, model), (items_dev, wr, model), (items_dev, wr, model), (wr, model)),
    ):
        scratch += [
            ("g_" + name, grad, BF), ("q_" + name, (share - 1,) + quarter, BF),
            ("s_" + name, quarter, BF), ("z_" + name, moved, BF), ("d_" + name, done, BF),
        ]
        if lines:
            scratch.append(("l_" + name, (lines,) + quarter, BF))
    copies = 320 + 16 * (seq - 8) + 12 * (bits - 2) + 12 * lines
    names = [x[0] for x in ins + outs + scratch] + ["send_sems", "recv_sems"]
    results = pl.pallas_call(
        functools.partial(layer_kernel, dims, names),
        name="layer",
        out_shape=[shape(x[1], x[2]) for x in outs],
        in_specs=[x[2] for x in ins],
        out_specs=[x[3] for x in outs],
        scratch_shapes=[pltpu.VMEM(x[1], x[2]) for x in scratch]
        + [pltpu.SemaphoreType.DMA((copies,)), pltpu.SemaphoreType.DMA((copies,))],
        compiler_params=pltpu.CompilerParams(
            collective_id=0, has_side_effects=True, vmem_limit_bytes=VMEM_BYTES
        ),
    )(*[x[1] for x in ins])
    layer_out, grad_dec, grad_memory, sums, r_cross, r_self, r_co, r_so, r_fin, r_fout = results
    f_cross = r_cross.transpose(1, 0, 2, 3).reshape(3, share * wr, model).astype(F32)
    f_self = r_self.transpose(1, 0, 2, 3).reshape(3, share * wr, model).astype(F32)
    return (
        layer_out, grad_dec, grad_memory,
        f_self[0], f_self[1], f_self[2], r_so.reshape(share * wr, model).astype(F32),
        f_cross[0], f_cross[1], f_cross[2], r_co.reshape(share * wr, model).astype(F32),
        r_fin.reshape(model, hidden).astype(F32), r_fout.reshape(hidden, model).astype(F32),
        sums[0:3], sums[3:6],
    )


def solution(mesh):
    rows = P("seq", None)
    tokens = P("items", "seq", None)
    placed = (
        (tokens, tokens, P("items"), P("items"), P("items", "seq"))
        + (rows,) * 8
        + (P(None, "seq"), rows, P(), P(), tokens)
    )
    return jax.shard_map(
        functools.partial(shards, mesh),
        mesh=mesh,
        in_specs=placed,
        out_specs=(tokens,) * 3 + (rows,) * 8 + (P(None, "seq"), rows, P(), P()),
        check_vma=False,
    )
```

time: 541 us -> 288 us (0.53)
  Pallas kernels: 480 us -> 273 us
  other arithmetic: 27.5 us -> 8.52 us
  local copies, waits for them, and re-layouts: 20.1 us -> 5.4 us
  blocking collectives: 11.2 us -> 0 us
    pallas_call x16 -> x1, Pallas kernels: 480 us -> 273 us  [shards(): pl.pallas_call(functools.partial(layer_kernel, dims, names), name='layer'...]
    reduce_sum x12 -> x0, other arithmetic: 12 us -> none  [the longest x6 9.87 us: shards(): jnp.sum(value.astype(F32), axis=0).astype(BF)]
    all_gather x1 -> x0, blocking collectives: 11.2 us -> none  [shards(): cells = lax.all_gather(cell_mask.astype(BF), 'seq', axis=1, tiled=True)]
    convert_element_type x10 -> x5, other arithmetic: 12 us -> 6.88 us  [the longest x1 1.78 us: shards(): r_cross.transpose(1, 0, 2, 3).reshape(3, share * wr, model).astype(F32)]
where the time goes in v2:
time: 288 us
  Pallas kernels  273 us (95%)
  other arithmetic  8.52 us (3%)
  local copies, waits for them, and re-layouts  5.4 us (2%)
    pallas_call x1, Pallas kernels, shards(): pl.pallas_call(functools.partial(layer_kernel, dims, names), name='layer'...  273 us

profile of v2, /device:TPU:0, one launch (start us, length us, event | category | flops | bytes accessed | tf_op | source)
XLA Modules:
  0.0 287.7 jit_solution(5865220862946854871)
XLA Ops:
  0.6 0.7 compare_convert_fusion
  1.3 0.1 broadcast_in_dim.2
  1.4 1.6 pad_maximum_fusion.refs_1_
  3.0 273.1 %layer.1 = (bf16[2,64,1024]{2,1,0:T(8,128)(2,1)}, f32[2,64,1024]{2,1,0:T(8,128)}, f32[2,48,1024]{2,1,0:T(8,128)}, f32[8,1024]{1,0:T(8,128)}, bf16[4,3,32,1024]{3...) custom-call(bf16[2,64,1024]{2,1,0:T(8,128)(2,1)} %refs_0_.1, ...), custom_call_target="tpu_custom_call" | custom-call | tf_op jit(solution)/shard_map/layer/pallas_call | solution.py:1026
  276.1 1.8 convert_bitcast_fusion
  277.9 1.2 fusion.1
  279.1 0.0 copy-start.5
  279.1 0.0 copy-start.6
  279.1 1.2 fusion
  280.3 0.0 copy-start.7
  280.3 0.0 copy-start.1
  280.3 0.0 copy-done.5
  280.3 0.1 copy-done.6
  280.3 1.1 bitcast_convert_fusion.2
  281.5 0.0 copy-done.7
  281.5 0.6 fusion.2
  282.1 0.0 copy-done.1
  282.1 0.0 copy-start
  282.1 1.6 bitcast_convert_fusion
  283.7 0.0 copy-done
  283.7 0.0 copy-start.4
  283.7 0.0 copy-start.2
  283.7 1.7 bitcast_convert_fusion.1
  285.4 0.0 copy-start.3
  285.4 0.0 copy-done.4
  285.4 0.7 copy.36
  286.1 0.0 copy-done.2
  286.1 0.8 copy.37
  286.9 0.0 copy-done.3
  286.9 0.7 copy.38
Async XLA Ops:
  279.1 1.2 copy-start.5
  279.1 1.3 copy-start.6
  280.3 1.2 copy-start.7
  280.3 1.8 copy-start.1
  282.1 1.6 copy-start
  283.7 1.7 copy-start.4
  283.7 2.4 copy-start.2
  285.4 1.5 copy-start.3

commit v3 on v2

--- a/solution.py
+++ b/solution.py
@@ -13,7 +13,7 @@
 SCALE = HEAD_DIM ** (-0.5)
 BF = jnp.bfloat16
 F32 = jnp.float32
-VMEM_BYTES = 61 * 1024 * 1024
+VMEM_BYTES = 63 * 1024 * 1024
 MESH = pl.DeviceIdType.MESH
 VM = pl.BlockSpec(memory_space=pltpu.VMEM)
 HBM = pl.BlockSpec(memory_space=pl.ANY)
@@ -33,12 +33,14 @@
 
 
 class Link:
-    def __init__(self, send_sems, recv_sems):
-        self.send_sems, self.recv_sems, self.count, self.open = send_sems, recv_sems, 0, []
-
-    def make(self, src, dst, device):
-        index = self.count
+    def __init__(self, send_sems, recv_sems, first=0):
+        self.send_sems, self.recv_sems, self.count, self.open = send_sems, recv_sems, first, []
+
+    def index(self):
         self.count += 1
+        return self.count - 1
+
+    def make(self, src, dst, device, index):
         return pltpu.make_async_remote_copy(
             src_ref=src,
             dst_ref=dst,
@@ -49,21 +51,30 @@
         )
 
     def send(self, src, dst, device):
-        copy = self.make(src, dst, device)
+        copy = self.make(src, dst, device, self.index())
         copy.start()
         self.open.append(copy)
         return copy
 
+    def batch(self, copies, whole):
+        index = self.index()
+        for copy in copies:
+            self.make(*copy, index).start()
+        wait = self.make(whole, whole, copies[0][2], index)
+        self.open.append(wait)
+        return wait
+
     def local(self, src, dst):
-        index = self.count
-        self.count += 1
-        copy = pltpu.make_async_copy(src, dst, self.send_sems.at[index])
+        copy = pltpu.make_async_copy(src, dst, self.send_sems.at[self.index()])
         copy.start()
         return copy
 
-    def finish(self):
+    def finish(self, kept=()):
+        late = {id(copy) for copy in kept}
         for copy in self.open:
-            copy.wait_send()
+            if id(copy) not in late:
+                copy.wait_send()
+        self.open = [copy for copy in self.open if id(copy) in late]
 
 
 def greet(devices):
@@ -86,6 +97,8 @@
         self.it = lax.axis_index("items")
         self.base = (self.it // share) * share
         self.t = self.it % share
+        x, y = self.t % 2, self.t // 2
+        self.tx, self.ty, self.txy = y * 2 + 1 - x, (1 - y) * 2 + x, (1 - y) * 2 + 1 - x
 
     def across(self, bit):
         value = (self.q // (1 << bit)) % 2
@@ -97,8 +110,8 @@
     def seq_shift(self, d):
         return lax.rem(self.me + d, self.dims["seq"])
 
-    def share_shift(self, e):
-        return lax.rem(self.t + e, self.dims["share"])
+    def line(self, t):
+        return {"items": self.base + t}
 
     def seq_peers(self):
         return [{"seq": self.seq_shift(d)} for d in range(1, self.dims["seq"])]
@@ -130,11 +143,12 @@
 
 def columns_out(link, place, src, dst, width):
     seq, group = place.dims["seq"], place.dims["group"]
-    steps = []
+    copies = []
     for d in range(1, seq):
         target = place.seq_shift(d)
         cols = pl.ds(pl.multiple_of(lax.rem(target, group) * width, width), width)
-        steps.append(link.send(src.at[:, cols], dst.at[place.me, place.t], {"seq": target}))
+        copies.append((src.at[:, cols], dst.at[place.me, place.t], {"seq": target}))
+    steps = [link.batch(copies, dst.at[0 : seq - 1, place.t])]
     cols = pl.ds(pl.multiple_of(place.q * width, width), width)
     return steps, link.local(src.at[:, cols], dst.at[place.me, place.t])
 
@@ -183,12 +197,24 @@
     return arrived, sent
 
 
-def to_share(link, place, src, dst):
-    steps = []
-    for e in range(1, place.dims["share"]):
-        other = place.share_shift(e)
-        steps.append(link.send(src(other), dst, {"items": place.base + other}))
-    return steps
+class Share:
+    def __init__(self, link, place, slab, half):
+        self.link, self.place, self.half = link, place, half
+        t = place.t
+        self.from_x = link.send(slab(t), slab(t), place.line(place.tx))
+        self.from_y = link.send(slab(t), slab(t), place.line(place.ty))
+
+    def forward(self):
+        link, place, half = self.link, self.place, self.half
+        self.from_y.wait_recv()
+        part = half(place.ty, 0)
+        self.steps = [link.send(part, part, place.line(place.tx))]
+        self.from_x.wait_recv()
+        part = half(place.tx, 1)
+        self.steps.append(link.send(part, part, place.line(place.ty)))
+
+    def wait(self):
+        arrive(self.steps)
 
 
 def arrive(steps):
@@ -307,7 +333,7 @@
     return (lax.broadcasted_iota(jnp.int32, (rows, 128), 1) // HEAD_DIM) == half
 
 
-def attend(q_ref, k_ref, v_ref, valid, p_ref, mix_ref, causal, block, first, last):
+def attend(q_ref, k_ref, v_ref, valid, p_ref, mix_ref, causal, block, first, last, pump):
     keys = k_ref.shape[0]
     for pair in range(q_ref.shape[1] // 128):
         lanes = slice(pair * 128, pair * 128 + 128)
@@ -326,10 +352,13 @@
                 mixed = tn(v_ref[:stop, lanes], probs)
                 halves.append(mixed[half * HEAD_DIM : (half + 1) * HEAD_DIM])
             mix_ref[start : start + block, lanes] = jnp.concatenate(halves, axis=0).T.astype(BF)
+        if pair == 0:
+            pump()
 
 
 def attend_back(
-    q_ref, k_ref, v_ref, p_ref, grad_ref, dq_ref, dk_ref, dv_ref, causal, block, first, last
+    q_ref, k_ref, v_ref, p_ref, grad_ref, dq_ref, dk_ref, dv_ref, causal, block, first, last,
+    pump,
 ):
     keys = k_ref.shape[0]
     for pair in range(q_ref.shape[1] // 128):
@@ -361,6 +390,8 @@
                 if old < stop:
                     ref[old:stop, lanes] = value[old:]
             dq_ref[start : start + block, lanes] = jnp.concatenate(halves, axis=0).T.astype(BF)
+        if pair == 0:
+            pump()
 
 
 class Box:
@@ -372,38 +403,49 @@
 class Quarters:
     def __init__(self, link, place, grad, box_names, box):
         self.link, self.place, self.grad = link, place, grad
-        self.recv, self.lines, self.total, self.moved, self.done, self.out = (
+        self.recv, self.sums, self.last, self.lines, self.total, self.moved, self.done, self.out = (
             getattr(box, name) if name else None for name in box_names
         )
 
     def send(self):
-        place = self.place
+        place, piece, link = self.place, self.piece, self.link
         self.steps = []
-        for e in range(1, place.dims["share"]):
-            other = place.share_shift(e)
-            self.steps.append(
-                self.link.send(
-                    self.pick(other), self.recv.at[e - 1], {"items": place.base + other}
-                )
-            )
+        for i, near in enumerate((place.tx, place.ty)):
+            copies = [
+                (self.grad.at[piece(near, i)], self.recv.at[i, 0], place.line(near)),
+                (self.grad.at[piece(place.txy, i)], self.recv.at[i, 1], place.line(near)),
+            ]
+            self.steps.append(link.batch(copies, self.recv.at[i]))
+        self.flying = list(self.steps)
+
+    def turn(self):
+        place, piece, link = self.place, self.piece, self.link
+        steps = []
+        for i, far in enumerate((place.ty, place.tx)):
+            self.steps[i].wait_recv()
+            value = self.grad[piece(far, i)].astype(F32) + self.recv[i, 1].astype(F32)
+            self.sums[i] = value.astype(BF)
+            steps.append(link.send(self.sums.at[i], self.last.at[i], place.line(far)))
+        self.steps = steps
+        self.flying += steps
 
     def add(self):
         place = self.place
-        arrive(self.steps)
-        value = self.mine().astype(F32)
-        for e in range(1, place.dims["share"]):
-            value = value + self.recv[e - 1].astype(F32)
-        self.total[...] = value.astype(BF)
+        for i in range(2):
+            self.steps[i].wait_recv()
+            value = self.grad[self.piece(place.t, i)].astype(F32)
+            value = value + self.recv[i, 0].astype(F32) + self.last[i].astype(F32)
+            self.total[self.halves(i)] = value.astype(BF)
         if self.lines is not None:
             share, items = place.dims["share"], place.dims["items"]
-            steps = []
+            copies = []
             for a in range(1, items // share):
                 target = {"items": lax.rem(place.it + a * share, items)}
-                steps.append(self.link.send(self.total, self.lines.at[a - 1], target))
-            arrive(steps)
-            for step in steps:
-                step.wait_send()
-            del self.link.open[-len(steps) :]
+                copies.append((self.total, self.lines.at[a - 1], target))
+            step = self.link.batch(copies, self.lines)
+            step.wait()
+            self.link.open.pop()
+            value = self.total[...].astype(F32)
             for a in range(1, items // share):
                 value = value + self.lines[a - 1].astype(F32)
             self.total[...] = value.astype(BF)
@@ -411,9 +453,20 @@
 
     def gather(self):
         self.close()
-        place = self.place
-        self.steps = to_share(self.link, place, lambda p: self.done, self.out.at[place.t])
-        self.own = self.link.local(self.done, self.out.at[place.t])
+        place, out = self.place, self.out
+        self.own = self.link.local(self.done, out.at[place.t])
+        self.near = [
+            self.link.send(self.done, out.at[place.t], place.line(near))
+            for near in (place.tx, place.ty)
+        ]
+
+    def forward(self):
+        place, out, link = self.place, self.out, self.link
+        self.steps = []
+        for i, (source, near) in enumerate(((place.ty, place.tx), (place.tx, place.ty))):
+            self.near[1 - i].wait_recv()
+            part = out.at[self.cut(source, i)]
+            self.steps.append(link.send(part, part, place.line(near)))
 
     def finish(self):
         arrive(self.steps)
@@ -421,11 +474,17 @@
 
 
 class Hidden(Quarters):
-    def pick(self, other):
-        return self.grad.at[:, other]
-
-    def mine(self):
-        return self.grad[:, self.place.t]
+    def piece(self, t, i):
+        rows = self.grad.shape[2] // 2
+        return slice(None), t, slice(i * rows, (i + 1) * rows)
+
+    def halves(self, i):
+        rows = self.grad.shape[2] // 2
+        return slice(None), slice(i * rows, (i + 1) * rows)
+
+    def cut(self, t, i):
+        rows = self.out.shape[1] // 2
+        return t, slice(i * rows, (i + 1) * rows)
 
     def along(self):
         self.steps = [self.link.send(self.total.at[1], self.moved, self.place.partner())]
@@ -436,22 +495,25 @@
 
 
 class Columns(Quarters):
-    def pick(self, other):
-        return self.grad.at[:, :, other]
-
-    def mine(self):
-        return self.grad[:, :, self.place.t]
+    def piece(self, t, i):
+        blocks = self.grad.shape[1] // 2
+        return slice(None), slice(i * blocks, (i + 1) * blocks), t
+
+    def halves(self, i):
+        blocks = self.grad.shape[1] // 2
+        return slice(None), slice(i * blocks, (i + 1) * blocks)
+
+    def cut(self, t, i):
+        cols = self.out.shape[3] // 2
+        return t, slice(None), slice(None), slice(i * cols, (i + 1) * cols)
 
     def along(self):
         place = self.place
-        self.steps = []
+        copies = []
         for d in range(1, place.dims["seq"]):
             target = place.seq_shift(d)
-            self.steps.append(
-                self.link.send(
-                    self.total.at[:, target], self.moved.at[place.me], {"seq": target}
-                )
-            )
+            copies.append((self.total.at[:, target], self.moved.at[place.me], {"seq": target}))
+        self.steps = [self.link.batch(copies, self.moved.at[0 : place.dims["seq"] - 1])]
         self.own = self.link.local(self.total.at[:, place.me], self.moved.at[place.me])
 
     def close(self):
@@ -468,7 +530,15 @@
 
 
 class Rows(Quarters):
-    pick, mine = Hidden.pick, Hidden.mine
+    def piece(self, t, i):
+        return i, t
+
+    def halves(self, i):
+        return i
+
+    def cut(self, t, i):
+        cols = self.out.shape[2] // 2
+        return t, slice(None), slice(i * cols, (i + 1) * cols)
 
     def along(self):
         self.moved_done = rows_back(self.link, self.place, self.total, self.moved)
@@ -482,9 +552,10 @@
 
 
 class Stage:
-    def __init__(self, link, place, part, bufs, mid, spread):
-        self.link, self.place, self.mid, self.spread = link, place, mid, spread
-        self.reduce = Reduce(link, place, part, bufs)
+    def __init__(self, sems, place, part, bufs, mid, spread, before):
+        self.link, self.place, self.mid, self.spread = Link(*sems), place, mid, spread
+        self.before = before
+        self.reduce = Reduce(self.link, place, part, bufs)
         self.started, self.waits = {}, {}
 
     def start(self, k):
@@ -504,12 +575,22 @@
     def arrive(self, k):
         arrive(self.waits[k])
 
-
-def stage_steps(stage, compute, flight=None, ended=None):
-    compute(0)
+    def release(self, k):
+        done = (self.reduce.zero[k], self.reduce.one[k])
+        for copy in done:
+            copy.wait_send()
+        late = {id(copy) for copy in done}
+        self.link.open = [copy for copy in self.link.open if id(copy) not in late]
+
+
+def stage_steps(stage, compute, flight=None, ended=None, after=None):
+    before = stage.before
+    compute(0, (lambda: before.forward(1)) if before else (lambda: None))
     stage.start(0)
-    compute(1)
+    compute(1, lambda: None)
     stage.start(1)
+    if before:
+        before.link.finish()
     stage.middle(0)
     stage.middle(1)
     if flight:
@@ -519,14 +600,16 @@
     if ended:
         ended()
     stage.forward(0)
-    stage.forward(1)
+    if after:
+        after()
 
 
 def layer_kernel(dims, names, *refs):
     b = Box(names, refs)
     b.grad_third, b.grad_r2, b.grad_r1, b.gc1_all = b.first, b.second, b.first, b.gy_all
     place = Place(dims)
-    link = Link(b.send_sems, b.recv_sems)
+    sems = b.send_sems, b.recv_sems
+    link = Link(*sems, dims["chain"])
     width, block, items_dev = dims["width"], dims["block"], dims["items_dev"]
     h, t, q_place = place.h, place.t, place.q
     c, b1, b0 = place.c, place.b1, place.b0
@@ -547,7 +630,9 @@
     def span(k):
         return slice(k * half_rows, (k + 1) * half_rows)
 
-    def put(k, value):
+    def put(k, value, before=None):
+        if before:
+            before.release(k)
         b.part[k] = value.astype(BF).reshape(b.part.shape[1:])
 
     def weight(ref, index):
@@ -574,22 +659,47 @@
     def share_columns(steps, dst):
         arrive(steps[0])
         steps[1].wait()
-        return to_share(link, place, lambda _: dst.at[:, t], dst.at[:, t])
+        blocks = dims["seq"] // 2
+        return Share(
+            link, place, lambda t: dst.at[:, t],
+            lambda t, i: dst.at[i * blocks : (i + 1) * blocks, t],
+        )
+
+    def share_rows(dst):
+        return Share(link, place, lambda t: dst.at[:, t], lambda t, i: dst.at[i, t])
+
+    def share_hidden(dst):
+        rows = dst.shape[1] // 2
+        return Share(
+            link, place, lambda t: dst.at[t], lambda t, i: dst.at[t, i * rows : (i + 1) * rows]
+        )
 
     self_share = [share_columns(self_steps[i], b.o_self.at[i]) for i in range(3)]
     waits += spread_end(link, place, b.x_all, 1 - h, second_x)
     so_arrived()
-    so_share = to_share(link, place, lambda _: b.o_so.at[:, t], b.o_so.at[:, t])
-
-    b.m_all[h, c, b1, b0] = b.mem[h]
-    swap_m = link.send(b.mem.at[1 - h], b.m_all.at[h, c, b1, b0], partner)
-    first_m = spread_start(link, place, b.m_all, h)
+    so_share = share_rows(b.o_so)
     cross_steps = [
         columns_out(link, place, b.staged.at[4 + i], b.o_cross.at[i], width) for i in range(3)
     ]
     co_arrived, co_sent = rows_out(link, place, b.staged.at[7], b.o_co)
-    b.c_own[h] = b.cot[h]
-    swap_c = link.send(b.cot.at[1 - h], b.c_own.at[h], partner)
+    b.m_all[h, c, b1, b0] = b.mem[h]
+    swap_m = link.send(b.mem.at[1 - h], b.m_all.at[h, c, b1, b0], partner)
+    first_m = spread_start(link, place, b.m_all, h)
+    for share in self_share:
+        share.forward()
+
+    arrive(waits)
+    rows = rows_of(b.x_all)
+    for index, dst in enumerate((b.sq, b.sk, b.sv)):
+        self_share[index].wait()
+        dst[...] = nn(rows, weight(b.o_self, index)).astype(BF)
+    so_share.forward()
+    cross_share = [share_columns(cross_steps[i], b.o_cross.at[i]) for i in range(3)]
+    co_arrived()
+    co_share = share_rows(b.o_co)
+    mem_waits = spread_end(link, place, b.m_all, h, first_m)
+    swap_m.wait_recv()
+    second_m = spread_start(link, place, b.m_all, 1 - h)
     own_fin.wait()
     own_fout.wait()
     fr, gr = b.o_fin.shape[1], b.o_fout.shape[1]
@@ -597,19 +707,6 @@
     step_fout = link.send(
         b.own_fout.at[pl.ds(pl.multiple_of(t * gr, gr), gr)], b.o_fout.at[t], partner
     )
-    mem_waits = spread_end(link, place, b.m_all, h, first_m)
-    swap_m.wait_recv()
-    second_m = spread_start(link, place, b.m_all, 1 - h)
-    mem_waits += spread_end(link, place, b.m_all, 1 - h, second_m)
-
-    arrive(waits)
-    rows = rows_of(b.x_all)
-    for index, dst in enumerate((b.sq, b.sk, b.sv)):
-        arrive(self_share[index])
-        dst[...] = nn(rows, weight(b.o_self, index)).astype(BF)
-    cross_share = [share_columns(cross_steps[i], b.o_cross.at[i]) for i in range(3)]
-    co_arrived()
-    co_share = to_share(link, place, lambda _: b.o_co.at[:, t], b.o_co.at[:, t])
     length, mem_length = b.dec_len[h], b.mem_len[h]
 
     def self_ok(start, stop):
@@ -632,77 +729,82 @@
 
         return mid
 
-    def sent(kept=()):
-        late = {id(copy) for copy in kept}
-        for copy in link.open:
-            if id(copy) not in late:
-                copy.wait_send()
-        link.open[:] = [copy for copy in link.open if id(copy) in late]
-
-    def self_part(k):
+    def self_part(k, pump):
         attend(
             b.sq, b.sk, b.sv, self_ok, b.sp, b.smix, True, block,
-            k * half_rows, (k + 1) * half_rows,
+            k * half_rows, (k + 1) * half_rows, pump,
         )
         if k == 0:
-            arrive(so_share)
+            so_share.wait()
         put(k, nn(b.smix[span(k)], rows_of(b.o_so)))
 
     def memory_part():
         arrive(mem_waits)
         mems = rows_of(b.m_all)
-        arrive(cross_share[0])
+        cross_share[0].wait()
         b.ck[...] = nn(mems, weight(b.o_cross, 0)).astype(BF)
-        arrive(cross_share[1])
+        cross_share[1].wait()
         b.cv[...] = nn(mems, weight(b.o_cross, 1)).astype(BF)
         spots = lax.broadcasted_iota(jnp.int32, (total_mem, 128), 0)
         cells = b.m_all[...].reshape(-1, b.m_all.shape[-1])[:, model:].astype(F32)
         b.keep[...] = ((spots < mem_length) & ((cells > 0.5) | (spots == 0))).astype(F32)
 
     stage = Stage(
-        link, place, b.part, bufs,
-        forward(0, lambda k: b.x_all[k, c, b1, b0].astype(F32), b.sum_one, b.first), b.first_all,
-    )
-    stage_steps(stage, self_part)
-    step_fin.wait_recv()
-    step_fout.wait_recv()
-    ffn_share = to_share(link, place, lambda _: b.o_fin.at[t], b.o_fin.at[t])
-    ffn_share += to_share(link, place, lambda _: b.o_fout.at[t], b.o_fout.at[t])
+        sems, place, b.part, bufs,
+        forward(0, lambda k: b.x_all[k, c, b1, b0].astype(F32), b.sum_one, b.first), b.first_all, None,
+    )
+    def cross_weights():
+        mem_waits.extend(spread_end(link, place, b.m_all, 1 - h, second_m))
+        for share in cross_share + [co_share]:
+            share.forward()
+
+    stage_steps(stage, self_part, after=cross_weights)
     memory_part()
-
-    def cross_part(k):
+    b.c_own[h] = b.cot[h]
+    swap_c = link.send(b.cot.at[1 - h], b.c_own.at[h], partner)
+    ffn_share = []
+
+    def cross_part(k, pump):
         last.arrive(k)
         if k == 0:
-            sent(ffn_share)
-            arrive(cross_share[2])
+            cross_share[2].wait()
         b.cq[span(k)] = nn(chunk(b.first_all, k), weight(b.o_cross, 2)).astype(BF)
         attend(
             b.cq, b.ck, b.cv, lambda start, stop: b.keep[:, 0:1] > 0.5, b.cp, b.cmix, False, block,
-            k * half_rows, (k + 1) * half_rows,
+            k * half_rows, (k + 1) * half_rows, pump,
         )
         if k == 0:
-            arrive(co_share)
-        put(k, nn(b.cmix[span(k)], rows_of(b.o_co)))
+            co_share.wait()
+            step_fin.wait_recv()
+            ffn_share.append(share_hidden(b.o_fin))
+        put(k, nn(b.cmix[span(k)], rows_of(b.o_co)), last)
 
     last = stage
     stage = Stage(
-        link, place, b.part, bufs, forward(1, lambda k: b.first[k], b.sum_two, b.second),
-        b.second_all,
-    )
-    stage_steps(stage, cross_part)
+        sems, place, b.part, bufs, forward(1, lambda k: b.first[k], b.sum_two, b.second),
+        b.second_all, last,
+    )
+    def ffn_weights():
+        step_fout.wait_recv()
+        ffn_share.append(share_hidden(b.o_fout))
+        for share in ffn_share:
+            share.forward()
+
+    stage_steps(stage, cross_part, after=ffn_weights)
 
     w_ins = (lambda: b.own_fin[...], lambda: b.o_fin[...].reshape(model, -1))
     w_outs = (lambda: b.own_fout[...], lambda: b.o_fout[...].reshape(-1, model))
     hidden = b.own_fin.shape[1]
     last_second = stage
 
-    def ffn_part(k):
+    def ffn_part(k, pump):
         last_second.arrive(k)
         if k == 0:
-            sent()
-            arrive(ffn_share)
+            ffn_share[0].wait()
         rows = chunk(b.second_all, k)
         for index in range(2):
+            if index:
+                pump()
             pre = nn(rows, w_ins[index]())
             cdf = 0.5 * (1.0 + lax.erf(pre * (0.5**0.5)))
             cols = slice(index * hidden, (index + 1) * hidden)
@@ -710,7 +812,10 @@
             b.slope[span(k), cols] = (
                 cdf + pre * (jnp.exp(-0.5 * pre * pre) * 0.3989422804014327)
             ).astype(BF)
-        put(k, nn(b.act[span(k), :hidden], w_outs[0]()) + nn(b.act[span(k), hidden:], w_outs[1]()))
+        if k == 0:
+            ffn_share[1].wait()
+        total = nn(b.act[span(k), :hidden], w_outs[0]())
+        put(k, total + nn(b.act[span(k), hidden:], w_outs[1]()), last_second)
 
     swap_c.wait_recv()
 
@@ -731,42 +836,42 @@
         b.grad_third[k] = result
         return result.astype(BF)
 
-    stage = Stage(link, place, b.part, bufs, turn, b.gy_all)
+    stage = Stage(sems, place, b.part, bufs, turn, b.gy_all, last_second)
     stage_steps(stage, ffn_part)
 
     last_turn = stage
 
-    def ffn_back(k):
+    def ffn_back(k, pump):
         last_turn.arrive(k)
-        if k == 0:
-            sent()
         grad = chunk(b.gy_all, k)
         total = None
         for index in range(2):
+            if index:
+                pump()
             cols = slice(index * hidden, (index + 1) * hidden)
             grad_pre = (nt(grad, w_outs[index]()) * b.slope[span(k), cols].astype(F32)).astype(BF)
             b.slope[span(k), cols] = grad_pre
             term = nt(grad_pre, w_ins[index]())
             total = term if total is None else total + term
-        put(k, total)
+        put(k, total, last_turn)
 
     way_fout = Hidden(
-        link, place, b.g_fout, ("q_fout", dims["lines"] and "l_fout", "s_fout", "z_fout", "d_fout", "r_fout"), b
+        link, place, b.g_fout, ("q_fout", "t_fout", "u_fout", dims["lines"] and "l_fout", "s_fout", "z_fout", "d_fout", "r_fout"), b
     )
     way_fin = Hidden(
-        link, place, b.g_fin, ("q_fin", dims["lines"] and "l_fin", "s_fin", "z_fin", "d_fin", "r_fin"), b
+        link, place, b.g_fin, ("q_fin", "t_fin", "u_fin", dims["lines"] and "l_fin", "s_fin", "z_fin", "d_fin", "r_fin"), b
     )
     way_cross = Columns(
-        link, place, b.g_cross, ("q_cross", dims["lines"] and "l_cross", "s_cross", "z_cross", "d_cross", "r_cross"), b
+        link, place, b.g_cross, ("q_cross", "t_cross", "u_cross", dims["lines"] and "l_cross", "s_cross", "z_cross", "d_cross", "r_cross"), b
     )
     way_self = Columns(
-        link, place, b.g_self, ("q_self", dims["lines"] and "l_self", "s_self", "z_self", "d_self", "r_self"), b
+        link, place, b.g_self, ("q_self", "t_self", "u_self", dims["lines"] and "l_self", "s_self", "z_self", "d_self", "r_self"), b
     )
     way_co = Rows(
-        link, place, b.g_co, ("q_co", dims["lines"] and "l_co", "s_co", "z_co", "d_co", "r_co"), b
+        link, place, b.g_co, ("q_co", "t_co", "u_co", dims["lines"] and "l_co", "s_co", "z_co", "d_co", "r_co"), b
     )
     way_so = Rows(
-        link, place, b.g_so, ("q_so", dims["lines"] and "l_so", "s_so", "z_so", "d_so", "r_so"), b
+        link, place, b.g_so, ("q_so", "t_so", "u_so", dims["lines"] and "l_so", "s_so", "z_so", "d_so", "r_so"), b
     )
 
     def backward(index, res, summed, out):
@@ -797,25 +902,24 @@
         way_fin.send()
 
     stage = Stage(
-        link, place, b.part, bufs, backward(1, b.grad_third, b.sum_two, b.grad_r2), b.gc2_all
+        sems, place, b.part, bufs, backward(1, b.grad_third, b.sum_two, b.grad_r2), b.gc2_all,
+        last_turn,
     )
     stage_steps(stage, ffn_back, out_grads, in_grads)
 
     last_back = stage
-    flying = way_fout.steps + way_fin.steps
-
-    def cross_back(k):
+
+    def cross_back(k, pump):
         last_back.arrive(k)
-        if k == 0:
-            sent(flying)
         b.dmix[span(k)] = nt(chunk(b.gc2_all, k), rows_of(b.o_co)).astype(BF)
         attend_back(
             b.cq, b.ck, b.cv, b.cp, b.dmix, b.dq, b.sum_dk, b.sum_dv, False, block,
-            k * half_rows, (k + 1) * half_rows,
+            k * half_rows, (k + 1) * half_rows, pump,
         )
-        put(k, nt(b.dq[span(k)], weight(b.o_cross, 2)))
+        put(k, nt(b.dq[span(k)], weight(b.o_cross, 2)), last_back)
 
     def cross_grads():
+        way_fout.turn()
         mems = rows_of(b.m_all)
         shape = b.g_cross.shape[1:]
         b.dck[...] = (b.sum_dk[:total_mem] * SCALE).astype(BF)
@@ -832,31 +936,32 @@
         b.part_m[...] = value.astype(BF).reshape(b.part_m.shape)
 
     stage = Stage(
-        link, place, b.part, bufs, backward(0, b.grad_r2, b.sum_one, b.grad_r1), b.gc1_all
-    )
-    stage_steps(stage, cross_back, cross_grads, part_mem)
-    flying += way_cross.steps + way_co.steps
+        sems, place, b.part, bufs, backward(0, b.grad_r2, b.sum_one, b.grad_r1), b.gc1_all,
+        last_back,
+    )
+    def cross_ended():
+        part_mem()
+        way_fin.turn()
+
+    stage_steps(stage, cross_back, cross_grads, cross_ended)
 
     for k in range(2):
         stage.arrive(k)
+        pump = (lambda: stage.forward(1)) if k == 0 else (lambda: None)
         b.dmix[span(k)] = nt(chunk(b.gc1_all, k), rows_of(b.o_so)).astype(BF)
         attend_back(
             b.sq, b.sk, b.sv, b.sp, b.dmix, b.dq, b.sum_dk, b.sum_dv, True, block,
-            k * half_rows, (k + 1) * half_rows,
+            k * half_rows, (k + 1) * half_rows, pump,
         )
-    sent(flying)
     b.dsk[...] = (b.sum_dk[...] * SCALE).astype(BF)
     b.dsv[...] = b.sum_dv[...].astype(BF)
     for k in range(2):
         total = nt(b.dq[span(k)], weight(b.o_self, 0)) + nt(b.dsk[span(k)], weight(b.o_self, 1))
-        put(k, total + nt(b.dsv[span(k)], weight(b.o_self, 2)))
-    seq_sums = []
-    for d in range(1, dims["seq"]):
-        seq_sums.append(
-            link.send(b.sums, b.sums_seq.at[d - 1], {"seq": place.seq_shift(d)})
-        )
+        put(k, total + nt(b.dsv[span(k)], weight(b.o_self, 2)), stage)
+    stage.link.finish()
+    chain = Link(*sems)
     ks = (1 - h, h)
-    red_x = Reduce(link, place, b.part, bufs)
+    red_x = Reduce(chain, place, b.part, bufs)
     mem_bufs = [b.recv0_m, b.send1_m, b.recv1_m, b.keep1_m]
     if dims["bits"] == 3:
         mem_bufs += [b.send2_m, b.recv2_m]
@@ -864,11 +969,6 @@
     for red in (red_x, red_m):
         for index in range(2):
             red.start(index, ks[index])
-    for red in (red_x, red_m):
-        for index in range(2):
-            red.middle(index, ks[index])
-    swap_l = link.send(b.layer.at[1 - h], b.layer_out.at[h], partner)
-    b.layer_out[h] = b.layer[h]
     rows = rows_of(b.x_all)
     shape = b.g_self.shape[1:]
     b.g_self[0] = tn(rows, b.dq[...]).astype(BF).reshape(shape)
@@ -878,46 +978,67 @@
     b.g_so[...] = tn(b.smix[...], rows_of(b.gc1_all)).astype(BF).reshape(b.g_so.shape)
     way_so.send()
     way_fout.add()
+    way_cross.turn()
+    way_co.turn()
+    for red in (red_x, red_m):
+        for index in range(2):
+            red.middle(index, ks[index])
+    copies = []
+    for d in range(1, dims["seq"]):
+        copies.append((b.sums, b.sums_seq.at[d - 1], {"seq": place.seq_shift(d)}))
+    seq_sums = link.batch(copies, b.sums_seq)
+    way_fin.add()
+    swap_l = link.send(b.layer.at[1 - h], b.layer_out.at[h], partner)
+    b.layer_out[h] = b.layer[h]
     b.send_x[...] = (red_x.end(0) + b.grad_r1[1 - h]).astype(BF)
     swap_x = link.send(b.send_x, b.recv_x, partner)
     b.grad_dec[h] = red_x.end(1) + b.grad_r1[h]
     b.send_m[...] = red_m.end(0).astype(BF)
     swap_m = link.send(b.send_m, b.recv_m, partner)
     b.grad_mem[h] = red_m.end(1)
-    arrive(seq_sums)
+    way_fout.gather()
+    way_self.turn()
+    way_so.turn()
+    way_cross.add()
+    way_co.add()
+    way_fin.gather()
+    way_fout.forward()
+    seq_sums.wait_recv()
     value = b.sums[...]
     for d in range(1, dims["seq"]):
         value = value + b.sums_seq[d - 1]
     b.sums_line[...] = value
-    item_sums = []
+    copies = []
     for e in range(1, dims["items"]):
         target = {"items": lax.rem(place.it + e, dims["items"])}
-        item_sums.append(link.send(b.sums_line, b.sums_items.at[e - 1], target))
-    way_fin.add()
+        copies.append((b.sums_line, b.sums_items.at[e - 1], target))
+    item_sums = link.batch(copies, b.sums_items)
     swap_x.wait_recv()
     b.grad_dec[1 - h] = b.recv_x[...].astype(F32)
     swap_m.wait_recv()
     b.grad_mem[1 - h] = b.recv_m[...].astype(F32)
     swap_l.wait_recv()
-    way_fout.gather()
-    way_cross.add()
-    way_co.add()
-    way_fin.gather()
     way_self.add()
     way_so.add()
     way_cross.gather()
     way_co.gather()
-    arrive(item_sums)
+    way_fin.forward()
+    item_sums.wait_recv()
     value = b.sums_line[...]
     for e in range(1, dims["items"]):
         value = value + b.sums_items[e - 1]
     b.sums_out[...] = value
+    way_cross.forward()
+    way_co.forward()
     way_self.gather()
     way_so.gather()
+    way_self.forward()
+    way_so.forward()
     for way in (way_fout, way_fin, way_cross, way_co, way_self, way_so):
         way.finish()
     so_sent()
     co_sent()
+    chain.finish()
     link.finish()
 
 
@@ -947,6 +1068,7 @@
         "items_dev": items_dev, "items": items, "seq": seq, "group": group, "share": share,
         "bits": bits, "chips": chips, "width": width, "model": model, "block": 256,
         "total_dec": total_dec, "total_mem": total_mem, "lines": lines,
+        "chain": 12 + 2 * (bits - 2),
     }
     cells = jnp.broadcast_to((cell_mask == 1).astype(BF)[:, :, None], (items_dev, mb, 128))
     mem_cells = jnp.concatenate([memory, cells], axis=2)
@@ -1007,21 +1129,27 @@
                 ("send2" + name, (items_dev, rows, model), BF),
                 ("recv2" + name, (items_dev, rows, model), BF),
             ]
-    for name, grad, quarter, moved, done in (
-        ("fin", (2, share, fr, hidden), (2, fr, hidden), (fr, hidden), (fr, hidden)),
-        ("fout", (2, share, gr, model), (2, gr, model), (gr, model), (gr, model)),
-        ("cross", cols, (3, seq, wr, width), (seq, 3, wr, width), (3, wr, model)),
-        ("self", cols, (3, seq, wr, width), (seq, 3, wr, width), (3, wr, model)),
-        ("co", (items_dev, share, wr, model), (items_dev, wr, model), (items_dev, wr, model), (wr, model)),
-        ("so", (items_dev, share, wr, model), (items_dev, wr, model), (items_dev, wr, model), (wr, model)),
+    for name, grad, quarter, piece, moved, done in (
+        ("fin", (2, share, fr, hidden), (2, fr, hidden), (2, fr // 2, hidden), (fr, hidden),
+         (fr, hidden)),
+        ("fout", (2, share, gr, model), (2, gr, model), (2, gr // 2, model), (gr, model), (gr, model)),
+        ("cross", cols, (3, seq, wr, width), (3, seq // 2, wr, width), (seq, 3, wr, width),
+         (3, wr, model)),
+        ("self", cols, (3, seq, wr, width), (3, seq // 2, wr, width), (seq, 3, wr, width),
+         (3, wr, model)),
+        ("co", (items_dev, share, wr, model), (items_dev, wr, model), (wr, model),
+         (items_dev, wr, model), (wr, model)),
+        ("so", (items_dev, share, wr, model), (items_dev, wr, model), (wr, model),
+         (items_dev, wr, model), (wr, model)),
     ):
         scratch += [
-            ("g_" + name, grad, BF), ("q_" + name, (share - 1,) + quarter, BF),
-            ("s_" + name, quarter, BF), ("z_" + name, moved, BF), ("d_" + name, done, BF),
+            ("g_" + name, grad, BF), ("q_" + name, (2, 2) + piece, BF), ("t_" + name, (2,) + piece, BF),
+            ("u_" + name, (2,) + piece, BF), ("s_" + name, quarter, BF), ("z_" + name, moved, BF),
+            ("d_" + name, done, BF),
         ]
         if lines:
             scratch.append(("l_" + name, (lines,) + quarter, BF))
-    copies = 320 + 16 * (seq - 8) + 12 * (bits - 2) + 12 * lines
+    copies = dims["chain"] + 160 + 12 * (bits - 2)
     names = [x[0] for x in ins + outs + scratch] + ["send_sems", "recv_sems"]
     results = pl.pallas_call(
         functools.partial(layer_kernel, dims, names),

time: 288 us -> 257 us (0.89)
  Pallas kernels: 273 us -> 242 us
    pallas_call x1, Pallas kernels: 273 us -> 242 us  [shards(): pl.pallas_call(functools.partial(layer_kernel, dims, names), name='layer'...]
where the time goes in v3:
time: 257 us
  Pallas kernels  242 us (94%)
  other arithmetic  8.52 us (3%)
  local copies, waits for them, and re-layouts  5.4 us (2%)
    pallas_call x1, Pallas kernels, shards(): pl.pallas_call(functools.partial(layer_kernel, dims, names), name='layer'...  242 us

profile of v3, /device:TPU:0, one launch (start us, length us, event | category | flops | bytes accessed | tf_op | source)
XLA Modules:
  0.0 256.6 jit_solution(13888744537731764731)
XLA Ops:
  0.6 0.7 compare_convert_fusion
  1.3 0.1 broadcast_in_dim.2
  1.4 1.6 pad_maximum_fusion.refs_1_
  3.0 242.0 %layer.1 = (bf16[2,64,1024]{2,1,0:T(8,128)(2,1)}, f32[2,64,1024]{2,1,0:T(8,128)}, f32[2,48,1024]{2,1,0:T(8,128)}, f32[8,1024]{1,0:T(8,128)}, bf16[4,3,32,1024]{3...) custom-call(bf16[2,64,1024]{2,1,0:T(8,128)(2,1)} %refs_0_.1, ...), custom_call_target="tpu_custom_call" | custom-call | tf_op jit(solution)/shard_map/layer/pallas_call | solution.py:1154
  245.1 1.8 convert_bitcast_fusion
  246.9 1.2 fusion.1
  248.0 0.0 copy-start.5
  248.0 0.0 copy-start.6
  248.0 1.2 fusion
  249.2 0.0 copy-start.7
  249.2 0.0 copy-start.1
  249.2 0.0 copy-done.5
  249.2 0.1 copy-done.6
  249.3 1.1 bitcast_convert_fusion.2
  250.4 0.0 copy-done.7
  250.4 0.6 fusion.2
  251.0 0.0 copy-done.1
  251.0 0.0 copy-start
  251.0 1.6 bitcast_convert_fusion
  252.7 0.0 copy-done
  252.7 0.0 copy-start.4
  252.7 0.0 copy-start.2
  252.7 1.7 bitcast_convert_fusion.1
  254.4 0.0 copy-start.3
  254.4 0.0 copy-done.4
  254.4 0.7 copy.36
  255.1 0.0 copy-done.2
  255.1 0.8 copy.37
  255.9 0.0 copy-done.3
  255.9 0.7 copy.38
Async XLA Ops:
  248.0 1.2 copy-start.5
  248.0 1.3 copy-start.6
  249.2 1.2 copy-start.7
  249.2 1.8 copy-start.1
  251.0 1.6 copy-start
  252.7 1.7 copy-start.4
  252.7 2.4 copy-start.2
  254.4 1.5 copy-start.3

commit v4 on v3

--- a/solution.py
+++ b/solution.py
@@ -63,6 +63,10 @@
         wait = self.make(whole, whole, copies[0][2], index)
         self.open.append(wait)
         return wait
+
+    def settle(self, copy):
+        copy.wait_send()
+        self.open = [other for other in self.open if other is not copy]
 
     def local(self, src, dst):
         copy = pltpu.make_async_copy(src, dst, self.send_sems.at[self.index()])
@@ -640,22 +644,15 @@
 
     weights = (b.w_sq, b.w_sk, b.w_sv, b.w_so, b.w_ck, b.w_cv, b.w_cq, b.w_co)
     rows_t = pl.ds(pl.multiple_of(t * wr, wr), wr)
-    staged = [link.local(w.at[rows_t], b.staged.at[i]) for i, w in enumerate(weights)]
+    index = link.index()
+    for i, w in enumerate(weights):
+        pltpu.make_async_copy(w.at[rows_t], b.staged.at[i], b.send_sems.at[index]).start()
+    staged = pltpu.make_async_copy(b.staged, b.staged, b.send_sems.at[index])
     own_fin = link.local(b.f_in, b.own_fin)
     own_fout = link.local(b.f_out, b.own_fout)
     greet(place.seq_peers() + place.items_peers())
 
     swap_x = link.send(b.dec.at[1 - h], b.x_all.at[h, c, b1, b0], partner)
-    b.x_all[h, c, b1, b0] = b.dec[h]
-    first_x = spread_start(link, place, b.x_all, h)
-    for copy in staged:
-        copy.wait()
-    self_steps = [columns_out(link, place, b.staged.at[i], b.o_self.at[i], width) for i in range(3)]
-    waits = spread_end(link, place, b.x_all, h, first_x)
-    swap_x.wait_recv()
-    second_x = spread_start(link, place, b.x_all, 1 - h)
-    so_arrived, so_sent = rows_out(link, place, b.staged.at[3], b.o_so)
-
     def share_columns(steps, dst):
         arrive(steps[0])
         steps[1].wait()
@@ -674,23 +671,53 @@
             link, place, lambda t: dst.at[t], lambda t, i: dst.at[t, i * rows : (i + 1) * rows]
         )
 
-    self_share = [share_columns(self_steps[i], b.o_self.at[i]) for i in range(3)]
+    def join_cells():
+        mb = b.cells.shape[1]
+        same = lax.broadcasted_iota(jnp.int32, (mb, mb), 0) == lax.broadcasted_iota(
+            jnp.int32, (mb, mb), 1
+        )
+        for k in range(items_dev):
+            flags = (b.cells[k : k + 1] == 1).astype(F32)
+            column = jnp.sum(jnp.where(same, flags, 0.0), axis=1, keepdims=True)
+            b.mem_cells[k, :, :model] = b.mem[k]
+            b.mem_cells[k, :, model:] = jnp.broadcast_to(column, (mb, 128)).astype(BF)
+
+    def self_columns(i):
+        return columns_out(link, place, b.staged.at[i], b.o_self.at[i], width)
+
+    b.x_all[h, c, b1, b0] = b.dec[h]
+    staged.wait()
+    steps_q = self_columns(0)
+    first_x = spread_start(link, place, b.x_all, h)
+    link.settle(steps_q[0][0])
+    steps_k = self_columns(1)
+    waits = spread_end(link, place, b.x_all, h, first_x)
+    swap_x.wait_recv()
+    second_x = spread_start(link, place, b.x_all, 1 - h)
+    self_share = [share_columns(steps_q, b.o_self.at[0])]
+    link.settle(steps_k[0][0])
+    steps_v = self_columns(2)
+    so_arrived, so_sent = rows_out(link, place, b.staged.at[3], b.o_so)
     waits += spread_end(link, place, b.x_all, 1 - h, second_x)
+    self_share.append(share_columns(steps_k, b.o_self.at[1]))
+    self_share[0].forward()
+    self_share.append(share_columns(steps_v, b.o_self.at[2]))
     so_arrived()
     so_share = share_rows(b.o_so)
     cross_steps = [
         columns_out(link, place, b.staged.at[4 + i], b.o_cross.at[i], width) for i in range(3)
     ]
     co_arrived, co_sent = rows_out(link, place, b.staged.at[7], b.o_co)
-    b.m_all[h, c, b1, b0] = b.mem[h]
-    swap_m = link.send(b.mem.at[1 - h], b.m_all.at[h, c, b1, b0], partner)
+    join_cells()
+    b.m_all[h, c, b1, b0] = b.mem_cells[h]
+    swap_m = link.send(b.mem_cells.at[1 - h], b.m_all.at[h, c, b1, b0], partner)
     first_m = spread_start(link, place, b.m_all, h)
-    for share in self_share:
-        share.forward()
 
     arrive(waits)
     rows = rows_of(b.x_all)
     for index, dst in enumerate((b.sq, b.sk, b.sv)):
+        if index:
+            self_share[index].forward()
         self_share[index].wait()
         dst[...] = nn(rows, weight(b.o_self, index)).astype(BF)
     so_share.forward()
@@ -1046,6 +1073,22 @@
     return jax.ShapeDtypeStruct(tuple(dims), dtype)
 
 
+def outputs_kernel(layer, dec, mem, cross, own, co, so, fin, fout, sums, *outs):
+    o_layer, o_dec, o_mem = outs[:3]
+    o_layer[...] = layer[...]
+    o_dec[...] = dec[...]
+    o_mem[...] = mem[...]
+    for index in range(3):
+        outs[3 + index][...] = own[0, index].astype(F32)
+        outs[7 + index][...] = cross[0, index].astype(F32)
+    outs[6][...] = so[0].astype(F32)
+    outs[10][...] = co[0].astype(F32)
+    outs[11][...] = fin[0].astype(F32)
+    outs[12][...] = fout[0].astype(F32)
+    outs[13][...] = sums[0:3]
+    outs[14][...] = sums[3:6]
+
+
 def shards(
     mesh, dec_in, memory, dec_len, mem_len, cell_mask, self_query, self_key, self_value, self_out,
     cross_query, cross_key, cross_value, cross_out, ffn_in, ffn_out, norm_gain, norm_bias, cotangent,
@@ -1070,11 +1113,8 @@
         "total_dec": total_dec, "total_mem": total_mem, "lines": lines,
         "chain": 12 + 2 * (bits - 2),
     }
-    cells = jnp.broadcast_to((cell_mask == 1).astype(BF)[:, :, None], (items_dev, mb, 128))
-    mem_cells = jnp.concatenate([memory, cells], axis=2)
-
     ins = [
-        ("dec", dec_in, VM), ("mem", mem_cells, VM), ("cot", cotangent, VM),
+        ("dec", dec_in, VM), ("mem", memory, VM), ("cells", cell_mask, VM), ("cot", cotangent, VM),
         ("dec_len", dec_len, SM), ("mem_len", mem_len, SM),
         ("w_sq", self_query, HBM), ("w_sk", self_key, HBM), ("w_sv", self_value, HBM),
         ("w_so", self_out, HBM), ("w_cq", cross_query, HBM), ("w_ck", cross_key, HBM),
@@ -1093,7 +1133,7 @@
     cols = (3, seq, share, wr, width)
     scratch = [
         ("x_all", grid + (rb, model), BF), ("m_all", grid + (mb, model + 128), BF),
-        ("c_own", own, BF), ("staged", (8, wr, model), BF),
+        ("mem_cells", (items_dev, mb, model + 128), BF), ("c_own", own, BF), ("staged", (8, wr, model), BF),
         ("own_fin", (model, hidden), BF), ("own_fout", (hidden, model), BF),
         ("o_self", cols, BF), ("o_cross", cols, BF),
         ("o_so", (items_dev, share, wr, model), BF), ("o_co", (items_dev, share, wr, model), BF),
@@ -1149,7 +1189,7 @@
         ]
         if lines:
             scratch.append(("l_" + name, (lines,) + quarter, BF))
-    copies = dims["chain"] + 160 + 12 * (bits - 2)
+    copies = dims["chain"] + 153 + 12 * (bits - 2)
     names = [x[0] for x in ins + outs + scratch] + ["send_sems", "recv_sems"]
     results = pl.pallas_call(
         functools.partial(layer_kernel, dims, names),
@@ -1164,14 +1204,42 @@
         ),
     )(*[x[1] for x in ins])
     layer_out, grad_dec, grad_memory, sums, r_cross, r_self, r_co, r_so, r_fin, r_fout = results
-    f_cross = r_cross.transpose(1, 0, 2, 3).reshape(3, share * wr, model).astype(F32)
-    f_self = r_self.transpose(1, 0, 2, 3).reshape(3, share * wr, model).astype(F32)
+    tok, mem_rows = items_dev * rb, items_dev * mb
+    pieces = (
+        ((tok, model), (tok // share, model), BF), ((tok, model), (tok // share, model), F32),
+        ((mem_rows, model), (mem_rows // share, model), F32),
+    )
+    heads_in = [
+        pl.BlockSpec((1, 3, wr, model), lambda i: (i, 0, 0, 0)),
+        pl.BlockSpec((1, 3, wr, model), lambda i: (i, 0, 0, 0)),
+        pl.BlockSpec((1, wr, model), lambda i: (i, 0, 0)),
+        pl.BlockSpec((1, wr, model), lambda i: (i, 0, 0)),
+        pl.BlockSpec((1, fr, hidden), lambda i: (i, 0, 0)),
+        pl.BlockSpec((1, gr, model), lambda i: (i, 0, 0)),
+        pl.BlockSpec((8, model), lambda i: (0, 0)),
+    ]
+    row_specs = [pl.BlockSpec(x[1], lambda i: (i, 0)) for x in pieces]
+    square = (share * wr, model)
+    outs = pl.pallas_call(
+        outputs_kernel,
+        name="outputs",
+        grid=(share,),
+        in_specs=row_specs + heads_in,
+        out_specs=row_specs
+        + [pl.BlockSpec((wr, model), lambda i: (i, 0))] * 8
+        + [pl.BlockSpec((fr, hidden), lambda i: (i, 0)), pl.BlockSpec((gr, model), lambda i: (i, 0))]
+        + [pl.BlockSpec((3, model), lambda i: (0, 0))] * 2,
+        out_shape=[shape(x[0], x[2]) for x in pieces]
+        + [shape(square, F32)] * 8
+        + [shape((model, hidden), F32), shape((hidden, model), F32)]
+        + [shape((3, model), F32)] * 2,
+        compiler_params=pltpu.CompilerParams(vmem_limit_bytes=VMEM_BYTES // 2),
+    )(
+        layer_out.reshape(tok, model), grad_dec.reshape(tok, model),
+        grad_memory.reshape(mem_rows, model), r_cross, r_self, r_co, r_so, r_fin, r_fout, sums,
+    )
     return (
-        layer_out, grad_dec, grad_memory,
-        f_self[0], f_self[1], f_self[2], r_so.reshape(share * wr, model).astype(F32),
-        f_cross[0], f_cross[1], f_cross[2], r_co.reshape(share * wr, model).astype(F32),
-        r_fin.reshape(model, hidden).astype(F32), r_fout.reshape(hidden, model).astype(F32),
-        sums[0:3], sums[3:6],
+        outs[0].reshape(own), outs[1].reshape(own), outs[2].reshape(own_m), *outs[3:],
     )
 
 

time: 257 us -> 258 us (level)
  other arithmetic: 8.52 us -> 0 us
  local copies, waits for them, and re-layouts: 5.4 us -> 10.3 us
  Pallas kernels: 242 us -> 246 us
    unnamed x19 -> x20, local copies, waits for them, and re-layouts: 2.35 us -> 10.3 us
    convert_element_type x5 -> x0, other arithmetic: 6.88 us -> none  [the longest x1 1.78 us: shards(): r_cross.transpose(1, 0, 2, 3).reshape(3, share * wr, model).astype(F32)]
    pallas_call x0 -> x1, Pallas kernels: none -> 3.88 us  [shards(): pl.pallas_call(outputs_kernel, name='outputs', grid=(share,), in_specs=ro...]
    slice x3 -> x0, local copies, waits for them, and re-layouts: 2.97 us -> none  [the longest x1 1.18 us: shards(): f_self[2]]
where the time goes in v4:
time: 258 us; the launch traced here: 257 us
  Pallas kernels  246 us (95%)
  local copies, waits for them, and re-layouts  10.3 us (4%)
    pallas_call x1, Pallas kernels, shards(): pl.pallas_call(functools.partial(layer_kernel, dims, names), name='layer'...  242 us
    unnamed x20, local copies, waits for them, and re-layouts  10.3 us

profile of v4, /device:TPU:0, one launch (start us, length us, event | category | flops | bytes accessed | tf_op | source)
XLA Modules:
  0.0 257.4 jit_solution(1082692606829862235)
XLA Ops:
  0.7 242.3 %layer.1 = (bf16[2,64,1024]{2,1,0:T(8,128)(2,1)}, f32[2,64,1024]{2,1,0:T(8,128)}, f32[2,48,1024]{2,1,0:T(8,128)}, f32[8,1024]{1,0:T(8,128)}, bf16[4,3,32,1024]{3...) custom-call(bf16[2,64,1024]{2,1,0:T(8,128)(2,1)} %refs_0_.1, ...), custom_call_target="tpu_custom_call" | custom-call | tf_op jit(solution)/shard_map/layer/pallas_call | solution.py:1194
  243.0 0.0 copy-start
  243.0 1.2 copy-done
  244.2 0.0 copy-start.1
  244.2 1.2 copy-done.1
  245.5 0.0 copy-start.2
  245.5 1.1 copy-done.2
  246.6 0.0 copy-start.3
  246.6 1.1 copy-done.3
  247.7 0.0 copy-start.4
  247.7 1.0 copy-done.4
  248.8 0.0 copy-start.5
  248.8 1.0 copy-done.5
  249.8 0.0 copy-start.6
  249.8 0.9 copy-done.6
  250.7 0.0 copy-start.7
  250.7 0.9 copy-done.7
  251.7 0.0 copy-start.8
  251.7 0.9 copy-done.8
  252.6 0.0 copy-start.9
  252.6 0.8 copy-done.9
  253.4 3.9 %outputs.1 = (bf16[128,1024]{1,0:T(8,128)(2,1)}, f32[128,1024]{1,0:T(8,128)}, f32[96,1024]{1,0:T(8,128)}, f32[128,1024]{1,0:T(8,128)}, f32[128,1024]{1,0:T(8,128...) custom-call(bf16[128,1024]{1,0:T(8,128)(2,1)S(1)} %bitcast.8, ...), custom_call_target="tpu_custom_call" | custom-call | tf_op jit(solution)/shard_map/outputs/pallas_call | solution.py:1223
Async XLA Ops:
  243.0 1.2 copy-start
  244.2 1.2 copy-start.1
  245.5 1.1 copy-start.2
  246.6 1.1 copy-start.3
  247.7 1.0 copy-start.4
  248.8 1.0 copy-start.5
  249.8 0.9 copy-start.6
  250.7 0.9 copy-start.7
  251.7 0.9 copy-start.8
  252.6 0.8 copy-start.9

commit v5 on v4

--- a/solution.py
+++ b/solution.py
@@ -151,10 +151,10 @@
     for d in range(1, seq):
         target = place.seq_shift(d)
         cols = pl.ds(pl.multiple_of(lax.rem(target, group) * width, width), width)
-        copies.append((src.at[:, cols], dst.at[place.me, place.t], {"seq": target}))
-    steps = [link.batch(copies, dst.at[0 : seq - 1, place.t])]
+        copies.append((src.at[:, :, cols], dst.at[:, place.me, place.t], {"seq": target}))
+    steps = link.batch(copies, dst.at[:, 0 : seq - 1, place.t])
     cols = pl.ds(pl.multiple_of(place.q * width, width), width)
-    return steps, link.local(src.at[:, cols], dst.at[place.me, place.t])
+    return steps, link.local(src.at[:, :, cols], dst.at[:, place.me, place.t])
 
 
 def rows_out(link, place, src, dst):
@@ -653,9 +653,7 @@
     greet(place.seq_peers() + place.items_peers())
 
     swap_x = link.send(b.dec.at[1 - h], b.x_all.at[h, c, b1, b0], partner)
-    def share_columns(steps, dst):
-        arrive(steps[0])
-        steps[1].wait()
+    def share_columns(dst):
         blocks = dims["seq"] // 2
         return Share(
             link, place, lambda t: dst.at[:, t],
@@ -682,51 +680,26 @@
             b.mem_cells[k, :, :model] = b.mem[k]
             b.mem_cells[k, :, model:] = jnp.broadcast_to(column, (mb, 128)).astype(BF)
 
-    def self_columns(i):
-        return columns_out(link, place, b.staged.at[i], b.o_self.at[i], width)
-
     b.x_all[h, c, b1, b0] = b.dec[h]
+    first_x = spread_start(link, place, b.x_all, h)
     staged.wait()
-    steps_q = self_columns(0)
-    first_x = spread_start(link, place, b.x_all, h)
-    link.settle(steps_q[0][0])
-    steps_k = self_columns(1)
+    steps, own_self = columns_out(link, place, b.staged.at[0:3], b.o_self, width)
     waits = spread_end(link, place, b.x_all, h, first_x)
     swap_x.wait_recv()
     second_x = spread_start(link, place, b.x_all, 1 - h)
-    self_share = [share_columns(steps_q, b.o_self.at[0])]
-    link.settle(steps_k[0][0])
-    steps_v = self_columns(2)
     so_arrived, so_sent = rows_out(link, place, b.staged.at[3], b.o_so)
+    steps.wait_recv()
+    own_self.wait()
+    self_share = [share_columns(b.o_self.at[i]) for i in range(3)]
     waits += spread_end(link, place, b.x_all, 1 - h, second_x)
-    self_share.append(share_columns(steps_k, b.o_self.at[1]))
-    self_share[0].forward()
-    self_share.append(share_columns(steps_v, b.o_self.at[2]))
     so_arrived()
     so_share = share_rows(b.o_so)
-    cross_steps = [
-        columns_out(link, place, b.staged.at[4 + i], b.o_cross.at[i], width) for i in range(3)
-    ]
+    cross_steps, own_cross = columns_out(link, place, b.staged.at[4:7], b.o_cross, width)
     co_arrived, co_sent = rows_out(link, place, b.staged.at[7], b.o_co)
     join_cells()
     b.m_all[h, c, b1, b0] = b.mem_cells[h]
     swap_m = link.send(b.mem_cells.at[1 - h], b.m_all.at[h, c, b1, b0], partner)
     first_m = spread_start(link, place, b.m_all, h)
-
-    arrive(waits)
-    rows = rows_of(b.x_all)
-    for index, dst in enumerate((b.sq, b.sk, b.sv)):
-        if index:
-            self_share[index].forward()
-        self_share[index].wait()
-        dst[...] = nn(rows, weight(b.o_self, index)).astype(BF)
-    so_share.forward()
-    cross_share = [share_columns(cross_steps[i], b.o_cross.at[i]) for i in range(3)]
-    co_arrived()
-    co_share = share_rows(b.o_co)
-    mem_waits = spread_end(link, place, b.m_all, h, first_m)
-    swap_m.wait_recv()
-    second_m = spread_start(link, place, b.m_all, 1 - h)
     own_fin.wait()
     own_fout.wait()
     fr, gr = b.o_fin.shape[1], b.o_fout.shape[1]
@@ -734,6 +707,23 @@
     step_fout = link.send(
         b.own_fout.at[pl.ds(pl.multiple_of(t * gr, gr), gr)], b.o_fout.at[t], partner
     )
+    for share in self_share:
+        share.forward()
+
+    arrive(waits)
+    rows = rows_of(b.x_all)
+    for index, dst in enumerate((b.sq, b.sk, b.sv)):
+        self_share[index].wait()
+        dst[...] = nn(rows, weight(b.o_self, index)).astype(BF)
+    so_share.forward()
+    cross_steps.wait_recv()
+    own_cross.wait()
+    cross_share = [share_columns(b.o_cross.at[i]) for i in range(3)]
+    co_arrived()
+    co_share = share_rows(b.o_co)
+    mem_waits = spread_end(link, place, b.m_all, h, first_m)
+    swap_m.wait_recv()
+    second_m = spread_start(link, place, b.m_all, 1 - h)
     length, mem_length = b.dec_len[h], b.mem_len[h]
 
     def self_ok(start, stop):
@@ -784,12 +774,16 @@
         mem_waits.extend(spread_end(link, place, b.m_all, 1 - h, second_m))
         for share in cross_share + [co_share]:
             share.forward()
-
+        step_fin.wait_recv()
+        ffn_share.append(share_hidden(b.o_fin))
+        step_fout.wait_recv()
+        ffn_share.append(share_hidden(b.o_fout))
+
+    ffn_share = []
     stage_steps(stage, self_part, after=cross_weights)
     memory_part()
     b.c_own[h] = b.cot[h]
     swap_c = link.send(b.cot.at[1 - h], b.c_own.at[h], partner)
-    ffn_share = []
 
     def cross_part(k, pump):
         last.arrive(k)
@@ -802,8 +796,6 @@
         )
         if k == 0:
             co_share.wait()
-            step_fin.wait_recv()
-            ffn_share.append(share_hidden(b.o_fin))
         put(k, nn(b.cmix[span(k)], rows_of(b.o_co)), last)
 
     last = stage
@@ -812,12 +804,10 @@
         b.second_all, last,
     )
     def ffn_weights():
-        step_fout.wait_recv()
-        ffn_share.append(share_hidden(b.o_fout))
         for share in ffn_share:
             share.forward()
 
-    stage_steps(stage, cross_part, after=ffn_weights)
+    stage_steps(stage, cross_part, ffn_weights)
 
     w_ins = (lambda: b.own_fin[...], lambda: b.o_fin[...].reshape(model, -1))
     w_outs = (lambda: b.own_fout[...], lambda: b.o_fout[...].reshape(-1, model))
@@ -1189,7 +1179,7 @@
         ]
         if lines:
             scratch.append(("l_" + name, (lines,) + quarter, BF))
-    copies = dims["chain"] + 153 + 12 * (bits - 2)
+    copies = dims["chain"] + 145 + 12 * (bits - 2)
     names = [x[0] for x in ins + outs + scratch] + ["send_sems", "recv_sems"]
     results = pl.pallas_call(
         functools.partial(layer_kernel, dims, names),
@@ -1233,7 +1223,7 @@
         + [shape(square, F32)] * 8
         + [shape((model, hidden), F32), shape((hidden, model), F32)]
         + [shape((3, model), F32)] * 2,
-        compiler_params=pltpu.CompilerParams(vmem_limit_bytes=VMEM_BYTES // 2),
+        compiler_params=pltpu.CompilerParams(vmem_limit_bytes=VMEM_BYTES),
     )(
         layer_out.reshape(tok, model), grad_dec.reshape(tok, model),
         grad_memory.reshape(mem_rows, model), r_cross, r_self, r_co, r_so, r_fin, r_fout, sums,

time: 258 us -> 247 us (0.957)
  local copies, waits for them, and re-layouts: 10.3 us -> 0 us
    unnamed x20 -> x0, local copies, waits for them, and re-layouts: 10.3 us -> none
    pallas_call x1, Pallas kernels: 242 us -> 239 us  [shards(): pl.pallas_call(functools.partial(layer_kernel, dims, names), name='layer'...]
    pallas_call x1, Pallas kernels: 3.88 us -> 6.71 us  [shards(): pl.pallas_call(outputs_kernel, name='outputs', grid=(share,), in_specs=ro...]
where the time goes in v5:
time: 247 us
  Pallas kernels  246 us (100%)
    pallas_call x1, Pallas kernels, shards(): pl.pallas_call(functools.partial(layer_kernel, dims, names), name='layer'...  239 us
    pallas_call x1, Pallas kernels, shards(): pl.pallas_call(outputs_kernel, name='outputs', grid=(share,), in_specs=ro...  6.71 us

profile of v5, /device:TPU:0, one launch (start us, length us, event | category | flops | bytes accessed | tf_op | source)
XLA Modules:
  0.0 246.7 jit_solution(8710062623166296260)
XLA Ops:
  0.7 239.2 %layer.1 = (bf16[2,64,1024]{2,1,0:T(8,128)(2,1)}, f32[2,64,1024]{2,1,0:T(8,128)}, f32[2,48,1024]{2,1,0:T(8,128)}, f32[8,1024]{1,0:T(8,128)}, bf16[4,3,32,1024]{3...) custom-call(bf16[2,64,1024]{2,1,0:T(8,128)(2,1)} %refs_0_.1, ...), custom_call_target="tpu_custom_call" | custom-call | tf_op jit(solution)/shard_map/layer/pallas_call | solution.py:1184
  239.8 6.7 %outputs.1 = (bf16[128,1024]{1,0:T(8,128)(2,1)}, f32[128,1024]{1,0:T(8,128)}, f32[96,1024]{1,0:T(8,128)}, f32[128,1024]{1,0:T(8,128)}, f32[128,1024]{1,0:T(8,128...) custom-call(bf16[128,1024]{1,0:T(8,128)(2,1)} %bitcast.8, ...), custom_call_target="tpu_custom_call" | custom-call | tf_op jit(solution)/shard_map/outputs/pallas_call | solution.py:1213

commit v6 on v5

--- a/solution.py
+++ b/solution.py
@@ -498,6 +498,35 @@
         self.done[...] = (self.total[0].astype(F32) + self.moved[...].astype(F32)).astype(BF)
 
 
+class HiddenFirst(Quarters):
+    def cross(self):
+        self.step = self.link.send(self.grad.at[1], self.moved, self.place.partner())
+
+    def send(self):
+        self.step.wait_recv()
+        for t in range(self.place.dims["share"]):
+            value = self.grad[0, t].astype(F32) + self.moved[t].astype(F32)
+            self.grad[0, t] = value.astype(BF)
+        self.total = self.done
+        super().send()
+
+    def piece(self, t, i):
+        rows = self.grad.shape[2] // 2
+        return 0, t, slice(i * rows, (i + 1) * rows)
+
+    def halves(self, i):
+        rows = self.grad.shape[2] // 2
+        return slice(i * rows, (i + 1) * rows)
+
+    cut = Hidden.cut
+
+    def along(self):
+        pass
+
+    def close(self):
+        pass
+
+
 class Columns(Quarters):
     def piece(self, t, i):
         blocks = self.grad.shape[1] // 2
@@ -858,8 +887,22 @@
 
     last_turn = stage
 
+    way_fout = HiddenFirst(
+        link, place, b.g_fout,
+        ("q_fout", "t_fout", "u_fout", dims["lines"] and "l_fout", "", "z_fout", "d_fout", "r_fout"), b
+    )
+    def out_grads():
+        grad = rows_of(b.gy_all)
+        for index in range(2):
+            cols = slice(index * hidden, (index + 1) * hidden)
+            value = tn(b.act[:, cols], grad)
+            b.g_fout[index] = value.astype(BF).reshape(b.g_fout.shape[1:])
+        way_fout.cross()
+
     def ffn_back(k, pump):
         last_turn.arrive(k)
+        if k == 1:
+            out_grads()
         grad = chunk(b.gy_all, k)
         total = None
         for index in range(2):
@@ -872,9 +915,6 @@
             total = term if total is None else total + term
         put(k, total, last_turn)
 
-    way_fout = Hidden(
-        link, place, b.g_fout, ("q_fout", "t_fout", "u_fout", dims["lines"] and "l_fout", "s_fout", "z_fout", "d_fout", "r_fout"), b
-    )
     way_fin = Hidden(
         link, place, b.g_fin, ("q_fin", "t_fin", "u_fin", dims["lines"] and "l_fin", "s_fin", "z_fin", "d_fin", "r_fin"), b
     )
@@ -902,14 +942,6 @@
 
         return mid
 
-    def out_grads():
-        grad = rows_of(b.gy_all)
-        for index in range(2):
-            cols = slice(index * hidden, (index + 1) * hidden)
-            value = tn(b.act[:, cols], grad)
-            b.g_fout[index] = value.astype(BF).reshape(b.g_fout.shape[1:])
-        way_fout.send()
-
     def in_grads():
         rows = rows_of(b.second_all)
         for index in range(2):
@@ -922,7 +954,7 @@
         sems, place, b.part, bufs, backward(1, b.grad_third, b.sum_two, b.grad_r2), b.gc2_all,
         last_turn,
     )
-    stage_steps(stage, ffn_back, out_grads, in_grads)
+    stage_steps(stage, ffn_back, in_grads)
 
     last_back = stage
 
@@ -934,9 +966,10 @@
             k * half_rows, (k + 1) * half_rows, pump,
         )
         put(k, nt(b.dq[span(k)], weight(b.o_cross, 2)), last_back)
+        if k == 1:
+            way_fin.turn()
 
     def cross_grads():
-        way_fout.turn()
         mems = rows_of(b.m_all)
         shape = b.g_cross.shape[1:]
         b.dck[...] = (b.sum_dk[:total_mem] * SCALE).astype(BF)
@@ -956,11 +989,7 @@
         sems, place, b.part, bufs, backward(0, b.grad_r2, b.sum_one, b.grad_r1), b.gc1_all,
         last_back,
     )
-    def cross_ended():
-        part_mem()
-        way_fin.turn()
-
-    stage_steps(stage, cross_back, cross_grads, cross_ended)
+    stage_steps(stage, cross_back, cross_grads, part_mem)
 
     for k in range(2):
         stage.arrive(k)
@@ -994,9 +1023,9 @@
     way_self.send()
     b.g_so[...] = tn(b.smix[...], rows_of(b.gc1_all)).astype(BF).reshape(b.g_so.shape)
     way_so.send()
-    way_fout.add()
     way_cross.turn()
     way_co.turn()
+    way_fin.add()
     for red in (red_x, red_m):
         for index in range(2):
             red.middle(index, ks[index])
@@ -1004,7 +1033,7 @@
     for d in range(1, dims["seq"]):
         copies.append((b.sums, b.sums_seq.at[d - 1], {"seq": place.seq_shift(d)}))
     seq_sums = link.batch(copies, b.sums_seq)
-    way_fin.add()
+    way_fout.send()
     swap_l = link.send(b.layer.at[1 - h], b.layer_out.at[h], partner)
     b.layer_out[h] = b.layer[h]
     b.send_x[...] = (red_x.end(0) + b.grad_r1[1 - h]).astype(BF)
@@ -1013,13 +1042,12 @@
     b.send_m[...] = red_m.end(0).astype(BF)
     swap_m = link.send(b.send_m, b.recv_m, partner)
     b.grad_mem[h] = red_m.end(1)
-    way_fout.gather()
     way_self.turn()
     way_so.turn()
+    way_fout.turn()
     way_cross.add()
     way_co.add()
     way_fin.gather()
-    way_fout.forward()
     seq_sums.wait_recv()
     value = b.sums[...]
     for d in range(1, dims["seq"]):
@@ -1037,9 +1065,12 @@
     swap_l.wait_recv()
     way_self.add()
     way_so.add()
+    way_fout.add()
+    way_fout.gather()
     way_cross.gather()
     way_co.gather()
     way_fin.forward()
+    way_fout.forward()
     item_sums.wait_recv()
     value = b.sums_line[...]
     for e in range(1, dims["items"]):
@@ -1162,7 +1193,7 @@
     for name, grad, quarter, piece, moved, done in (
         ("fin", (2, share, fr, hidden), (2, fr, hidden), (2, fr // 2, hidden), (fr, hidden),
          (fr, hidden)),
-        ("fout", (2, share, gr, model), (2, gr, model), (2, gr // 2, model), (gr, model), (gr, model)),
+        ("fout", (2, share, gr, model), (gr, model), (gr // 2, model), (share, gr, model), (gr, model)),
         ("cross", cols, (3, seq, wr, width), (3, seq // 2, wr, width), (seq, 3, wr, width),
          (3, wr, model)),
         ("self", cols, (3, seq, wr, width), (3, seq // 2, wr, width), (seq, 3, wr, width),
@@ -1174,9 +1205,10 @@
     ):
         scratch += [
             ("g_" + name, grad, BF), ("q_" + name, (2, 2) + piece, BF), ("t_" + name, (2,) + piece, BF),
-            ("u_" + name, (2,) + piece, BF), ("s_" + name, quarter, BF), ("z_" + name, moved, BF),
-            ("d_" + name, done, BF),
+            ("u_" + name, (2,) + piece, BF), ("z_" + name, moved, BF), ("d_" + name, done, BF),
         ]
+        if name != "fout":
+            scratch.append(("s_" + name, quarter, BF))
         if lines:
             scratch.append(("l_" + name, (lines,) + quarter, BF))
     copies = dims["chain"] + 145 + 12 * (bits - 2)

time: 247 us -> 278 us (1.13)
  Pallas kernels: 246 us -> 277 us
    pallas_call x1, Pallas kernels: 239 us -> 270 us  [shards(): pl.pallas_call(functools.partial(layer_kernel, dims, names), name='layer'...]
where the time goes in v6:
time: 278 us
  Pallas kernels  277 us (100%)
    pallas_call x1, Pallas kernels, shards(): pl.pallas_call(functools.partial(layer_kernel, dims, names), name='layer'...  270 us
    pallas_call x1, Pallas kernels, shards(): pl.pallas_call(outputs_kernel, name='outputs', grid=(share,), in_specs=ro...  6.71 us

profile of v6, /device:TPU:0, one launch (start us, length us, event | category | flops | bytes accessed | tf_op | source)
XLA Modules:
  0.0 277.6 jit_solution(16947483577041498796)
XLA Ops:
  0.7 270.1 %layer.1 = (bf16[2,64,1024]{2,1,0:T(8,128)(2,1)}, f32[2,64,1024]{2,1,0:T(8,128)}, f32[2,48,1024]{2,1,0:T(8,128)}, f32[8,1024]{1,0:T(8,128)}, bf16[4,3,32,1024]{3...) custom-call(bf16[2,64,1024]{2,1,0:T(8,128)(2,1)} %refs_0_.1, ...), custom_call_target="tpu_custom_call" | custom-call | tf_op jit(solution)/shard_map/layer/pallas_call | solution.py:1216
  270.7 6.7 %outputs.1 = (bf16[128,1024]{1,0:T(8,128)(2,1)}, f32[128,1024]{1,0:T(8,128)}, f32[96,1024]{1,0:T(8,128)}, f32[128,1024]{1,0:T(8,128)}, f32[128,1024]{1,0:T(8,128...) custom-call(bf16[128,1024]{1,0:T(8,128)(2,1)} %bitcast.8, ...), custom_call_target="tpu_custom_call" | custom-call | tf_op jit(solution)/shard_map/outputs/pallas_call | solution.py:1245

commit v7 on v5

--- a/solution.py
+++ b/solution.py
@@ -704,9 +704,6 @@
     own_fout.wait()
     fr, gr = b.o_fin.shape[1], b.o_fout.shape[1]
     step_fin = link.send(b.own_fin.at[pl.ds(pl.multiple_of(t * fr, fr), fr)], b.o_fin.at[t], partner)
-    step_fout = link.send(
-        b.own_fout.at[pl.ds(pl.multiple_of(t * gr, gr), gr)], b.o_fout.at[t], partner
-    )
     for share in self_share:
         share.forward()
 
@@ -776,14 +773,14 @@
             share.forward()
         step_fin.wait_recv()
         ffn_share.append(share_hidden(b.o_fin))
-        step_fout.wait_recv()
-        ffn_share.append(share_hidden(b.o_fout))
 
     ffn_share = []
     stage_steps(stage, self_part, after=cross_weights)
+    step_fout = link.send(
+        b.own_fout.at[pl.ds(pl.multiple_of(t * gr, gr), gr)], b.o_fout.at[t], partner
+    )
     memory_part()
     b.c_own[h] = b.cot[h]
-    swap_c = link.send(b.cot.at[1 - h], b.c_own.at[h], partner)
 
     def cross_part(k, pump):
         last.arrive(k)
@@ -804,10 +801,12 @@
         b.second_all, last,
     )
     def ffn_weights():
-        for share in ffn_share:
-            share.forward()
+        ffn_share[0].forward()
+        step_fout.wait_recv()
+        ffn_share.append(share_hidden(b.o_fout))
 
     stage_steps(stage, cross_part, ffn_weights)
+    swap_c = link.send(b.cot.at[1 - h], b.c_own.at[h], partner)
 
     w_ins = (lambda: b.own_fin[...], lambda: b.o_fin[...].reshape(model, -1))
     w_outs = (lambda: b.own_fout[...], lambda: b.o_fout[...].reshape(-1, model))
@@ -830,6 +829,7 @@
                 cdf + pre * (jnp.exp(-0.5 * pre * pre) * 0.3989422804014327)
             ).astype(BF)
         if k == 0:
+            ffn_share[1].forward()
             ffn_share[1].wait()
         total = nn(b.act[span(k), :hidden], w_outs[0]())
         put(k, total + nn(b.act[span(k), hidden:], w_outs[1]()), last_second)
@@ -858,8 +858,21 @@
 
     last_turn = stage
 
+    way_fout = Hidden(
+        link, place, b.g_fout, ("q_fout", "t_fout", "u_fout", dims["lines"] and "l_fout", "s_fout", "z_fout", "d_fout", "r_fout"), b
+    )
+    def out_grads():
+        grad = rows_of(b.gy_all)
+        for index in range(2):
+            cols = slice(index * hidden, (index + 1) * hidden)
+            value = tn(b.act[:, cols], grad)
+            b.g_fout[index] = value.astype(BF).reshape(b.g_fout.shape[1:])
+        way_fout.send()
+
     def ffn_back(k, pump):
         last_turn.arrive(k)
+        if k == 1:
+            out_grads()
         grad = chunk(b.gy_all, k)
         total = None
         for index in range(2):
@@ -872,9 +885,6 @@
             total = term if total is None else total + term
         put(k, total, last_turn)
 
-    way_fout = Hidden(
-        link, place, b.g_fout, ("q_fout", "t_fout", "u_fout", dims["lines"] and "l_fout", "s_fout", "z_fout", "d_fout", "r_fout"), b
-    )
     way_fin = Hidden(
         link, place, b.g_fin, ("q_fin", "t_fin", "u_fin", dims["lines"] and "l_fin", "s_fin", "z_fin", "d_fin", "r_fin"), b
     )
@@ -902,14 +912,6 @@
 
         return mid
 
-    def out_grads():
-        grad = rows_of(b.gy_all)
-        for index in range(2):
-            cols = slice(index * hidden, (index + 1) * hidden)
-            value = tn(b.act[:, cols], grad)
-            b.g_fout[index] = value.astype(BF).reshape(b.g_fout.shape[1:])
-        way_fout.send()
-
     def in_grads():
         rows = rows_of(b.second_all)
         for index in range(2):
@@ -922,7 +924,7 @@
         sems, place, b.part, bufs, backward(1, b.grad_third, b.sum_two, b.grad_r2), b.gc2_all,
         last_turn,
     )
-    stage_steps(stage, ffn_back, out_grads, in_grads)
+    stage_steps(stage, ffn_back, in_grads)
 
     last_back = stage
 
@@ -934,9 +936,10 @@
             k * half_rows, (k + 1) * half_rows, pump,
         )
         put(k, nt(b.dq[span(k)], weight(b.o_cross, 2)), last_back)
+        if k == 1:
+            way_fout.turn()
 
     def cross_grads():
-        way_fout.turn()
         mems = rows_of(b.m_all)
         shape = b.g_cross.shape[1:]
         b.dck[...] = (b.sum_dk[:total_mem] * SCALE).astype(BF)
@@ -947,21 +950,27 @@
         way_cross.send()
         b.g_co[...] = tn(b.cmix[...], rows_of(b.gc2_all)).astype(BF).reshape(b.g_co.shape)
         way_co.send()
+        way_fin.turn()
 
     def part_mem():
         value = nt(b.dck[...], weight(b.o_cross, 0)) + nt(b.dcv[...], weight(b.o_cross, 1))
         b.part_m[...] = value.astype(BF).reshape(b.part_m.shape)
+        for index in range(2):
+            red_m.start(index, ks[index])
 
     stage = Stage(
         sems, place, b.part, bufs, backward(0, b.grad_r2, b.sum_one, b.grad_r1), b.gc1_all,
         last_back,
     )
-    def cross_ended():
-        part_mem()
-        way_fin.turn()
-
-    stage_steps(stage, cross_back, cross_grads, cross_ended)
-
+    ks = (1 - h, h)
+    mem_bufs = [b.recv0_m, b.send1_m, b.recv1_m, b.keep1_m]
+    if dims["bits"] == 3:
+        mem_bufs += [b.send2_m, b.recv2_m]
+    red_m = Reduce(link, place, b.part_m, mem_bufs)
+    stage_steps(stage, cross_back, cross_grads, part_mem)
+
+    swap_l = link.send(b.layer.at[1 - h], b.layer_out.at[h], partner)
+    b.layer_out[h] = b.layer[h]
     for k in range(2):
         stage.arrive(k)
         pump = (lambda: stage.forward(1)) if k == 0 else (lambda: None)
@@ -970,6 +979,7 @@
             b.sq, b.sk, b.sv, b.sp, b.dmix, b.dq, b.sum_dk, b.sum_dv, True, block,
             k * half_rows, (k + 1) * half_rows, pump,
         )
+        red_m.middle(k, ks[k])
     b.dsk[...] = (b.sum_dk[...] * SCALE).astype(BF)
     b.dsv[...] = b.sum_dv[...].astype(BF)
     for k in range(2):
@@ -977,15 +987,9 @@
         put(k, total + nt(b.dsv[span(k)], weight(b.o_self, 2)), stage)
     stage.link.finish()
     chain = Link(*sems)
-    ks = (1 - h, h)
     red_x = Reduce(chain, place, b.part, bufs)
-    mem_bufs = [b.recv0_m, b.send1_m, b.recv1_m, b.keep1_m]
-    if dims["bits"] == 3:
-        mem_bufs += [b.send2_m, b.recv2_m]
-    red_m = Reduce(link, place, b.part_m, mem_bufs)
-    for red in (red_x, red_m):
-        for index in range(2):
-            red.start(index, ks[index])
+    for index in range(2):
+        red_x.start(index, ks[index])
     rows = rows_of(b.x_all)
     shape = b.g_self.shape[1:]
     b.g_self[0] = tn(rows, b.dq[...]).astype(BF).reshape(shape)
@@ -994,32 +998,27 @@
     way_self.send()
     b.g_so[...] = tn(b.smix[...], rows_of(b.gc1_all)).astype(BF).reshape(b.g_so.shape)
     way_so.send()
+    for index in range(2):
+        red_x.middle(index, ks[index])
     way_fout.add()
     way_cross.turn()
     way_co.turn()
-    for red in (red_x, red_m):
-        for index in range(2):
-            red.middle(index, ks[index])
     copies = []
     for d in range(1, dims["seq"]):
         copies.append((b.sums, b.sums_seq.at[d - 1], {"seq": place.seq_shift(d)}))
     seq_sums = link.batch(copies, b.sums_seq)
     way_fin.add()
-    swap_l = link.send(b.layer.at[1 - h], b.layer_out.at[h], partner)
-    b.layer_out[h] = b.layer[h]
     b.send_x[...] = (red_x.end(0) + b.grad_r1[1 - h]).astype(BF)
     swap_x = link.send(b.send_x, b.recv_x, partner)
     b.grad_dec[h] = red_x.end(1) + b.grad_r1[h]
     b.send_m[...] = red_m.end(0).astype(BF)
     swap_m = link.send(b.send_m, b.recv_m, partner)
     b.grad_mem[h] = red_m.end(1)
-    way_fout.gather()
     way_self.turn()
     way_so.turn()
     way_cross.add()
     way_co.add()
-    way_fin.gather()
-    way_fout.forward()
+    way_fout.gather()
     seq_sums.wait_recv()
     value = b.sums[...]
     for d in range(1, dims["seq"]):
@@ -1030,13 +1029,15 @@
         target = {"items": lax.rem(place.it + e, dims["items"])}
         copies.append((b.sums_line, b.sums_items.at[e - 1], target))
     item_sums = link.batch(copies, b.sums_items)
+    way_self.add()
+    way_so.add()
+    way_fin.gather()
+    way_fout.forward()
     swap_x.wait_recv()
     b.grad_dec[1 - h] = b.recv_x[...].astype(F32)
     swap_m.wait_recv()
     b.grad_mem[1 - h] = b.recv_m[...].astype(F32)
     swap_l.wait_recv()
-    way_self.add()
-    way_so.add()
     way_cross.gather()
     way_co.gather()
     way_fin.forward()
@@ -1045,10 +1046,10 @@
     for e in range(1, dims["items"]):
         value = value + b.sums_items[e - 1]
     b.sums_out[...] = value
+    way_self.gather()
+    way_so.gather()
     way_cross.forward()
     way_co.forward()
-    way_self.gather()
-    way_so.gather()
     way_self.forward()
     way_so.forward()
     for way in (way_fout, way_fin, way_cross, way_co, way_self, way_so):

time: 247 us -> 244 us (0.988)
  Pallas kernels: 246 us -> 243 us
    pallas_call x1, Pallas kernels: 239 us -> 236 us  [shards(): pl.pallas_call(functools.partial(layer_kernel, dims, names), name='layer'...]
where the time goes in v7:
time: 244 us
  Pallas kernels  243 us (100%)
    pallas_call x1, Pallas kernels, shards(): pl.pallas_call(functools.partial(layer_kernel, dims, names), name='layer'...  236 us
    pallas_call x1, Pallas kernels, shards(): pl.pallas_call(outputs_kernel, name='outputs', grid=(share,), in_specs=ro...  6.71 us

profile of v7, /device:TPU:0, one launch (start us, length us, event | category | flops | bytes accessed | tf_op | source)
XLA Modules:
  0.0 243.5 jit_solution(10670398237037239097)
XLA Ops:
  0.7 236.0 %layer.1 = (bf16[2,64,1024]{2,1,0:T(8,128)(2,1)}, f32[2,64,1024]{2,1,0:T(8,128)}, f32[2,48,1024]{2,1,0:T(8,128)}, f32[8,1024]{1,0:T(8,128)}, bf16[4,3,32,1024]{3...) custom-call(bf16[2,64,1024]{2,1,0:T(8,128)(2,1)} %refs_0_.1, ...), custom_call_target="tpu_custom_call" | custom-call | tf_op jit(solution)/shard_map/layer/pallas_call | solution.py:1185
  236.6 6.7 %outputs.1 = (bf16[128,1024]{1,0:T(8,128)(2,1)}, f32[128,1024]{1,0:T(8,128)}, f32[96,1024]{1,0:T(8,128)}, f32[128,1024]{1,0:T(8,128)}, f32[128,1024]{1,0:T(8,128...) custom-call(bf16[128,1024]{1,0:T(8,128)(2,1)} %bitcast.8, ...), custom_call_target="tpu_custom_call" | custom-call | tf_op jit(solution)/shard_map/outputs/pallas_call | solution.py:1214

commit v8 on v7

--- a/solution.py
+++ b/solution.py
@@ -768,17 +768,16 @@
         forward(0, lambda k: b.x_all[k, c, b1, b0].astype(F32), b.sum_one, b.first), b.first_all, None,
     )
     def cross_weights():
+        rows = pl.ds(pl.multiple_of(t * gr, gr), gr)
+        steps_fout.append(link.send(b.own_fout.at[rows], b.o_fout.at[t], partner))
         mem_waits.extend(spread_end(link, place, b.m_all, 1 - h, second_m))
         for share in cross_share + [co_share]:
             share.forward()
         step_fin.wait_recv()
         ffn_share.append(share_hidden(b.o_fin))
 
-    ffn_share = []
+    ffn_share, steps_fout = [], []
     stage_steps(stage, self_part, after=cross_weights)
-    step_fout = link.send(
-        b.own_fout.at[pl.ds(pl.multiple_of(t * gr, gr), gr)], b.o_fout.at[t], partner
-    )
     memory_part()
     b.c_own[h] = b.cot[h]
 
@@ -802,7 +801,7 @@
     )
     def ffn_weights():
         ffn_share[0].forward()
-        step_fout.wait_recv()
+        arrive(steps_fout)
         ffn_share.append(share_hidden(b.o_fout))
 
     stage_steps(stage, cross_part, ffn_weights)
@@ -971,6 +970,7 @@
 
     swap_l = link.send(b.layer.at[1 - h], b.layer_out.at[h], partner)
     b.layer_out[h] = b.layer[h]
+    way_fout.add()
     for k in range(2):
         stage.arrive(k)
         pump = (lambda: stage.forward(1)) if k == 0 else (lambda: None)
@@ -990,6 +990,9 @@
     red_x = Reduce(chain, place, b.part, bufs)
     for index in range(2):
         red_x.start(index, ks[index])
+    way_cross.turn()
+    way_co.turn()
+    way_fin.add()
     rows = rows_of(b.x_all)
     shape = b.g_self.shape[1:]
     b.g_self[0] = tn(rows, b.dq[...]).astype(BF).reshape(shape)
@@ -1000,25 +1003,28 @@
     way_so.send()
     for index in range(2):
         red_x.middle(index, ks[index])
-    way_fout.add()
-    way_cross.turn()
-    way_co.turn()
+    b.send_m[...] = red_m.end(0).astype(BF)
+    swap_m = link.send(b.send_m, b.recv_m, partner)
+    b.grad_mem[h] = red_m.end(1)
     copies = []
     for d in range(1, dims["seq"]):
         copies.append((b.sums, b.sums_seq.at[d - 1], {"seq": place.seq_shift(d)}))
     seq_sums = link.batch(copies, b.sums_seq)
-    way_fin.add()
+    way_cross.add()
+    way_co.add()
     b.send_x[...] = (red_x.end(0) + b.grad_r1[1 - h]).astype(BF)
     swap_x = link.send(b.send_x, b.recv_x, partner)
     b.grad_dec[h] = red_x.end(1) + b.grad_r1[h]
-    b.send_m[...] = red_m.end(0).astype(BF)
-    swap_m = link.send(b.send_m, b.recv_m, partner)
-    b.grad_mem[h] = red_m.end(1)
+    way_fout.gather()
     way_self.turn()
     way_so.turn()
-    way_cross.add()
-    way_co.add()
-    way_fout.gather()
+    way_fin.gather()
+    way_fout.forward()
+    way_self.add()
+    way_so.add()
+    way_cross.gather()
+    way_co.gather()
+    way_fin.forward()
     seq_sums.wait_recv()
     value = b.sums[...]
     for d in range(1, dims["seq"]):
@@ -1029,27 +1035,20 @@
         target = {"items": lax.rem(place.it + e, dims["items"])}
         copies.append((b.sums_line, b.sums_items.at[e - 1], target))
     item_sums = link.batch(copies, b.sums_items)
-    way_self.add()
-    way_so.add()
-    way_fin.gather()
-    way_fout.forward()
     swap_x.wait_recv()
     b.grad_dec[1 - h] = b.recv_x[...].astype(F32)
     swap_m.wait_recv()
     b.grad_mem[1 - h] = b.recv_m[...].astype(F32)
     swap_l.wait_recv()
-    way_cross.gather()
-    way_co.gather()
-    way_fin.forward()
+    way_self.gather()
+    way_so.gather()
+    way_cross.forward()
+    way_co.forward()
     item_sums.wait_recv()
     value = b.sums_line[...]
     for e in range(1, dims["items"]):
         value = value + b.sums_items[e - 1]
     b.sums_out[...] = value
-    way_self.gather()
-    way_so.gather()
-    way_cross.forward()
-    way_co.forward()
     way_self.forward()
     way_so.forward()
     for way in (way_fout, way_fin, way_cross, way_co, way_self, way_so):

time: 244 us -> 238 us (0.975)
  Pallas kernels: 243 us -> 237 us
    pallas_call x1, Pallas kernels: 236 us -> 230 us  [shards(): pl.pallas_call(functools.partial(layer_kernel, dims, names), name='layer'...]
where the time goes in v8:
time: 238 us
  Pallas kernels  237 us (100%)
    pallas_call x1, Pallas kernels, shards(): pl.pallas_call(functools.partial(layer_kernel, dims, names), name='layer'...  230 us
    pallas_call x1, Pallas kernels, shards(): pl.pallas_call(outputs_kernel, name='outputs', grid=(share,), in_specs=ro...  6.71 us

profile of v8, /device:TPU:0, one launch (start us, length us, event | category | flops | bytes accessed | tf_op | source)
XLA Modules:
  0.0 237.8 jit_solution(9060176509579817653)
XLA Ops:
  0.7 230.3 %layer.1 = (bf16[2,64,1024]{2,1,0:T(8,128)(2,1)}, f32[2,64,1024]{2,1,0:T(8,128)}, f32[2,48,1024]{2,1,0:T(8,128)}, f32[8,1024]{1,0:T(8,128)}, bf16[4,3,32,1024]{3...) custom-call(bf16[2,64,1024]{2,1,0:T(8,128)(2,1)} %refs_0_.1, ...), custom_call_target="tpu_custom_call" | custom-call | tf_op jit(solution)/shard_map/layer/pallas_call | solution.py:1184
  230.9 6.7 %outputs.1 = (bf16[128,1024]{1,0:T(8,128)(2,1)}, f32[128,1024]{1,0:T(8,128)}, f32[96,1024]{1,0:T(8,128)}, f32[128,1024]{1,0:T(8,128)}, f32[128,1024]{1,0:T(8,128...) custom-call(bf16[128,1024]{1,0:T(8,128)(2,1)} %bitcast.8, ...), custom_call_target="tpu_custom_call" | custom-call | tf_op jit(solution)/shard_map/outputs/pallas_call | solution.py:1213

commit v9 on v8

--- a/solution.py
+++ b/solution.py
@@ -652,7 +652,6 @@
     own_fout = link.local(b.f_out, b.own_fout)
     greet(place.seq_peers() + place.items_peers())
 
-    swap_x = link.send(b.dec.at[1 - h], b.x_all.at[h, c, b1, b0], partner)
     def share_columns(dst):
         blocks = dims["seq"] // 2
         return Share(
@@ -680,24 +679,24 @@
             b.mem_cells[k, :, :model] = b.mem[k]
             b.mem_cells[k, :, model:] = jnp.broadcast_to(column, (mb, 128)).astype(BF)
 
-    b.x_all[h, c, b1, b0] = b.dec[h]
-    first_x = spread_start(link, place, b.x_all, h)
     staged.wait()
     steps, own_self = columns_out(link, place, b.staged.at[0:3], b.o_self, width)
-    waits = spread_end(link, place, b.x_all, h, first_x)
-    swap_x.wait_recv()
-    second_x = spread_start(link, place, b.x_all, 1 - h)
+    b.x_all[h, c, b1, b0] = b.dec[h]
+    join_cells()
+    b.m_all[h, c, b1, b0] = b.mem_cells[h]
+    link.settle(steps)
+    swap_x = link.send(b.dec.at[1 - h], b.x_all.at[h, c, b1, b0], partner)
+    first_x = spread_start(link, place, b.x_all, h)
     so_arrived, so_sent = rows_out(link, place, b.staged.at[3], b.o_so)
     steps.wait_recv()
     own_self.wait()
     self_share = [share_columns(b.o_self.at[i]) for i in range(3)]
+    waits = spread_end(link, place, b.x_all, h, first_x)
+    swap_x.wait_recv()
+    second_x = spread_start(link, place, b.x_all, 1 - h)
     waits += spread_end(link, place, b.x_all, 1 - h, second_x)
-    so_arrived()
-    so_share = share_rows(b.o_so)
     cross_steps, own_cross = columns_out(link, place, b.staged.at[4:7], b.o_cross, width)
     co_arrived, co_sent = rows_out(link, place, b.staged.at[7], b.o_co)
-    join_cells()
-    b.m_all[h, c, b1, b0] = b.mem_cells[h]
     swap_m = link.send(b.mem_cells.at[1 - h], b.m_all.at[h, c, b1, b0], partner)
     first_m = spread_start(link, place, b.m_all, h)
     own_fin.wait()
@@ -706,6 +705,8 @@
     step_fin = link.send(b.own_fin.at[pl.ds(pl.multiple_of(t * fr, fr), fr)], b.o_fin.at[t], partner)
     for share in self_share:
         share.forward()
+    so_arrived()
+    so_share = share_rows(b.o_so)
 
     arrive(waits)
     rows = rows_of(b.x_all)
@@ -820,6 +821,8 @@
         for index in range(2):
             if index:
                 pump()
+                if k == 0:
+                    ffn_share[1].forward()
             pre = nn(rows, w_ins[index]())
             cdf = 0.5 * (1.0 + lax.erf(pre * (0.5**0.5)))
             cols = slice(index * hidden, (index + 1) * hidden)
@@ -828,7 +831,6 @@
                 cdf + pre * (jnp.exp(-0.5 * pre * pre) * 0.3989422804014327)
             ).astype(BF)
         if k == 0:
-            ffn_share[1].forward()
             ffn_share[1].wait()
         total = nn(b.act[span(k), :hidden], w_outs[0]())
         put(k, total + nn(b.act[span(k), hidden:], w_outs[1]()), last_second)

time: 238 us -> 239 us (level)
  no operation moved by 1% of the time
where the time goes in v9:
time: 239 us
  Pallas kernels  238 us (100%)
    pallas_call x1, Pallas kernels, shards(): pl.pallas_call(functools.partial(layer_kernel, dims, names), name='layer'...  231 us
    pallas_call x1, Pallas kernels, shards(): pl.pallas_call(outputs_kernel, name='outputs', grid=(share,), in_specs=ro...  6.71 us

profile of v9, /device:TPU:0, one launch (start us, length us, event | category | flops | bytes accessed | tf_op | source)
XLA Modules:
  0.0 239.0 jit_solution(11262875590089583169)
XLA Ops:
  0.7 231.5 %layer.1 = (bf16[2,64,1024]{2,1,0:T(8,128)(2,1)}, f32[2,64,1024]{2,1,0:T(8,128)}, f32[2,48,1024]{2,1,0:T(8,128)}, f32[8,1024]{1,0:T(8,128)}, bf16[4,3,32,1024]{3...) custom-call(bf16[2,64,1024]{2,1,0:T(8,128)(2,1)} %refs_0_.1, ...), custom_call_target="tpu_custom_call" | custom-call | tf_op jit(solution)/shard_map/layer/pallas_call | solution.py:1186
  232.1 6.7 %outputs.1 = (bf16[128,1024]{1,0:T(8,128)(2,1)}, f32[128,1024]{1,0:T(8,128)}, f32[96,1024]{1,0:T(8,128)}, f32[128,1024]{1,0:T(8,128)}, f32[128,1024]{1,0:T(8,128...) custom-call(bf16[128,1024]{1,0:T(8,128)(2,1)} %bitcast.8, ...), custom_call_target="tpu_custom_call" | custom-call | tf_op jit(solution)/shard_map/outputs/pallas_call | solution.py:1215

commit v10 on v9

--- a/solution.py
+++ b/solution.py
@@ -699,10 +699,6 @@
     co_arrived, co_sent = rows_out(link, place, b.staged.at[7], b.o_co)
     swap_m = link.send(b.mem_cells.at[1 - h], b.m_all.at[h, c, b1, b0], partner)
     first_m = spread_start(link, place, b.m_all, h)
-    own_fin.wait()
-    own_fout.wait()
-    fr, gr = b.o_fin.shape[1], b.o_fout.shape[1]
-    step_fin = link.send(b.own_fin.at[pl.ds(pl.multiple_of(t * fr, fr), fr)], b.o_fin.at[t], partner)
     for share in self_share:
         share.forward()
     so_arrived()
@@ -722,6 +718,10 @@
     mem_waits = spread_end(link, place, b.m_all, h, first_m)
     swap_m.wait_recv()
     second_m = spread_start(link, place, b.m_all, 1 - h)
+    own_fin.wait()
+    own_fout.wait()
+    fr, gr = b.o_fin.shape[1], b.o_fout.shape[1]
+    step_fin = link.send(b.own_fin.at[pl.ds(pl.multiple_of(t * fr, fr), fr)], b.o_fin.at[t], partner)
     length, mem_length = b.dec_len[h], b.mem_len[h]
 
     def self_ok(start, stop):

time: 239 us -> 237 us (level)
    pallas_call x1, Pallas kernels: 231 us -> 229 us  [shards(): pl.pallas_call(functools.partial(layer_kernel, dims, names), name='layer'...]
where the time goes in v10:
time: 237 us
  Pallas kernels  236 us (100%)
    pallas_call x1, Pallas kernels, shards(): pl.pallas_call(functools.partial(layer_kernel, dims, names), name='layer'...  229 us
    pallas_call x1, Pallas kernels, shards(): pl.pallas_call(outputs_kernel, name='outputs', grid=(share,), in_specs=ro...  6.71 us

profile of v10, /device:TPU:0, one launch (start us, length us, event | category | flops | bytes accessed | tf_op | source)
XLA Modules:
  0.0 236.6 jit_solution(14465071406517884565)
XLA Ops:
  0.7 229.0 %layer.1 = (bf16[2,64,1024]{2,1,0:T(8,128)(2,1)}, f32[2,64,1024]{2,1,0:T(8,128)}, f32[2,48,1024]{2,1,0:T(8,128)}, f32[8,1024]{1,0:T(8,128)}, bf16[4,3,32,1024]{3...) custom-call(bf16[2,64,1024]{2,1,0:T(8,128)(2,1)} %refs_0_.1, ...), custom_call_target="tpu_custom_call" | custom-call | tf_op jit(solution)/shard_map/layer/pallas_call | solution.py:1186
  229.7 6.7 %outputs.1 = (bf16[128,1024]{1,0:T(8,128)(2,1)}, f32[128,1024]{1,0:T(8,128)}, f32[96,1024]{1,0:T(8,128)}, f32[128,1024]{1,0:T(8,128)}, f32[128,1024]{1,0:T(8,128...) custom-call(bf16[128,1024]{1,0:T(8,128)(2,1)} %bitcast.8, ...), custom_call_target="tpu_custom_call" | custom-call | tf_op jit(solution)/shard_map/outputs/pallas_call | solution.py:1215

commit v11 on v10

--- a/solution.py
+++ b/solution.py
@@ -219,6 +219,15 @@
 
     def wait(self):
         arrive(self.steps)
+
+
+class Direct(Share):
+    def __init__(self, link, place, slab):
+        lines = (place.tx, place.ty, place.txy)
+        self.steps = [link.send(slab(place.t), slab(place.t), place.line(line)) for line in lines]
+
+    def forward(self):
+        pass
 
 
 def arrive(steps):
@@ -712,9 +721,11 @@
     so_share.forward()
     cross_steps.wait_recv()
     own_cross.wait()
-    cross_share = [share_columns(b.o_cross.at[i]) for i in range(3)]
+    cross_share = [
+        Direct(link, place, lambda _, dst=b.o_cross.at[i]: dst.at[:, t]) for i in range(3)
+    ]
     co_arrived()
-    co_share = share_rows(b.o_co)
+    co_share = Direct(link, place, lambda _: b.o_co.at[:, t])
     mem_waits = spread_end(link, place, b.m_all, h, first_m)
     swap_m.wait_recv()
     second_m = spread_start(link, place, b.m_all, 1 - h)
@@ -772,8 +783,6 @@
         rows = pl.ds(pl.multiple_of(t * gr, gr), gr)
         steps_fout.append(link.send(b.own_fout.at[rows], b.o_fout.at[t], partner))
         mem_waits.extend(spread_end(link, place, b.m_all, 1 - h, second_m))
-        for share in cross_share + [co_share]:
-            share.forward()
         step_fin.wait_recv()
         ffn_share.append(share_hidden(b.o_fin))
 
@@ -803,7 +812,7 @@
     def ffn_weights():
         ffn_share[0].forward()
         arrive(steps_fout)
-        ffn_share.append(share_hidden(b.o_fout))
+        ffn_share.append(Direct(link, place, lambda _: b.o_fout.at[t]))
 
     stage_steps(stage, cross_part, ffn_weights)
     swap_c = link.send(b.cot.at[1 - h], b.c_own.at[h], partner)
@@ -821,8 +830,6 @@
         for index in range(2):
             if index:
                 pump()
-                if k == 0:
-                    ffn_share[1].forward()
             pre = nn(rows, w_ins[index]())
             cdf = 0.5 * (1.0 + lax.erf(pre * (0.5**0.5)))
             cols = slice(index * hidden, (index + 1) * hidden)
@@ -1181,7 +1188,7 @@
         ]
         if lines:
             scratch.append(("l_" + name, (lines,) + quarter, BF))
-    copies = dims["chain"] + 145 + 12 * (bits - 2)
+    copies = dims["chain"] + 140 + 12 * (bits - 2)
     names = [x[0] for x in ins + outs + scratch] + ["send_sems", "recv_sems"]
     results = pl.pallas_call(
         functools.partial(layer_kernel, dims, names),

time: 237 us -> 231 us (0.975)
  Pallas kernels: 236 us -> 230 us
    pallas_call x1, Pallas kernels: 229 us -> 223 us  [shards(): pl.pallas_call(functools.partial(layer_kernel, dims, names), name='layer'...]
where the time goes in v11:
time: 231 us; the launch traced here: 230 us
  Pallas kernels  230 us (100%)
    pallas_call x1, Pallas kernels, shards(): pl.pallas_call(functools.partial(layer_kernel, dims, names), name='layer'...  223 us
    pallas_call x1, Pallas kernels, shards(): pl.pallas_call(outputs_kernel, name='outputs', grid=(share,), in_specs=ro...  6.71 us

profile of v11, /device:TPU:0, one launch (start us, length us, event | category | flops | bytes accessed | tf_op | source)
XLA Modules:
  0.0 230.4 jit_solution(8645974830802559340)
XLA Ops:
  0.7 222.8 %layer.1 = (bf16[2,64,1024]{2,1,0:T(8,128)(2,1)}, f32[2,64,1024]{2,1,0:T(8,128)}, f32[2,48,1024]{2,1,0:T(8,128)}, f32[8,1024]{1,0:T(8,128)}, bf16[4,3,32,1024]{3...) custom-call(bf16[2,64,1024]{2,1,0:T(8,128)(2,1)} %refs_0_.1, ...), custom_call_target="tpu_custom_call" | custom-call | tf_op jit(solution)/shard_map/layer/pallas_call | solution.py:1193
  223.5 6.7 %outputs.1 = (bf16[128,1024]{1,0:T(8,128)(2,1)}, f32[128,1024]{1,0:T(8,128)}, f32[96,1024]{1,0:T(8,128)}, f32[128,1024]{1,0:T(8,128)}, f32[128,1024]{1,0:T(8,128...) custom-call(bf16[128,1024]{1,0:T(8,128)(2,1)} %bitcast.8, ...), custom_call_target="tpu_custom_call" | custom-call | tf_op jit(solution)/shard_map/outputs/pallas_call | solution.py:1222

commit v12 on v11

--- a/solution.py
+++ b/solution.py
@@ -668,9 +668,6 @@
             lambda t, i: dst.at[i * blocks : (i + 1) * blocks, t],
         )
 
-    def share_rows(dst):
-        return Share(link, place, lambda t: dst.at[:, t], lambda t, i: dst.at[i, t])
-
     def share_hidden(dst):
         rows = dst.shape[1] // 2
         return Share(
@@ -711,14 +708,13 @@
     for share in self_share:
         share.forward()
     so_arrived()
-    so_share = share_rows(b.o_so)
+    so_share = Direct(link, place, lambda _: b.o_so.at[:, t])
 
     arrive(waits)
     rows = rows_of(b.x_all)
     for index, dst in enumerate((b.sq, b.sk, b.sv)):
         self_share[index].wait()
         dst[...] = nn(rows, weight(b.o_self, index)).astype(BF)
-    so_share.forward()
     cross_steps.wait_recv()
     own_cross.wait()
     cross_share = [
@@ -783,12 +779,12 @@
         rows = pl.ds(pl.multiple_of(t * gr, gr), gr)
         steps_fout.append(link.send(b.own_fout.at[rows], b.o_fout.at[t], partner))
         mem_waits.extend(spread_end(link, place, b.m_all, 1 - h, second_m))
-        step_fin.wait_recv()
-        ffn_share.append(share_hidden(b.o_fin))
 
     ffn_share, steps_fout = [], []
     stage_steps(stage, self_part, after=cross_weights)
     memory_part()
+    step_fin.wait_recv()
+    ffn_share.append(share_hidden(b.o_fin))
     b.c_own[h] = b.cot[h]
 
     def cross_part(k, pump):

time: 231 us -> 231 us (level)
  no operation moved by 1% of the time
where the time goes in v12:
time: 231 us; the launch traced here: 230 us
  Pallas kernels  230 us (100%)
    pallas_call x1, Pallas kernels, shards(): pl.pallas_call(functools.partial(layer_kernel, dims, names), name='layer'...  223 us
    pallas_call x1, Pallas kernels, shards(): pl.pallas_call(outputs_kernel, name='outputs', grid=(share,), in_specs=ro...  6.71 us

profile of v12, /device:TPU:0, one launch (start us, length us, event | category | flops | bytes accessed | tf_op | source)
XLA Modules:
  0.0 230.4 jit_solution(9242954362715591698)
XLA Ops:
  0.7 222.9 %layer.1 = (bf16[2,64,1024]{2,1,0:T(8,128)(2,1)}, f32[2,64,1024]{2,1,0:T(8,128)}, f32[2,48,1024]{2,1,0:T(8,128)}, f32[8,1024]{1,0:T(8,128)}, bf16[4,3,32,1024]{3...) custom-call(bf16[2,64,1024]{2,1,0:T(8,128)(2,1)} %refs_0_.1, ...), custom_call_target="tpu_custom_call" | custom-call | tf_op jit(solution)/shard_map/layer/pallas_call | solution.py:1189
  223.5 6.7 %outputs.1 = (bf16[128,1024]{1,0:T(8,128)(2,1)}, f32[128,1024]{1,0:T(8,128)}, f32[96,1024]{1,0:T(8,128)}, f32[128,1024]{1,0:T(8,128)}, f32[128,1024]{1,0:T(8,128...) custom-call(bf16[128,1024]{1,0:T(8,128)(2,1)} %bitcast.8, ...), custom_call_target="tpu_custom_call" | custom-call | tf_op jit(solution)/shard_map/outputs/pallas_call | solution.py:1218

commit v13 on v12

--- a/solution.py
+++ b/solution.py
@@ -776,11 +776,20 @@
         forward(0, lambda k: b.x_all[k, c, b1, b0].astype(F32), b.sum_one, b.first), b.first_all, None,
     )
     def cross_weights():
-        rows = pl.ds(pl.multiple_of(t * gr, gr), gr)
-        steps_fout.append(link.send(b.own_fout.at[rows], b.o_fout.at[t], partner))
+        for i in range(2):
+            rows = pl.ds(pl.multiple_of(t * gr + i * (gr // 2), gr // 2), gr // 2)
+            steps_fout.append(link.send(b.own_fout.at[rows], out_rows(i), partner))
         mem_waits.extend(spread_end(link, place, b.m_all, 1 - h, second_m))
 
     ffn_share, steps_fout = [], []
+
+    def out_rows(i):
+        return b.o_fout.at[t, i * (gr // 2) : (i + 1) * (gr // 2)]
+
+    def share_out(i):
+        steps_fout[i].wait_recv()
+        ffn_share.append(Direct(link, place, lambda _: out_rows(i)))
+
     stage_steps(stage, self_part, after=cross_weights)
     memory_part()
     step_fin.wait_recv()
@@ -799,6 +808,8 @@
         if k == 0:
             co_share.wait()
         put(k, nn(b.cmix[span(k)], rows_of(b.o_co)), last)
+        if k == 1:
+            share_out(0)
 
     last = stage
     stage = Stage(
@@ -807,8 +818,7 @@
     )
     def ffn_weights():
         ffn_share[0].forward()
-        arrive(steps_fout)
-        ffn_share.append(Direct(link, place, lambda _: b.o_fout.at[t]))
+        share_out(1)
 
     stage_steps(stage, cross_part, ffn_weights)
     swap_c = link.send(b.cot.at[1 - h], b.c_own.at[h], partner)
@@ -835,6 +845,7 @@
             ).astype(BF)
         if k == 0:
             ffn_share[1].wait()
+            ffn_share[2].wait()
         total = nn(b.act[span(k), :hidden], w_outs[0]())
         put(k, total + nn(b.act[span(k), hidden:], w_outs[1]()), last_second)
 
@@ -1184,7 +1195,7 @@
         ]
         if lines:
             scratch.append(("l_" + name, (lines,) + quarter, BF))
-    copies = dims["chain"] + 140 + 12 * (bits - 2)
+    copies = dims["chain"] + 144 + 12 * (bits - 2)
     names = [x[0] for x in ins + outs + scratch] + ["send_sems", "recv_sems"]
     results = pl.pallas_call(
         functools.partial(layer_kernel, dims, names),

time: 231 us -> 231 us (level)
  no operation moved by 1% of the time
where the time goes in v13:
time: 231 us
  Pallas kernels  230 us (100%)
    pallas_call x1, Pallas kernels, shards(): pl.pallas_call(functools.partial(layer_kernel, dims, names), name='layer'...  223 us
    pallas_call x1, Pallas kernels, shards(): pl.pallas_call(outputs_kernel, name='outputs', grid=(share,), in_specs=ro...  6.71 us

profile of v13, /device:TPU:0, one launch (start us, length us, event | category | flops | bytes accessed | tf_op | source)
XLA Modules:
  0.0 230.5 jit_solution(140151661132847172)
XLA Ops:
  0.7 223.0 %layer.1 = (bf16[2,64,1024]{2,1,0:T(8,128)(2,1)}, f32[2,64,1024]{2,1,0:T(8,128)}, f32[2,48,1024]{2,1,0:T(8,128)}, f32[8,1024]{1,0:T(8,128)}, bf16[4,3,32,1024]{3...) custom-call(bf16[2,64,1024]{2,1,0:T(8,128)(2,1)} %refs_0_.1, ...), custom_call_target="tpu_custom_call" | custom-call | tf_op jit(solution)/shard_map/layer/pallas_call | solution.py:1200
  223.6 6.7 %outputs.1 = (bf16[128,1024]{1,0:T(8,128)(2,1)}, f32[128,1024]{1,0:T(8,128)}, f32[96,1024]{1,0:T(8,128)}, f32[128,1024]{1,0:T(8,128)}, f32[128,1024]{1,0:T(8,128...) custom-call(bf16[128,1024]{1,0:T(8,128)(2,1)} %bitcast.8, ...), custom_call_target="tpu_custom_call" | custom-call | tf_op jit(solution)/shard_map/outputs/pallas_call | solution.py:1229
